TPU v7x, 768 devices: a whole 4x8x12 slice. The times are simulated.
768 devices in a mesh: gr: 32 (over z_lo, x, core), gc: 24 (over y, z_hi).
Axes of the slice: x: 4, y: 8, z: 12 (z_hi: 3, z_lo: 4; z = z_hi * 4 + z_lo), core: 2. Of those that a mesh axis runs over, the one named last changes fastest.
Arguments:
- features: bfloat16 [98304, 256], P(('gr', 'gc')), may hold values from -6 to 6
- degrees: int32 [98304], P(('gr', 'gc')), may hold values from 4 to 32
- weight: bfloat16 [256, 256], replicated, may hold values from -0.375 to 0.375
- bias_term: float32 [256], replicated, may hold values from -3 to 3
- tile_weights: bfloat16 [32, 24, 128, 128, 128], P('gr', 'gc'), may hold values from 0 to 1, as said below
- tile_rows: int32 [32, 24, 128], P('gr', 'gc'), may hold values from 0 to 23
- tile_columns: int32 [32, 24, 128], P('gr', 'gc'), may hold values from 0 to 31
- tile_count: int32 [32, 24], P('gr', 'gc'), may hold values from 16 to 128, as said below
- cotangent: bfloat16 [98304, 256], P(('gr', 'gc')), may hold values from -6 to 6
Outputs:
- activations: bfloat16 [98304, 256], P(('gr', 'gc'))
- feature_grad: bfloat16 [98304, 256], P(('gr', 'gc'))
Inputs may be any that keep to these rules, and one draw needn't show every extreme that they name: `tile_weights`: edge weights; a tile's block holds a minority of nonzero entries. `tile_count`: 128 divided by 1, 2, 4 or 8; the occupied slots are the first ones; 128 is reached by some pair in every draw. `tile_rows`: slots may share a position. `tile_columns`: slots may share a position.
All inputs are finite; a program needn't handle non-finite values.
Results may differ from a plain program's by a relative error of at most 0.033.
Values may be sent and summed in bfloat16 or wider, within the bound.
No kernel may reach another device: no remote copies, remote signals or barrier semaphores. Data moves between devices by JAX's collectives and lax.ppermute only.
A program may use at most 64 MiB of HBM per device.

v0:
```python
import math

import jax
import jax.numpy as jnp
from jax import lax
from jax.sharding import PartitionSpec as P


def spread_tiles(tile_block, pick_ids, place_ids, sources, place_blocks, live_count, transposed):
    tile_total = tile_block.shape[0]
    tile_edge = tile_block.shape[-1]
    feat_width = sources.shape[-1]
    blocks = sources.reshape(-1, tile_edge, feat_width)
    group_size = math.gcd(tile_total, 32)
    slot_ids = jnp.arange(group_size, dtype=jnp.int32)

    def add_group(counter, summed):
        first_slot = counter * group_size
        tile_part = lax.dynamic_slice_in_dim(tile_block, first_slot, group_size, 0)
        pick_part = lax.dynamic_slice_in_dim(pick_ids, first_slot, group_size, 0)
        place_part = lax.dynamic_slice_in_dim(place_ids, first_slot, group_size, 0)
        chosen = jnp.take(blocks, pick_part, axis=0)
        if transposed:
            product = jnp.einsum(
                "tik,tif->tkf", tile_part, chosen, preferred_element_type=jnp.float32
            )
        else:
            product = jnp.einsum(
                "tik,tkf->tif", tile_part, chosen, preferred_element_type=jnp.float32
            )
        is_live = first_slot + slot_ids < live_count
        target_part = jnp.where(is_live, place_part, place_blocks)
        return summed.at[target_part].add(product, mode="drop")

    start_sum = jnp.zeros((place_blocks, tile_edge, feat_width), jnp.float32)
    loop_count = tile_total // group_size
    summed = lax.fori_loop(0, loop_count, add_group, start_sum)
    return summed.reshape(-1, feat_width)


def body(
    features,
    degrees,
    weight,
    bias_term,
    tile_weights,
    tile_rows,
    tile_columns,
    tile_count,
    cotangent,
):
    tile_block = tile_weights[0, 0]
    row_ids = tile_rows[0, 0]
    column_ids = tile_columns[0, 0]
    live_count = tile_count[0, 0]
    shard_rows = features.shape[0]
    tile_edge = tile_block.shape[-1]
    inv_root = lax.rsqrt(degrees.astype(jnp.float32))[:, None]
    hidden = jnp.dot(features, weight, preferred_element_type=jnp.float32)
    scaled = (hidden * inv_root).astype(jnp.bfloat16)
    sources = lax.all_gather(scaled, "gr", axis=0, tiled=True)
    row_blocks = lax.axis_size("gc") * shard_rows // tile_edge
    column_blocks = lax.axis_size("gr") * shard_rows // tile_edge
    partial_value = spread_tiles(
        tile_block, column_ids, row_ids, sources, row_blocks, live_count, False
    )
    summed = lax.psum(partial_value.astype(jnp.bfloat16), "gc").astype(jnp.float32)
    own_rows = lax.dynamic_slice_in_dim(summed, lax.axis_index("gc") * shard_rows, shard_rows, 0)
    preact = inv_root * (own_rows + scaled.astype(jnp.float32)) + bias_term[None, :]
    sigmoid_value = jax.nn.sigmoid(preact)
    activations = (preact * sigmoid_value).astype(jnp.bfloat16)
    slope_value = sigmoid_value * (1.0 + preact * (1.0 - sigmoid_value))
    upstream = (cotangent.astype(jnp.float32) * slope_value * inv_root).astype(jnp.bfloat16)
    targets = lax.all_gather(upstream, "gc", axis=0, tiled=True)
    back_partial = spread_tiles(
        tile_block, row_ids, column_ids, targets, column_blocks, live_count, True
    )
    own_back = lax.psum_scatter(
        back_partial.astype(jnp.bfloat16), "gr", scatter_dimension=0, tiled=True
    ).astype(jnp.float32)
    grad_hidden = (inv_root * (own_back + upstream.astype(jnp.float32))).astype(jnp.bfloat16)
    feature_grad = jnp.einsum("nf,gf->ng", grad_hidden, weight, preferred_element_type=jnp.float32)
    return (activations, feature_grad.astype(jnp.bfloat16))


def solution(mesh):
    return jax.shard_map(
        body,
        mesh=mesh,
        in_specs=(
            P(("gr", "gc"), None),
            P(("gr", "gc")),
            P(),
            P(),
            P("gr", "gc", None, None, None),
            P("gr", "gc", None),
            P("gr", "gc", None),
            P("gr", "gc"),
            P(("gr", "gc"), None),
        ),
        out_specs=(P(("gr", "gc"), None), P(("gr", "gc"), None)),
        check_vma=False,
    )
```

profile of v0, /device:TPU:24, one launch (start us, length us, event | category | flops | bytes accessed | tf_op | source)
XLA Modules:
  0.0 797.8 jit_solution(2016283820178113356)
XLA Ops:
  7.2 0.0 all-gather.3.cloned.1.call-start
  7.2 0.7 convert_rsqrt_fusion
  7.9 0.2 copy-done
  8.1 1.6 fusion.18
  9.7 0.0 all-gather.3.cloned.1.call-update
  9.7 0.0 all-reduce.2.cloned.1.call-start
  9.8 73.7 %all-gather.3.cloned.1.call-done = bf16[4096,256]{1,0:T(8,128)(2,1)} async-done(((bf16[128,256]{1,0:T(8,128)(2,1)}), bf16[4096,256]{1,0:T(8,128)(2,1)}) %all-gather.3.cloned.1.call-update) | async-done | bytes 2097168 | tf_op jit(solution)/shard_map/all_gather | solution.py:61
  83.5 0.3 broadcast_in_dim.85
  83.9 62.4 %while.28 = (s32[]{:T(128)}, f32[24,128,256]{2,1,0:T(8,128)S(1)}, s32[]{:T(128)}, s32[128]{0:T(128)S(1)}, bf16[128,128,128]{2,1,0:T(8,128)(2,1)}, /*index=5*/s32...) while((s32[]{:T(128)}, f32[24,128,256]{2,1,0:T(8,128)S(1)}, ...), condition=%wide.region_2.3_spmd.clone, body=%wide.region_0.2_spmd.clone.sunk | while | flops 270534016 | bytes 24122480 | solution.py:37
  83.9 0.7 compare_select_fusion.10
  84.6 0.1 compare_and_fusion.4
  84.7 3.6 gather_fusion
  88.3 4.6 fusion.31
  93.0 6.5 scatter_fusion
  99.5 0.7 compare_select_fusion.10
  100.2 0.1 compare_and_fusion.4
  100.3 3.6 gather_fusion
  103.9 4.7 fusion.31
  108.5 6.5 scatter_fusion
  115.1 0.7 compare_select_fusion.10
  115.8 0.1 compare_and_fusion.4
  115.9 3.6 gather_fusion
  119.5 4.7 fusion.31
  124.1 6.5 scatter_fusion
  130.7 0.7 compare_select_fusion.10
  131.4 0.1 compare_and_fusion.4
  131.5 3.6 gather_fusion
  135.1 4.7 fusion.31
  139.7 6.5 scatter_fusion
  146.3 1.4 convert_element_type.47
  147.6 0.0 all-reduce.2.cloned.1.call-update
  147.7 0.0 all-gather.5.cloned.1.call-start
  147.7 307.3 %all-reduce.2.cloned.1.call-done = bf16[3072,256]{1,0:T(8,128)(2,1)} async-done(((bf16[3072,256]{1,0:T(8,128)(2,1)}), bf16[3072,256]{1,0:T(8,128)(2,1)}) %all-reduce.2.cloned.1.call-update) | async-done | bytes 1572880 | tf_op jit(solution)/shard_map/psum | solution.py:67
  455.1 1.6 multiply_convert_fusion.1
  456.7 0.0 all-gather.5.cloned.1.call-update
  456.8 0.0 reduce-scatter.2.cloned.1.call-start
  456.8 6.4 copy.11
  463.2 105.4 %all-gather.5.cloned.1.call-done = bf16[3072,256]{1,0:T(8,128)(2,1)} async-done(((bf16[128,256]{1,0:T(8,128)(2,1)}), bf16[3072,256]{1,0:T(8,128)(2,1)}) %all-gather.5.cloned.1.call-update) | async-done | bytes 1572880 | tf_op jit(solution)/shard_map/all_gather | solution.py:74
  568.6 2.4 broadcast_in_dim.86
  571.1 67.0 %while.29 = (s32[]{:T(128)}, f32[32,128,256]{2,1,0:T(8,128)}, s32[]{:T(128)}, s32[128]{0:T(128)S(1)}, bf16[128,128,128]{1,2,0:T(8,128)(2,1)}, /*index=5*/s32[128...) while((s32[]{:T(128)}, f32[32,128,256]{2,1,0:T(8,128)}, ...), condition=%wide.region_6.7_spmd.clone, body=%wide.region_4.6_spmd.clone.sunk | while | flops 270534016 | bytes 24122480 | solution.py:37
  571.1 0.7 compare_select_fusion.11
  571.8 0.1 compare_and_fusion.5
  571.9 2.1 gather_fusion.1
  574.0 4.0 fusion.34
  577.9 9.7 %scatter_fusion.1 = f32[32,128,256]{2,1,0:T(8,128)} fusion(f32[32,128,256]{2,1,0:T(8,128)} %get-tuple-element.494, s32[32]{0:T(128)S(1)} %compare_select_fusion.11, f32[32,128,256]{2,1,0:T(8,128)} %fusion.34), kind=kCustom, calls=%fused_computation.3.clone.clone.1 | custom fusion | flops 1048576 | bytes 12583040 | tf_op jit(solution)/shard_map/while/body/eval_jaxpr/scatter-add | solution.py:33
  587.6 0.7 compare_select_fusion.11
  588.3 0.1 compare_and_fusion.5
  588.4 2.1 gather_fusion.1
  590.5 4.0 fusion.34
  594.5 9.8 %scatter_fusion.1 = f32[32,128,256]{2,1,0:T(8,128)} fusion(f32[32,128,256]{2,1,0:T(8,128)} %get-tuple-element.494, s32[32]{0:T(128)S(1)} %compare_select_fusion.11, f32[32,128,256]{2,1,0:T(8,128)} %fusion.34), kind=kCustom, calls=%fused_computation.3.clone.clone.1 | custom fusion | flops 1048576 | bytes 12583040 | tf_op jit(solution)/shard_map/while/body/eval_jaxpr/scatter-add | solution.py:33
  604.3 0.7 compare_select_fusion.11
  605.0 0.1 compare_and_fusion.5
  605.1 2.1 gather_fusion.1
  607.2 4.0 fusion.34
  611.2 10.0 %scatter_fusion.1 = f32[32,128,256]{2,1,0:T(8,128)} fusion(f32[32,128,256]{2,1,0:T(8,128)} %get-tuple-element.494, s32[32]{0:T(128)S(1)} %compare_select_fusion.11, f32[32,128,256]{2,1,0:T(8,128)} %fusion.34), kind=kCustom, calls=%fused_computation.3.clone.clone.1 | custom fusion | flops 1048576 | bytes 12583040 | tf_op jit(solution)/shard_map/while/body/eval_jaxpr/scatter-add | solution.py:33
  621.2 0.7 compare_select_fusion.11
  621.9 0.1 compare_and_fusion.5
  622.0 2.1 gather_fusion.1
  624.1 4.0 fusion.34
  628.1 10.0 %scatter_fusion.1 = f32[32,128,256]{2,1,0:T(8,128)} fusion(f32[32,128,256]{2,1,0:T(8,128)} %get-tuple-element.494, s32[32]{0:T(128)S(1)} %compare_select_fusion.11, f32[32,128,256]{2,1,0:T(8,128)} %fusion.34), kind=kCustom, calls=%fused_computation.3.clone.clone.1 | custom fusion | flops 1048576 | bytes 12583040 | tf_op jit(solution)/shard_map/while/body/eval_jaxpr/scatter-add | solution.py:33
  638.0 3.8 convert_element_type.54
  641.9 0.0 reduce-scatter.2.cloned.1.call-update
  641.9 147.7 %reduce-scatter.2.cloned.1.call-done = bf16[128,256]{1,0:T(8,128)(2,1)} async-done(((bf16[4096,256]{1,0:T(8,128)(2,1)}), bf16[128,256]{1,0:T(8,128)(2,1)}) %reduce-scatter.2.cloned.1.call-update) | async-done | bytes 65552 | tf_op jit(solution)/shard_map/reduce_scatter | solution.py:78
  789.6 1.7 convolution_convert_fusion
  (21 shorter events, 0.1 us)
Async XLA Ops:
  7.2 0.9 copy-start
  7.2 76.7 %copy-start.5 = (s32[1,1,128]{2,1,0:T(1,128)S(1)}, s32[1,1,128]{2,1,0:T(1,128)}, u32[]{:S(2)}) copy-start(s32[1,1,128]{2,1,0:T(1,128)} %param.19) | copy-start | bytes 1540
  7.2 76.7 %copy-start.4 = (s32[1,1,128]{2,1,0:T(1,128)S(1)}, s32[1,1,128]{2,1,0:T(1,128)}, u32[]{:S(2)}) copy-start(s32[1,1,128]{2,1,0:T(1,128)} %param.18) | copy-start | bytes 1540
  7.2 76.3 %all-gather.3.cloned.1.call-start = ((), (), s32[]{:S(2)}) async-start(), calls=%async_computation.1 | async-start | bytes 2162688 | tf_op jit(solution)/shard_map/all_gather | solution.py:61
  9.7 445.4 %all-reduce.2.cloned.1.call-start = ((), (), s32[]{:S(2)}) async-start(), calls=%async_computation.2 | async-start | bytes 3145728 | tf_op jit(solution)/shard_map/psum | solution.py:67
  146.2 308.8 %copy-start.2 = (bf16[128,256]{1,0:T(8,128)(2,1)S(1)}, bf16[128,256]{1,0:T(8,128)(2,1)}, u32[]{:S(2)}) copy-start(bf16[128,256]{1,0:T(8,128)(2,1)} %fusion.18) | copy-start | bytes 196612
  146.3 308.8 %copy-start.3 = (bf16[128,256]{1,0:T(8,128)(2,1)S(1)}, bf16[128,256]{1,0:T(8,128)(2,1)}, u32[]{:S(2)}) copy-start(bf16[128,256]{1,0:T(8,128)(2,1)} %param.21) | copy-start | bytes 196612
  146.3 308.8 %copy-start.6 = (f32[256]{0:T(256)S(1)}, f32[256]{0:T(256)}, u32[]{:S(2)}) copy-start(f32[256]{0:T(256)} %param.16) | copy-start | bytes 3076
  147.7 420.9 %all-gather.5.cloned.1.call-start = ((), (), s32[]{:S(2)}) async-start(), calls=%async_computation.3 | async-start | bytes 1638400 | tf_op jit(solution)/shard_map/all_gather | solution.py:74
  456.8 332.9 %reduce-scatter.2.cloned.1.call-start = ((), (), s32[]{:S(2)}) async-start(), calls=%async_computation.4 | async-start | bytes 2162688 | tf_op jit(solution)/shard_map/reduce_scatter | solution.py:78
  638.0 151.6 %copy-start.1 = (bf16[128,256]{1,0:T(8,128)(2,1)S(1)}, bf16[128,256]{1,0:T(8,128)(2,1)}, u32[]{:S(2)}) copy-start(bf16[128,256]{1,0:T(8,128)(2,1)} %get-tuple-element.353) | copy-start | bytes 196612
Sparse Core Ops, SparseCore 0:
  11.0 72.4 all-gather.2
  147.8 307.2 all-reduce.1
  460.4 108.1 all-gather.4
  642.0 147.5 reduce-scatter.1
where the time goes:
time: 799 us; the launch traced here: 798 us
  waiting for transfers between devices  634 us (79%)
  other arithmetic  79.4 us (10%)
  matrix products  37.8 us (5%)
  local copies, waits for them, and re-layouts  32.1 us (4%)
  between operations  13.9 us (2%)
    psum x1, waiting for transfers between devices, body(): lax.psum(partial_value.astype(jnp.bfloat16), 'gc').astype(jnp.float32)  307 us
    reduce_scatter x1, waiting for transfers between devices, body(): lax.psum_scatter(back_partial.astype(jnp.bfloat16), 'gr', scatter_dimensi...  148 us
    all_gather x1, waiting for transfers between devices, body(): targets = lax.all_gather(upstream, 'gc', axis=0, tiled=True)  105 us
    all_gather x1, waiting for transfers between devices, body(): sources = lax.all_gather(scaled, 'gr', axis=0, tiled=True)  73.7 us
    scatter-add x8, other arithmetic, add_group(): return summed.at[target_part].add(product, mode='drop')  65.5 us
    gather x8, local copies, waits for them, and re-layouts, add_group(): chosen = jnp.take(blocks, pick_part, axis=0)  22.8 us
    dot_general x4, matrix products, add_group(): jnp.einsum('tik,tkf->tif', tile_part, chosen, preferred_element_type=jnp....  18.6 us
  transfers between devices with their start and end apart: 4, of which 4 were waited for; matrix products, arithmetic and copies ran while one was open for 1% of the time, Pallas kernels for 0%

commit v1 on v0

v1 whole, which is shorter than its diff:
```python
import functools

import jax
import jax.numpy as jnp
from jax import lax
from jax.experimental import pallas as pl
from jax.experimental.pallas import tpu as pltpu
from jax.sharding import Mesh
from jax.sharding import PartitionSpec as P

ZL, X, C, Y, ZH = 4, 4, 2, 8, 3
BF, F32 = jnp.bfloat16, jnp.float32
NODE_AXES = ("zl", "x", "c", "y", "zh")
UNROLL = 4


def accumulate(count_ref, pick_ref, place_ref, tiles_ref, src_ref, acc_ref, transposed):
    edge = tiles_ref.shape[-1]
    dims = (((0,), (0,)), ((), ())) if transposed else (((1,), (0,)), ((), ()))
    acc_ref[...] = jnp.zeros_like(acc_ref)

    def step(s, carry):
        products = []
        for u in range(UNROLL):
            t = s * UNROLL + u
            block = src_ref[pl.ds(pl.multiple_of(pick_ref[t] * edge, edge), edge), :]
            products.append(lax.dot_general(tiles_ref[t], block, dims, preferred_element_type=F32))
        for u in range(UNROLL):
            q = place_ref[s * UNROLL + u]
            acc_ref[pl.ds(pl.multiple_of(q * edge, edge), edge), :] += products[u]
        return carry

    lax.fori_loop(0, count_ref[0] // UNROLL, step, 0)


def forward_kernel(
    rows_a, count_ref, pick_ref, place_ref, tiles_ref, near_ref, far_ref, out_a, out_b, src, acc
):
    half = near_ref.shape[0]
    edge = tiles_ref.shape[-1]
    src[:half] = near_ref[...]
    src[half:] = far_ref[...]
    accumulate(count_ref, pick_ref, place_ref, tiles_ref, src, acc, False)
    for y in range(Y):
        for z in range(ZH):
            base = (y * ZH + z) * edge
            out_a[y, z] = acc[base : base + rows_a, :].astype(BF)
            out_b[z, y] = acc[base + rows_a : base + edge, :].astype(BF)


def backward_kernel(
    count_ref, pick_ref, place_ref, tiles_ref, part_a, part_b, near_ref, far_ref, src, acc
):
    edge = tiles_ref.shape[-1]
    rows_a = part_a.shape[2]
    for y in range(Y):
        for z in range(ZH):
            base = (y * ZH + z) * edge
            src[base : base + rows_a, :] = part_a[y, z]
            src[base + rows_a : base + edge, :] = part_b[z, y]
    accumulate(count_ref, pick_ref, place_ref, tiles_ref, src, acc, True)
    half = near_ref.shape[0]
    near_ref[...] = acc[:half, :].astype(BF)
    far_ref[...] = acc[half:, :].astype(BF)


SMEM = pl.BlockSpec(memory_space=pltpu.SMEM)
VMEM = pl.BlockSpec(memory_space=pltpu.VMEM)


def call(kernel, outs, src_rows, acc_rows, feat, *args):
    return pl.pallas_call(
        kernel,
        out_shape=tuple(jax.ShapeDtypeStruct(s, BF) for s in outs),
        in_specs=[SMEM] * 3 + [VMEM] * (len(args) - 3),
        out_specs=tuple(VMEM for _ in outs),
        scratch_shapes=[pltpu.VMEM((src_rows, feat), BF), pltpu.VMEM((acc_rows, feat), F32)],
        compiler_params=pltpu.CompilerParams(vmem_limit_bytes=40 * 1024 * 1024),
    )(*args)


def shift(n, k):
    return [(i, (i + k) % n) for i in range(n)]


def swap(value, axis):
    return lax.all_to_all(value, axis, 0, 0, tiled=True)


def spread(value, axis, size):
    return swap(jnp.broadcast_to(value[None], (size,) + value.shape), axis)


def total(value):
    return value.astype(F32).sum(0)


def body(
    features, degrees, weight, bias_term, tile_weights, tile_rows, tile_columns, tile_count, cotangent
):
    tiles = tile_weights[0, 0]
    rows, columns = tile_rows[0, 0], tile_columns[0, 0]
    count = tile_count[0]
    n, feat = features.shape
    my_x, my_c = lax.axis_index("x"), lax.axis_index("c")
    block_zl, block_x, block_c = columns // (X * C), columns // C % X, columns % C
    column_at = (block_c != my_c) * (X * ZL) + (my_x - block_x + X) % X * ZL + block_zl
    column_at = column_at.astype(jnp.int32)
    inv_root = lax.rsqrt(degrees.astype(F32))[:, None]
    hidden = jnp.dot(features, weight, preferred_element_type=F32)
    scaled = (hidden * inv_root).astype(BF)

    along_z = lax.all_gather(scaled, "zl", axis=0, tiled=True)
    near = jnp.concatenate(
        [along_z] + [lax.ppermute(along_z, "x", shift(X, k)) for k in range(1, X)], 0
    )
    far = lax.ppermute(near, "c", shift(C, 1))

    rows_a = 80
    rows_b = n - rows_a
    part_a, part_b = call(
        functools.partial(forward_kernel, rows_a),
        [(Y, ZH, rows_a, feat), (ZH, Y, rows_b, feat)],
        C * X * ZL * n, Y * ZH * n, feat,
        count, column_at, rows, tiles, near, far,
    )
    got_a = total(swap(part_a, "y")).astype(BF)
    got_b = total(swap(part_b, "zh")).astype(BF)
    own_a = total(swap(got_a, "zh"))
    own_b = total(swap(got_b, "y"))
    own_rows = jnp.concatenate([own_a, own_b], 0)

    preact = inv_root * (own_rows + scaled.astype(F32)) + bias_term[None, :]
    sigmoid_value = jax.nn.sigmoid(preact)
    activations = (preact * sigmoid_value).astype(BF)
    slope_value = sigmoid_value * (1.0 + preact * (1.0 - sigmoid_value))
    upstream = (cotangent.astype(F32) * slope_value * inv_root).astype(BF)

    up_a, up_b = upstream[:rows_a], upstream[rows_a:]
    up_a = spread(spread(up_a, "zh", ZH), "y", Y)
    up_b = spread(spread(up_b, "y", Y), "zh", ZH)
    half = (X * ZL * n, feat)
    own_half, other_half = call(
        backward_kernel, [half, half], Y * ZH * n, C * X * ZL * n, feat,
        count, rows, column_at, tiles, up_a, up_b,
    )
    other_half = lax.ppermute(other_half, "c", shift(C, 1))
    both = (own_half.astype(F32) + other_half.astype(F32)).astype(BF).reshape(X, ZL * n, feat)
    along_x = both[0].astype(F32)
    for k in range(1, X):
        along_x += lax.ppermute(both[k], "x", shift(X, -k)).astype(F32)
    own_back = total(swap(along_x.astype(BF).reshape(ZL, n, feat), "zl"))
    grad_hidden = (inv_root * (own_back + upstream.astype(F32))).astype(BF)
    feature_grad = jnp.einsum("nf,gf->ng", grad_hidden, weight, preferred_element_type=F32)
    return activations, feature_grad.astype(BF)


def solution(mesh):
    fine = Mesh(mesh.devices.reshape(ZL, X, C, Y, ZH), NODE_AXES)
    gr, gc = ("zl", "x", "c"), ("y", "zh")
    nodes = P(NODE_AXES, None)

    return jax.shard_map(
        body,
        mesh=fine,
        in_specs=(
            nodes, P(NODE_AXES), P(), P(), P(gr, gc, None, None, None), P(gr, gc, None), P(gr, gc, None),
            P(gr, gc), nodes,
        ),
        out_specs=(nodes, nodes),
        check_vma=False,
    )
```

time: 799 us -> 270 us (0.34)
  the two profiles are of different devices: /device:TPU:24 before, /device:TPU:8 now
where the time goes in v1:
time: 270 us; the launch traced here: 269 us
  blocking collectives  132 us (49%)
  waiting for transfers between devices  71.3 us (26%)
  starting transfers between devices  50.2 us (19%)
  Pallas kernels  5.05 us (2%)
  other arithmetic  3.62 us (1%)
  local copies, waits for them, and re-layouts  3.27 us (1%)
    all_to_all x5, blocking collectives, swap(): return lax.all_to_all(value, axis, 0, 0, tiled=True)  115 us
    all_to_all x4, waiting for transfers between devices, swap(): return lax.all_to_all(value, axis, 0, 0, tiled=True)  49.3 us
    all_to_all x4, starting transfers between devices, swap(): return lax.all_to_all(value, axis, 0, 0, tiled=True)  22.2 us
    all_gather x1, blocking collectives, body(): along_z = lax.all_gather(scaled, 'zl', axis=0, tiled=True)  16.4 us
    ppermute x3, waiting for transfers between devices, body(): along_x += lax.ppermute(both[k], 'x', shift(X, -k)).astype(F32)  11.4 us
    ppermute x3, starting transfers between devices, body(): lax.ppermute(along_z, 'x', shift(X, k))  11.4 us
    ppermute x3, starting transfers between devices, body(): along_x += lax.ppermute(both[k], 'x', shift(X, -k)).astype(F32)  7.78 us
    ppermute x1, starting transfers between devices, body(): other_half = lax.ppermute(other_half, 'c', shift(C, 1))  6.94 us
  transfers between devices with their start and end apart: 12, of which 11 were waited for; matrix products, arithmetic and copies ran while one was open for 1% of the time, Pallas kernels for 0%

profile of v1, /device:TPU:8, one launch (start us, length us, event | category | flops | bytes accessed | tf_op | source)
XLA Modules:
  0.0 268.6 jit_solution(17956092896607819318)
XLA Ops:
  0.6 0.0 copy-start
  0.6 0.0 copy-start.6
  0.7 0.0 copy-start.3
  0.7 0.7 convert_rsqrt_fusion
  1.4 0.2 copy-done
  1.5 1.0 fusion
  2.5 16.4 %all_gather.3 = bf16[512,256]{1,0:T(8,128)(2,1)S(1)} all-gather(bf16[128,256]{1,0:T(8,128)(2,1)S(1)} %fusion), channel_id=1, replica_groups=mesh['zl'=4,'x'=4,'c'=2,'y'=8,'zh'=3] {'zl'}, dimensions={0}, use_global_device_ids=true | all-gather | bytes 327680 | tf_op jit(solution)/shard_map/all_gather | solution.py:113
  18.9 3.4 %collective-permute-start = (bf16[512,256]{1,0:T(8,128)(2,1)S(1)}, bf16[512,256]{1,0:T(8,128)(2,1)S(1)}, u32[]{:S(2)}, u32[]{:S(2)}) collective-permute-start(bf16[512,256]{1,0:T(8,128)(2,1)S(1)} %all_gather.3), channel_id=1, source_target_pairs={{0,48},{48,96},{96,144},{144,0},{1,49},{49,97},{97,145},{145,1},{2... | collective-permute-start | bytes 786440 | tf_op jit(solution)/shard_map/ppermute | solution.py:115
  22.3 4.6 %collective-permute-start.1 = (bf16[512,256]{1,0:T(8,128)(2,1)S(1)}, bf16[512,256]{1,0:T(8,128)(2,1)S(1)}, u32[]{:S(2)}, u32[]{:S(2)}) collective-permute-start(bf16[512,256]{1,0:T(8,128)(2,1)S(1)} %all_gather.3), channel_id=1, source_target_pairs={{0,96},{48,144},{96,0},{144,48},{1,97},{49,145},{97,1},{145,49},{2... | collective-permute-start | bytes 786440 | tf_op jit(solution)/shard_map/ppermute | solution.py:115
  27.0 3.3 %collective-permute-start.2 = (bf16[512,256]{1,0:T(8,128)(2,1)S(1)}, bf16[512,256]{1,0:T(8,128)(2,1)S(1)}, u32[]{:S(2)}, u32[]{:S(2)}) collective-permute-start(bf16[512,256]{1,0:T(8,128)(2,1)S(1)} %all_gather.3), channel_id=1, source_target_pairs={{0,144},{48,0},{96,48},{144,96},{1,145},{49,1},{97,49},{145,97},{2... | collective-permute-start | bytes 786440 | tf_op jit(solution)/shard_map/ppermute | solution.py:115
  30.4 0.9 collective-permute-done
  31.2 3.3 %collective-permute-done.1 = bf16[512,256]{1,0:T(8,128)(2,1)S(1)} collective-permute-done((bf16[512,256]{1,0:T(8,128)(2,1)S(1)}, bf16[512,256]{1,0:T(8,128)(2,1)S(1)}, u32[]{:S(2)}, u32[]{:S(2)}) %collective-permute-start.1) | collective-permute-done | bytes 262176 | tf_op jit(solution)/shard_map/ppermute | solution.py:115
  34.6 2.2 collective-permute-done.2
  36.8 1.9 collective-permute-start.3
  39.4 0.0 copy-done.6
  39.4 1.9 collective-permute-done.3.far_ref
  41.4 0.0 copy-done.3
  41.4 0.0 copy-start.1
  41.4 2.2 copy-done.1
  43.6 2.9 %shard_map.104 = (bf16[8,3,80,256]{3,2,1,0:T(8,128)(2,1)}, bf16[3,8,48,256]{3,2,1,0:T(8,128)(2,1)S(1)}) custom-call(s32[1]{0:T(128)} %bitcast.23.count_ref, s32[128]{0:T(128)S(1)} %fusion.5.pick_ref.place_ref, s32[128]{0:T(128)S(1)} %bitcast.27, bf16[128,128,128]{2,1,0:T(8,128)(2,1)S(1)} %bitcast.25, ...), custom_call_target="tpu_custom_call" | custom-call | tf_op jit(solution)/shard_map/pallas_call | solution.py:72
  46.4 34.9 %all_to_all.45 = bf16[3,8,48,256]{3,2,1,0:T(8,128)(2,1)S(1)} all-to-all(bf16[3,8,48,256]{3,2,1,0:T(8,128)(2,1)S(1)} %get-tuple-element.7), channel_id=1, replica_groups=mesh['zl'=4,'x'=4,'c'=2,'y'=8,'zh'=3] {'zh'}, dimensions={0} | all-to-all | bytes 1179648 | tf_op jit(solution)/shard_map/all_to_all | solution.py:87
  81.3 0.0 copy-start.4
  81.3 0.0 copy-start.5
  81.3 9.4 %all-to-all-start = ((bf16[8,3,80,256]{3,2,1,0:T(8,128)(2,1)}), bf16[8,3,80,256]{3,2,1,0:T(8,128)(2,1)S(1)}, u32[]{:S(2)}, u32[]{:S(2)}) async-start(bf16[8,3,80,256]{3,2,1,0:T(8,128)(2,1)} %get-tuple-element.6), calls=%async_computation | async-start | bytes 1966080 | tf_op jit(solution)/shard_map/all_to_all | solution.py:87
  90.8 0.8 reduce_sum.53
  91.6 24.2 %all-to-all-done = bf16[8,3,80,256]{3,2,1,0:T(8,128)(2,1)S(1)} async-done(((bf16[8,3,80,256]{3,2,1,0:T(8,128)(2,1)}), bf16[8,3,80,256]{3,2,1,0:T(8,128)(2,1)S(1)}, u32[]{:S(2)}, u32[]{:S(2)}) %all-to-all-start) | async-done | bytes 983072 | tf_op jit(solution)/shard_map/all_to_all | solution.py:87
  115.8 4.8 %all-to-all-start.3 = ((bf16[8,48,256]{2,1,0:T(8,128)(2,1)}), bf16[8,48,256]{2,1,0:T(8,128)(2,1)S(1)}, u32[]{:S(2)}, u32[]{:S(2)}) async-start(bf16[8,48,256]{2,1,0:T(8,128)(2,1)} %reduce_sum.53), calls=%async_computation.3 | async-start | bytes 393216 | tf_op jit(solution)/shard_map/all_to_all | solution.py:87
  120.5 0.8 reduce_sum.51
  121.3 8.7 %all-to-all-done.3 = bf16[8,48,256]{2,1,0:T(8,128)(2,1)S(1)} async-done(((bf16[8,48,256]{2,1,0:T(8,128)(2,1)}), bf16[8,48,256]{2,1,0:T(8,128)(2,1)S(1)}, u32[]{:S(2)}, u32[]{:S(2)}) %all-to-all-start.3) | async-done | bytes 196640 | tf_op jit(solution)/shard_map/all_to_all | solution.py:87
  130.0 3.8 %all-to-all-start.1 = ((bf16[3,80,256]{2,1,0:T(8,128)(2,1)}), bf16[3,80,256]{2,1,0:T(8,128)(2,1)S(1)}, u32[]{:S(2)}, u32[]{:S(2)}) async-start(bf16[3,80,256]{2,1,0:T(8,128)(2,1)} %reduce_sum.51), calls=%async_computation.1 | async-start | bytes 245760 | tf_op jit(solution)/shard_map/all_to_all | solution.py:87
  133.9 8.1 %all-to-all-done.1 = bf16[3,80,256]{2,1,0:T(8,128)(2,1)S(1)} async-done(((bf16[3,80,256]{2,1,0:T(8,128)(2,1)}), bf16[3,80,256]{2,1,0:T(8,128)(2,1)S(1)}, u32[]{:S(2)}, u32[]{:S(2)}) %all-to-all-start.1) | async-done | bytes 122912 | tf_op jit(solution)/shard_map/all_to_all | solution.py:87
  142.1 0.0 copy-done.4
  142.1 0.0 copy-done.5
  142.1 0.8 multiply_convert_fusion.1
  142.9 0.7 broadcast_in_dim.8
  143.5 4.2 %all-to-all-start.4 = ((bf16[3,80,256]{2,1,0:T(8,128)(2,1)}), bf16[3,80,256]{2,1,0:T(8,128)(2,1)S(1)}, u32[]{:S(2)}, u32[]{:S(2)}) async-start(bf16[3,80,256]{2,1,0:T(8,128)(2,1)} %broadcast_in_dim.8), calls=%async_computation.4 | async-start | bytes 245760 | tf_op jit(solution)/shard_map/all_to_all | solution.py:87
  147.7 8.2 %all-to-all-done.4 = bf16[3,80,256]{2,1,0:T(8,128)(2,1)S(1)} async-done(((bf16[3,80,256]{2,1,0:T(8,128)(2,1)}), bf16[3,80,256]{2,1,0:T(8,128)(2,1)S(1)}, u32[]{:S(2)}, u32[]{:S(2)}) %all-to-all-start.4) | async-done | bytes 122912 | tf_op jit(solution)/shard_map/all_to_all | solution.py:87
  156.0 12.7 %all_to_all.46 = bf16[8,48,256]{2,1,0:T(8,128)(2,1)S(1)} all-to-all(bf16[8,48,256]{2,1,0:T(8,128)(2,1)S(1)} %broadcast_in_dim.10), channel_id=1, replica_groups=mesh['zl'=4,'x'=4,'c'=2,'y'=8,'zh'=3] {'y'}, dimensions={0} | all-to-all | bytes 393216 | tf_op jit(solution)/shard_map/all_to_all | solution.py:87
  168.7 0.0 copy-start.2
  168.7 23.2 %all_to_all.47.part_b = bf16[3,8,48,256]{3,2,1,0:T(8,128)(2,1)S(1)} all-to-all(bf16[3,8,48,256]{3,2,1,0:T(8,128)(2,1)S(1)} %broadcast_in_dim.11), channel_id=1, replica_groups=mesh['zl'=4,'x'=4,'c'=2,'y'=8,'zh'=3] {'zh'}, dimensions={0} | all-to-all | bytes 1179648 | tf_op jit(solution)/shard_map/all_to_all | solution.py:87
  191.9 0.1 broadcast_in_dim.9
  191.9 29.5 %all_to_all.48.part_a = bf16[8,3,80,256]{3,2,1,0:T(8,128)(2,1)S(1)} all-to-all(bf16[8,3,80,256]{3,2,1,0:T(8,128)(2,1)S(1)} %broadcast_in_dim.9), channel_id=1, replica_groups=mesh['zl'=4,'x'=4,'c'=2,'y'=8,'zh'=3] {'y'}, dimensions={0} | all-to-all | bytes 1966080 | tf_op jit(solution)/shard_map/all_to_all | solution.py:87
  221.4 0.0 copy-done.2
  221.4 2.2 shard_map.105
  223.6 6.9 %collective-permute-start.4 = (bf16[2048,256]{1,0:T(8,128)(2,1)S(1)}, bf16[2048,256]{1,0:T(8,128)(2,1)S(1)}, u32[]{:S(2)}, u32[]{:S(2)}) collective-permute-start(bf16[2048,256]{1,0:T(8,128)(2,1)S(1)} %get-tuple-element.9), channel_id=1, source_target_pairs={{0,24},{24,0},{1,25},{25,1},{2,26},{26,2},{3,27},{27,3},{4,28},{28... | collective-permute-start | bytes 3145736 | tf_op jit(solution)/shard_map/ppermute | solution.py:147
  230.6 2.3 collective-permute-done.4
  232.8 0.3 add_convert_fusion
  233.1 0.1 fusion.11
  233.2 1.9 collective-permute-start.5
  235.1 3.9 %collective-permute-start.7 = (bf16[512,256]{1,0:T(8,128)(2,1)S(1)}, bf16[512,256]{1,0:T(8,128)(2,1)S(1)}, u32[]{:S(2)}, u32[]{:S(2)}) collective-permute-start(bf16[512,256]{1,0:T(8,128)(2,1)S(1)} %get-tuple-element.11), channel_id=1, source_target_pairs={{0,48},{48,96},{96,144},{144,0},{1,49},{49,97},{97,145},{145,1},{2... | collective-permute-start | bytes 786440 | tf_op jit(solution)/shard_map/ppermute | solution.py:151
  239.1 1.9 collective-permute-start.6
  241.0 2.7 collective-permute-done.5
  243.7 8.8 %collective-permute-done.7 = bf16[512,256]{1,0:T(8,128)(2,1)S(1)} collective-permute-done((bf16[512,256]{1,0:T(8,128)(2,1)S(1)}, bf16[512,256]{1,0:T(8,128)(2,1)S(1)}, u32[]{:S(2)}, u32[]{:S(2)}) %collective-permute-start.7) | collective-permute-done | bytes 262176 | tf_op jit(solution)/shard_map/ppermute | solution.py:151
  252.4 0.0 collective-permute-done.6
  252.4 0.1 add_convert_fusion.1
  252.6 15.1 %all_to_all.49 = bf16[4,128,256]{2,1,0:T(8,128)(2,1)S(1)} all-to-all(bf16[4,128,256]{2,1,0:T(8,128)(2,1)S(1)} %bitcast.29), channel_id=1, replica_groups=mesh['zl'=4,'x'=4,'c'=2,'y'=8,'zh'=3] {'zl'}, dimensions={0} | all-to-all | bytes 524288 | tf_op jit(solution)/shard_map/all_to_all | solution.py:87
  267.7 0.8 convolution_convert_fusion
  (12 shorter events, 0.2 us)
Async XLA Ops:
  0.6 0.9 copy-start
  0.6 38.8 %copy-start.6 = (s32[1,1,128]{2,1,0:T(1,128)S(1)}, s32[1,1,128]{2,1,0:T(1,128)}, u32[]{:S(2)}) copy-start(s32[1,1,128]{2,1,0:T(1,128)} %param.15) | copy-start | bytes 1540
  0.7 40.7 %copy-start.3 = (s32[1,1,128]{2,1,0:T(1,128)S(1)}, s32[1,1,128]{2,1,0:T(1,128)}, u32[]{:S(2)}) copy-start(s32[1,1,128]{2,1,0:T(1,128)} %param.14) | copy-start | bytes 1540
  18.9 12.3 %collective-permute-start = (bf16[512,256]{1,0:T(8,128)(2,1)S(1)}, bf16[512,256]{1,0:T(8,128)(2,1)S(1)}, u32[]{:S(2)}, u32[]{:S(2)}) collective-permute-start(bf16[512,256]{1,0:T(8,128)(2,1)S(1)} %all_gather.3), channel_id=1, source_target_pairs={{0,48},{48,96},{96,144},{144,0},{1,49},{49,97},{97,145},{145,1},{2... | collective-permute-start | bytes 786440 | tf_op jit(solution)/shard_map/ppermute | solution.py:115
  22.3 12.2 %collective-permute-start.1 = (bf16[512,256]{1,0:T(8,128)(2,1)S(1)}, bf16[512,256]{1,0:T(8,128)(2,1)S(1)}, u32[]{:S(2)}, u32[]{:S(2)}) collective-permute-start(bf16[512,256]{1,0:T(8,128)(2,1)S(1)} %all_gather.3), channel_id=1, source_target_pairs={{0,96},{48,144},{96,0},{144,48},{1,97},{49,145},{97,1},{145,49},{2... | collective-permute-start | bytes 786440 | tf_op jit(solution)/shard_map/ppermute | solution.py:115
  27.0 9.8 %collective-permute-start.2 = (bf16[512,256]{1,0:T(8,128)(2,1)S(1)}, bf16[512,256]{1,0:T(8,128)(2,1)S(1)}, u32[]{:S(2)}, u32[]{:S(2)}) collective-permute-start(bf16[512,256]{1,0:T(8,128)(2,1)S(1)} %all_gather.3), channel_id=1, source_target_pairs={{0,144},{48,0},{96,48},{144,96},{1,145},{49,1},{97,49},{145,97},{2... | collective-permute-start | bytes 786440 | tf_op jit(solution)/shard_map/ppermute | solution.py:115
  36.8 4.6 %collective-permute-start.3 = (bf16[2048,256]{1,0:T(8,128)(2,1)S(1)}, bf16[2048,256]{1,0:T(8,128)(2,1)S(1)}, u32[]{:S(2)}, u32[]{:S(2)}) collective-permute-start(bf16[2048,256]{1,0:T(8,128)(2,1)S(1)} %constant_dynamic-update-slice_fusion.near_ref), channel_id=1, source_target_pairs={{0,24},{24,0},{1,25},{25,1},{2,26},{26,2},{3,27},{27,3},{4,28},{28... | collective-permute-start | bytes 3145736 | tf_op jit(solution)/shard_map/ppermute | solution.py:117
  41.4 2.2 copy-start.1
  81.3 60.7 %copy-start.4 = (bf16[128,256]{1,0:T(8,128)(2,1)S(1)}, bf16[128,256]{1,0:T(8,128)(2,1)}, u32[]{:S(2)}) copy-start(bf16[128,256]{1,0:T(8,128)(2,1)} %param.17) | copy-start | bytes 196612
  81.3 60.7 %copy-start.5 = (f32[256]{0:T(256)S(1)}, f32[256]{0:T(256)}, u32[]{:S(2)}) copy-start(f32[256]{0:T(256)} %param.12) | copy-start | bytes 3076
  81.3 34.4 %all-to-all-start = ((bf16[8,3,80,256]{3,2,1,0:T(8,128)(2,1)}), bf16[8,3,80,256]{3,2,1,0:T(8,128)(2,1)S(1)}, u32[]{:S(2)}, u32[]{:S(2)}) async-start(bf16[8,3,80,256]{3,2,1,0:T(8,128)(2,1)} %get-tuple-element.6), calls=%async_computation | async-start | bytes 1966080 | tf_op jit(solution)/shard_map/all_to_all | solution.py:87
  115.8 14.3 %all-to-all-start.3 = ((bf16[8,48,256]{2,1,0:T(8,128)(2,1)}), bf16[8,48,256]{2,1,0:T(8,128)(2,1)S(1)}, u32[]{:S(2)}, u32[]{:S(2)}) async-start(bf16[8,48,256]{2,1,0:T(8,128)(2,1)} %reduce_sum.53), calls=%async_computation.3 | async-start | bytes 393216 | tf_op jit(solution)/shard_map/all_to_all | solution.py:87
  130.0 12.0 %all-to-all-start.1 = ((bf16[3,80,256]{2,1,0:T(8,128)(2,1)}), bf16[3,80,256]{2,1,0:T(8,128)(2,1)S(1)}, u32[]{:S(2)}, u32[]{:S(2)}) async-start(bf16[3,80,256]{2,1,0:T(8,128)(2,1)} %reduce_sum.51), calls=%async_computation.1 | async-start | bytes 245760 | tf_op jit(solution)/shard_map/all_to_all | solution.py:87
  143.5 12.4 %all-to-all-start.4 = ((bf16[3,80,256]{2,1,0:T(8,128)(2,1)}), bf16[3,80,256]{2,1,0:T(8,128)(2,1)S(1)}, u32[]{:S(2)}, u32[]{:S(2)}) async-start(bf16[3,80,256]{2,1,0:T(8,128)(2,1)} %broadcast_in_dim.8), calls=%async_computation.4 | async-start | bytes 245760 | tf_op jit(solution)/shard_map/all_to_all | solution.py:87
  168.7 52.7 %copy-start.2 = (bf16[1,1,128,128,128]{4,3,2,1,0:T(8,128)(2,1)S(1)}, bf16[1,1,128,128,128]{4,3,2,1,0:T(8,128)(2,1)}, u32[]{:S(2)}) copy-start(bf16[1,1,128,128,128]{4,3,2,1,0:T(8,128)(2,1)} %param.13) | copy-start | bytes 12582916
  223.6 9.2 %collective-permute-start.4 = (bf16[2048,256]{1,0:T(8,128)(2,1)S(1)}, bf16[2048,256]{1,0:T(8,128)(2,1)S(1)}, u32[]{:S(2)}, u32[]{:S(2)}) collective-permute-start(bf16[2048,256]{1,0:T(8,128)(2,1)S(1)} %get-tuple-element.9), channel_id=1, source_target_pairs={{0,24},{24,0},{1,25},{25,1},{2,26},{26,2},{3,27},{27,3},{4,28},{28... | collective-permute-start | bytes 3145736 | tf_op jit(solution)/shard_map/ppermute | solution.py:147
  233.2 10.5 %collective-permute-start.5 = (bf16[512,256]{1,0:T(8,128)(2,1)S(1)}, bf16[512,256]{1,0:T(8,128)(2,1)S(1)}, u32[]{:S(2)}, u32[]{:S(2)}) collective-permute-start(bf16[512,256]{1,0:T(8,128)(2,1)S(1)} %get-tuple-element.10), channel_id=1, source_target_pairs={{0,144},{48,0},{96,48},{144,96},{1,145},{49,1},{97,49},{145,97},{2... | collective-permute-start | bytes 786440 | tf_op jit(solution)/shard_map/ppermute | solution.py:151
  235.1 17.3 %collective-permute-start.7 = (bf16[512,256]{1,0:T(8,128)(2,1)S(1)}, bf16[512,256]{1,0:T(8,128)(2,1)S(1)}, u32[]{:S(2)}, u32[]{:S(2)}) collective-permute-start(bf16[512,256]{1,0:T(8,128)(2,1)S(1)} %get-tuple-element.11), channel_id=1, source_target_pairs={{0,48},{48,96},{96,144},{144,0},{1,49},{49,97},{97,145},{145,1},{2... | collective-permute-start | bytes 786440 | tf_op jit(solution)/shard_map/ppermute | solution.py:151
  239.1 13.4 %collective-permute-start.6 = (bf16[512,256]{1,0:T(8,128)(2,1)S(1)}, bf16[512,256]{1,0:T(8,128)(2,1)S(1)}, u32[]{:S(2)}, u32[]{:S(2)}) collective-permute-start(bf16[512,256]{1,0:T(8,128)(2,1)S(1)} %get-tuple-element.12), channel_id=1, source_target_pairs={{0,96},{48,144},{96,0},{144,48},{1,97},{49,145},{97,1},{145,49},{2... | collective-permute-start | bytes 786440 | tf_op jit(solution)/shard_map/ppermute | solution.py:151

commit v2 on v1

--- a/solution.py
+++ b/solution.py
@@ -34,30 +34,30 @@
 
 
 def forward_kernel(
-    rows_a, count_ref, pick_ref, place_ref, tiles_ref, near_ref, far_ref, out_a, out_b, src, acc
+    rows_a, count_ref, pick_ref, place_ref, zh_ref, tiles_ref, near_ref, far_ref, out_a, *rest
 ):
+    out_b, (src, acc) = rest[:ZH], rest[ZH:]
     half = near_ref.shape[0]
     edge = tiles_ref.shape[-1]
     src[:half] = near_ref[...]
     src[half:] = far_ref[...]
     accumulate(count_ref, pick_ref, place_ref, tiles_ref, src, acc, False)
     for y in range(Y):
-        for z in range(ZH):
-            base = (y * ZH + z) * edge
-            out_a[y, z] = acc[base : base + rows_a, :].astype(BF)
-            out_b[z, y] = acc[base + rows_a : base + edge, :].astype(BF)
+        for k in range(ZH):
+            base = pl.multiple_of((y * ZH + (zh_ref[0] + k) % ZH) * edge, edge)
+            out_a[y, k] = acc[pl.ds(base, rows_a), :].astype(BF)
+            out_b[k][y] = acc[pl.ds(base + rows_a, edge - rows_a), :].astype(BF)
 
 
-def backward_kernel(
-    count_ref, pick_ref, place_ref, tiles_ref, part_a, part_b, near_ref, far_ref, src, acc
-):
+def backward_kernel(count_ref, pick_ref, place_ref, zh_ref, tiles_ref, part_a, *rest):
+    part_b, (near_ref, far_ref, src, acc) = rest[:ZH], rest[ZH:]
     edge = tiles_ref.shape[-1]
     rows_a = part_a.shape[2]
     for y in range(Y):
-        for z in range(ZH):
-            base = (y * ZH + z) * edge
-            src[base : base + rows_a, :] = part_a[y, z]
-            src[base + rows_a : base + edge, :] = part_b[z, y]
+        for k in range(ZH):
+            base = pl.multiple_of((y * ZH + (zh_ref[0] + ZH - k) % ZH) * edge, edge)
+            src[pl.ds(base, rows_a), :] = part_a[y, k]
+            src[pl.ds(base + rows_a, edge - rows_a), :] = part_b[k][y]
     accumulate(count_ref, pick_ref, place_ref, tiles_ref, src, acc, True)
     half = near_ref.shape[0]
     near_ref[...] = acc[:half, :].astype(BF)
@@ -72,7 +72,7 @@
     return pl.pallas_call(
         kernel,
         out_shape=tuple(jax.ShapeDtypeStruct(s, BF) for s in outs),
-        in_specs=[SMEM] * 3 + [VMEM] * (len(args) - 3),
+        in_specs=[SMEM] * 4 + [VMEM] * (len(args) - 4),
         out_specs=tuple(VMEM for _ in outs),
         scratch_shapes=[pltpu.VMEM((src_rows, feat), BF), pltpu.VMEM((acc_rows, feat), F32)],
         compiler_params=pltpu.CompilerParams(vmem_limit_bytes=40 * 1024 * 1024),
@@ -91,6 +91,15 @@
     return swap(jnp.broadcast_to(value[None], (size,) + value.shape), axis)
 
 
+def collect(pieces):
+    moved = [pieces[0]] + [lax.ppermute(pieces[k], "zh", shift(ZH, k)) for k in range(1, ZH)]
+    return sum(piece.astype(F32) for piece in moved)
+
+
+def share(value):
+    return [value] + [lax.ppermute(value, "zh", shift(ZH, k)) for k in range(1, ZH)]
+
+
 def total(value):
     return value.astype(F32).sum(0)
 
@@ -103,9 +112,11 @@
     count = tile_count[0]
     n, feat = features.shape
     my_x, my_c = lax.axis_index("x"), lax.axis_index("c")
+    my_zh = lax.axis_index("zh").astype(jnp.int32)[None]
     block_zl, block_x, block_c = columns // (X * C), columns // C % X, columns % C
-    column_at = (block_c != my_c) * (X * ZL) + (my_x - block_x + X) % X * ZL + block_zl
-    column_at = column_at.astype(jnp.int32)
+    other = (block_c != my_c).astype(jnp.int32) * (X * ZL)
+    column_at = other + (my_x - block_x + X) % X * ZL + block_zl
+    sum_at = other + block_x * ZL + block_zl
     inv_root = lax.rsqrt(degrees.astype(F32))[:, None]
     hidden = jnp.dot(features, weight, preferred_element_type=F32)
     scaled = (hidden * inv_root).astype(BF)
@@ -118,15 +129,15 @@
 
     rows_a = 80
     rows_b = n - rows_a
-    part_a, part_b = call(
+    part_a, *part_b = call(
         functools.partial(forward_kernel, rows_a),
-        [(Y, ZH, rows_a, feat), (ZH, Y, rows_b, feat)],
+        [(Y, ZH, rows_a, feat)] + [(Y, rows_b, feat)] * ZH,
         C * X * ZL * n, Y * ZH * n, feat,
-        count, column_at, rows, tiles, near, far,
+        count, column_at, rows, my_zh, tiles, near, far,
     )
+    got_b = collect(part_b).astype(BF)
     got_a = total(swap(part_a, "y")).astype(BF)
-    got_b = total(swap(part_b, "zh")).astype(BF)
-    own_a = total(swap(got_a, "zh"))
+    own_a = collect([got_a[k] for k in range(ZH)])
     own_b = total(swap(got_b, "y"))
     own_rows = jnp.concatenate([own_a, own_b], 0)
 
@@ -137,19 +148,17 @@
     upstream = (cotangent.astype(F32) * slope_value * inv_root).astype(BF)
 
     up_a, up_b = upstream[:rows_a], upstream[rows_a:]
-    up_a = spread(spread(up_a, "zh", ZH), "y", Y)
-    up_b = spread(spread(up_b, "y", Y), "zh", ZH)
+    up_b = share(spread(up_b, "y", Y))
+    up_a = spread(jnp.stack(share(up_a)), "y", Y)
     half = (X * ZL * n, feat)
     own_half, other_half = call(
         backward_kernel, [half, half], Y * ZH * n, C * X * ZL * n, feat,
-        count, rows, column_at, tiles, up_a, up_b,
+        count, rows, sum_at, my_zh, tiles, up_a, *up_b,
     )
     other_half = lax.ppermute(other_half, "c", shift(C, 1))
     both = (own_half.astype(F32) + other_half.astype(F32)).astype(BF).reshape(X, ZL * n, feat)
-    along_x = both[0].astype(F32)
-    for k in range(1, X):
-        along_x += lax.ppermute(both[k], "x", shift(X, -k)).astype(F32)
-    own_back = total(swap(along_x.astype(BF).reshape(ZL, n, feat), "zl"))
+    along_x = total(swap(both, "x")).astype(BF).reshape(ZL, n, feat)
+    own_back = total(swap(along_x, "zl"))
     grad_hidden = (inv_root * (own_back + upstream.astype(F32))).astype(BF)
     feature_grad = jnp.einsum("nf,gf->ng", grad_hidden, weight, preferred_element_type=F32)
     return activations, feature_grad.astype(BF)

time: 270 us -> 218 us (0.81)
  the two profiles are of different devices: /device:TPU:8 before, /device:TPU:2 now
where the time goes in v2:
time: 218 us; the launch traced here: 217 us
  starting transfers between devices  85.7 us (39%)
  waiting for transfers between devices  53.5 us (25%)
  blocking collectives  46.1 us (21%)
  Pallas kernels  19.1 us (9%)
  local copies, waits for them, and re-layouts  6.36 us (3%)
  other arithmetic  3.06 us (1%)
    all_to_all x2, blocking collectives, swap(): return lax.all_to_all(value, axis, 0, 0, tiled=True)  29.7 us
    all_to_all x4, starting transfers between devices, swap(): return lax.all_to_all(value, axis, 0, 0, tiled=True)  25.1 us
    ppermute x4, waiting for transfers between devices, collect(): lax.ppermute(pieces[k], 'zh', shift(ZH, k))  23.7 us
    ppermute x4, starting transfers between devices, collect(): lax.ppermute(pieces[k], 'zh', shift(ZH, k))  22.4 us
    ppermute x4, starting transfers between devices, share(): lax.ppermute(value, 'zh', shift(ZH, k))  19.5 us
    pallas_call x2, Pallas kernels, call(): pl.pallas_call(kernel, out_shape=tuple((jax.ShapeDtypeStruct(s, BF) for s...  19.1 us
    all_gather x1, blocking collectives, body(): along_z = lax.all_gather(scaled, 'zl', axis=0, tiled=True)  16.4 us
    ppermute x4, waiting for transfers between devices, share(): lax.ppermute(value, 'zh', shift(ZH, k))  15.4 us
  transfers between devices with their start and end apart: 17, of which 12 were waited for; matrix products, arithmetic and copies ran while one was open for 0% of the time, Pallas kernels for 0%

profile of v2, /device:TPU:2, one launch (start us, length us, event | category | flops | bytes accessed | tf_op | source)
XLA Modules:
  0.0 217.1 jit_solution(8958561897538300512)
XLA Ops:
  0.6 0.0 copy-start
  0.6 0.0 copy-start.6
  0.7 0.0 copy-start.3
  0.7 0.7 convert_rsqrt_fusion
  1.4 0.2 copy-done
  1.5 1.0 fusion
  2.5 16.4 %all_gather.3 = bf16[512,256]{1,0:T(8,128)(2,1)S(1)} all-gather(bf16[128,256]{1,0:T(8,128)(2,1)S(1)} %fusion), channel_id=1, replica_groups=mesh['zl'=4,'x'=4,'c'=2,'y'=8,'zh'=3] {'zl'}, dimensions={0}, use_global_device_ids=true | all-gather | bytes 327680 | tf_op jit(solution)/shard_map/all_gather | solution.py:124
  18.9 3.4 %collective-permute-start = (bf16[512,256]{1,0:T(8,128)(2,1)S(1)}, bf16[512,256]{1,0:T(8,128)(2,1)S(1)}, u32[]{:S(2)}, u32[]{:S(2)}) collective-permute-start(bf16[512,256]{1,0:T(8,128)(2,1)S(1)} %all_gather.3), channel_id=1, source_target_pairs={{0,48},{48,96},{96,144},{144,0},{1,49},{49,97},{97,145},{145,1},{2... | collective-permute-start | bytes 786440 | tf_op jit(solution)/shard_map/ppermute | solution.py:126
  22.3 9.5 %collective-permute-start.1 = (bf16[512,256]{1,0:T(8,128)(2,1)S(1)}, bf16[512,256]{1,0:T(8,128)(2,1)S(1)}, u32[]{:S(2)}, u32[]{:S(2)}) collective-permute-start(bf16[512,256]{1,0:T(8,128)(2,1)S(1)} %all_gather.3), channel_id=1, source_target_pairs={{0,96},{48,144},{96,0},{144,48},{1,97},{49,145},{97,1},{145,49},{2... | collective-permute-start | bytes 786440 | tf_op jit(solution)/shard_map/ppermute | solution.py:126
  31.8 1.9 collective-permute-start.2
  33.8 0.0 collective-permute-done
  33.8 2.3 %collective-permute-done.1 = bf16[512,256]{1,0:T(8,128)(2,1)S(1)} collective-permute-done((bf16[512,256]{1,0:T(8,128)(2,1)S(1)}, bf16[512,256]{1,0:T(8,128)(2,1)S(1)}, u32[]{:S(2)}, u32[]{:S(2)}) %collective-permute-start.1) | collective-permute-done | bytes 262176 | tf_op jit(solution)/shard_map/ppermute | solution.py:126
  36.2 3.9 %collective-permute-done.2 = bf16[512,256]{1,0:T(8,128)(2,1)S(1)} collective-permute-done((bf16[512,256]{1,0:T(8,128)(2,1)S(1)}, bf16[512,256]{1,0:T(8,128)(2,1)S(1)}, u32[]{:S(2)}, u32[]{:S(2)}) %collective-permute-start.2) | collective-permute-done | bytes 262176 | tf_op jit(solution)/shard_map/ppermute | solution.py:126
  40.1 1.9 collective-permute-start.3
  42.7 0.0 copy-done.6
  42.8 1.9 collective-permute-done.3.far_ref
  44.7 0.0 copy-done.3
  44.7 0.0 copy-start.1
  44.7 2.2 %copy-done.1 = bf16[1,1,128,128,128]{4,3,2,1,0:T(8,128)(2,1)S(1)} copy-done((bf16[1,1,128,128,128]{4,3,2,1,0:T(8,128)(2,1)S(1)}, bf16[1,1,128,128,128]{4,3,2,1,0:T(8,128)(2,1)}, u32[]{:S(2)}) %copy-start.1) | copy-done | bytes 4194328
  46.9 9.3 %shard_map.104 = (bf16[8,3,80,256]{3,2,1,0:T(8,128)(2,1)}, bf16[8,48,256]{2,1,0:T(8,128)(2,1)S(1)}, bf16[8,48,256]{2,1,0:T(8,128)(2,1)S(1)}, bf16[8,48,256]{2,1,0:T(8,128)(2,1)S(1)}) custom-call(s32[1]{0:T(128)} %bitcast.51.count_ref, s32[128]{0:T(128)S(1)} %fusion.7.pick_ref, s32[128]{0:T(128)S(1)} %bitcast.55, s32[1]{0:T(128)} %bitcast.3.zh_ref, ...), custom_call_target="tpu_custom_call" | custom-call | tf_op jit(solution)/shard_map/pallas_call | solution.py:72
  56.2 0.0 copy-start.4
  56.2 0.0 copy-start.5
  56.2 3.7 %all-to-all-start = ((bf16[8,3,80,256]{3,2,1,0:T(8,128)(2,1)}), bf16[8,3,80,256]{3,2,1,0:T(8,128)(2,1)S(1)}, u32[]{:S(2)}, u32[]{:S(2)}) async-start(bf16[8,3,80,256]{3,2,1,0:T(8,128)(2,1)} %get-tuple-element.8), calls=%async_computation | async-start | bytes 1966080 | tf_op jit(solution)/shard_map/all_to_all | solution.py:87
  59.9 10.7 %collective-permute-start.6 = (bf16[8,48,256]{2,1,0:T(8,128)(2,1)S(1)}, bf16[8,48,256]{2,1,0:T(8,128)(2,1)S(1)}, u32[]{:S(2)}, u32[]{:S(2)}) collective-permute-start(bf16[8,48,256]{2,1,0:T(8,128)(2,1)S(1)} %get-tuple-element.10), channel_id=1, source_target_pairs={{0,1},{1,2},{2,0},{3,4},{4,5},{5,3},{6,7},{7,8},{8,6},{9,10},{10,1... | collective-permute-start | bytes 589832 | tf_op jit(solution)/shard_map/ppermute | solution.py:95
  70.6 1.9 collective-permute-start.7
  72.6 15.1 %collective-permute-done.6 = bf16[8,48,256]{2,1,0:T(8,128)(2,1)S(1)} collective-permute-done((bf16[8,48,256]{2,1,0:T(8,128)(2,1)S(1)}, bf16[8,48,256]{2,1,0:T(8,128)(2,1)S(1)}, u32[]{:S(2)}, u32[]{:S(2)}) %collective-permute-start.6) | collective-permute-done | bytes 196640 | tf_op jit(solution)/shard_map/ppermute | solution.py:95
  87.6 4.6 %collective-permute-done.7 = bf16[8,48,256]{2,1,0:T(8,128)(2,1)S(1)} collective-permute-done((bf16[8,48,256]{2,1,0:T(8,128)(2,1)S(1)}, bf16[8,48,256]{2,1,0:T(8,128)(2,1)S(1)}, u32[]{:S(2)}, u32[]{:S(2)}) %collective-permute-start.7) | collective-permute-done | bytes 196640 | tf_op jit(solution)/shard_map/ppermute | solution.py:95
  92.2 0.8 add_convert_fusion.1
  93.0 0.0 all-to-all-done
  93.0 7.0 %all-to-all-start.1 = ((bf16[8,48,256]{2,1,0:T(8,128)(2,1)}), bf16[8,48,256]{2,1,0:T(8,128)(2,1)S(1)}, u32[]{:S(2)}, u32[]{:S(2)}) async-start(bf16[8,48,256]{2,1,0:T(8,128)(2,1)} %add_convert_fusion.1), calls=%async_computation.1 | async-start | bytes 393216 | tf_op jit(solution)/shard_map/all_to_all | solution.py:87
  100.0 0.1 reduce_sum.42
  100.1 4.2 %collective-permute-start.4 = (bf16[80,256]{1,0:T(8,128)(2,1)S(1)}, bf16[80,256]{1,0:T(8,128)(2,1)S(1)}, u32[]{:S(2)}, u32[]{:S(2)}) collective-permute-start(bf16[80,256]{1,0:T(8,128)(2,1)S(1)} %get-tuple-element.20), channel_id=1, source_target_pairs={{0,1},{1,2},{2,0},{3,4},{4,5},{5,3},{6,7},{7,8},{8,6},{9,10},{10,1... | collective-permute-start | bytes 122888 | tf_op jit(solution)/shard_map/ppermute | solution.py:95
  104.3 5.6 %collective-permute-start.5 = (bf16[80,256]{1,0:T(8,128)(2,1)S(1)}, bf16[80,256]{1,0:T(8,128)(2,1)S(1)}, u32[]{:S(2)}, u32[]{:S(2)}) collective-permute-start(bf16[80,256]{1,0:T(8,128)(2,1)S(1)} %get-tuple-element.21), channel_id=1, source_target_pairs={{0,2},{1,0},{2,1},{3,5},{4,3},{5,4},{6,8},{7,6},{8,7},{9,11},{10,9... | collective-permute-start | bytes 122888 | tf_op jit(solution)/shard_map/ppermute | solution.py:95
  109.9 0.2 all-to-all-done.1
  110.1 0.0 collective-permute-done.4
  110.1 4.0 %collective-permute-done.5 = bf16[80,256]{1,0:T(8,128)(2,1)S(1)} collective-permute-done((bf16[80,256]{1,0:T(8,128)(2,1)S(1)}, bf16[80,256]{1,0:T(8,128)(2,1)S(1)}, u32[]{:S(2)}, u32[]{:S(2)}) %collective-permute-start.5) | collective-permute-done | bytes 40992 | tf_op jit(solution)/shard_map/ppermute | solution.py:95
  114.2 0.0 copy-done.4
  114.2 0.0 copy-done.5
  114.2 0.8 multiply_convert_fusion.1
  115.0 0.7 broadcast_in_dim.8
  115.6 7.3 %all-to-all-start.3 = ((bf16[8,48,256]{2,1,0:T(8,128)(2,1)}), bf16[8,48,256]{2,1,0:T(8,128)(2,1)S(1)}, u32[]{:S(2)}, u32[]{:S(2)}) async-start(bf16[8,48,256]{2,1,0:T(8,128)(2,1)} %broadcast_in_dim.8), calls=%async_computation.3 | async-start | bytes 393216 | tf_op jit(solution)/shard_map/all_to_all | solution.py:87
  122.9 4.4 %collective-permute-start.8 = (bf16[80,256]{1,0:T(8,128)(2,1)S(1)}, bf16[80,256]{1,0:T(8,128)(2,1)S(1)}, u32[]{:S(2)}, u32[]{:S(2)}) collective-permute-start(bf16[80,256]{1,0:T(8,128)(2,1)S(1)} %get-tuple-element.23), channel_id=1, source_target_pairs={{0,1},{1,2},{2,0},{3,4},{4,5},{5,3},{6,7},{7,8},{8,6},{9,10},{10,1... | collective-permute-start | bytes 122888 | tf_op jit(solution)/shard_map/ppermute | solution.py:100
  127.3 5.4 %collective-permute-start.9 = (bf16[80,256]{1,0:T(8,128)(2,1)S(1)}, bf16[80,256]{1,0:T(8,128)(2,1)S(1)}, u32[]{:S(2)}, u32[]{:S(2)}) collective-permute-start(bf16[80,256]{1,0:T(8,128)(2,1)S(1)} %get-tuple-element.23), channel_id=1, source_target_pairs={{0,2},{1,0},{2,1},{3,5},{4,3},{5,4},{6,8},{7,6},{8,7},{9,11},{10,9... | collective-permute-start | bytes 122888 | tf_op jit(solution)/shard_map/ppermute | solution.py:100
  132.7 0.0 collective-permute-done.8
  132.7 4.4 %collective-permute-done.9 = bf16[80,256]{1,0:T(8,128)(2,1)S(1)} collective-permute-done((bf16[80,256]{1,0:T(8,128)(2,1)S(1)}, bf16[80,256]{1,0:T(8,128)(2,1)S(1)}, u32[]{:S(2)}, u32[]{:S(2)}) %collective-permute-start.9) | collective-permute-done | bytes 40992 | tf_op jit(solution)/shard_map/ppermute | solution.py:100
  137.1 0.0 all-to-all-done.3.rest_0_
  137.1 1.0 broadcast_in_dim.7
  138.2 7.2 %all-to-all-start.2 = ((bf16[8,3,80,256]{3,2,1,0:T(8,128)(2,1)}), bf16[8,3,80,256]{3,2,1,0:T(8,128)(2,1)S(1)}, u32[]{:S(2)}, u32[]{:S(2)}) async-start(bf16[8,3,80,256]{3,2,1,0:T(8,128)(2,1)} %broadcast_in_dim.7), calls=%async_computation.2 | async-start | bytes 1966080 | tf_op jit(solution)/shard_map/all_to_all | solution.py:87
  145.4 5.4 %collective-permute-start.11 = (bf16[8,48,256]{2,1,0:T(8,128)(2,1)S(1)}, bf16[8,48,256]{2,1,0:T(8,128)(2,1)S(1)}, u32[]{:S(2)}, u32[]{:S(2)}) collective-permute-start(bf16[8,48,256]{2,1,0:T(8,128)(2,1)S(1)} %all-to-all-done.3.rest_0_), channel_id=1, source_target_pairs={{0,2},{1,0},{2,1},{3,5},{4,3},{5,4},{6,8},{7,6},{8,7},{9,11},{10,9... | collective-permute-start | bytes 589832 | tf_op jit(solution)/shard_map/ppermute | solution.py:100
  150.8 4.4 %collective-permute-start.10 = (bf16[8,48,256]{2,1,0:T(8,128)(2,1)S(1)}, bf16[8,48,256]{2,1,0:T(8,128)(2,1)S(1)}, u32[]{:S(2)}, u32[]{:S(2)}) collective-permute-start(bf16[8,48,256]{2,1,0:T(8,128)(2,1)S(1)} %all-to-all-done.3.rest_0_), channel_id=1, source_target_pairs={{0,1},{1,2},{2,0},{3,4},{4,5},{5,3},{6,7},{7,8},{8,6},{9,10},{10,1... | collective-permute-start | bytes 589832 | tf_op jit(solution)/shard_map/ppermute | solution.py:100
  155.1 2.3 %collective-permute-done.11.rest_2_ = bf16[8,48,256]{2,1,0:T(8,128)(2,1)S(1)} collective-permute-done((bf16[8,48,256]{2,1,0:T(8,128)(2,1)S(1)}, bf16[8,48,256]{2,1,0:T(8,128)(2,1)S(1)}, u32[]{:S(2)}, u32[]{:S(2)}) %collective-permute-start.11) | collective-permute-done | bytes 196640 | tf_op jit(solution)/shard_map/ppermute | solution.py:100
  157.4 8.8 %collective-permute-done.10.rest_1_ = bf16[8,48,256]{2,1,0:T(8,128)(2,1)S(1)} collective-permute-done((bf16[8,48,256]{2,1,0:T(8,128)(2,1)S(1)}, bf16[8,48,256]{2,1,0:T(8,128)(2,1)S(1)}, u32[]{:S(2)}, u32[]{:S(2)}) %collective-permute-start.10) | collective-permute-done | bytes 196640 | tf_op jit(solution)/shard_map/ppermute | solution.py:100
  166.1 3.4 %all-to-all-done.2.part_a = bf16[8,3,80,256]{3,2,1,0:T(8,128)(2,1)S(1)} async-done(((bf16[8,3,80,256]{3,2,1,0:T(8,128)(2,1)}), bf16[8,3,80,256]{3,2,1,0:T(8,128)(2,1)S(1)}, u32[]{:S(2)}, u32[]{:S(2)}) %all-to-all-start.2) | async-done | bytes 983072 | tf_op jit(solution)/shard_map/all_to_all | solution.py:87
  169.5 0.0 copy-start.2
  169.5 2.2 %copy-done.2 = bf16[1,1,128,128,128]{4,3,2,1,0:T(8,128)(2,1)S(1)} copy-done((bf16[1,1,128,128,128]{4,3,2,1,0:T(8,128)(2,1)S(1)}, bf16[1,1,128,128,128]{4,3,2,1,0:T(8,128)(2,1)}, u32[]{:S(2)}) %copy-start.2) | copy-done | bytes 4194328
  171.7 9.7 %shard_map.105 = (bf16[2048,256]{1,0:T(8,128)(2,1)S(1)}, bf16[2048,256]{1,0:T(8,128)(2,1)S(1)}) custom-call(s32[1]{0:T(128)} %bitcast.52.count_ref, s32[128]{0:T(128)S(1)} %bitcast.56, s32[128]{0:T(128)S(1)} %get-tuple-element.14.place_ref, s32[1]{0:T(128)} %bitcast.3.zh_ref, bf16[128,128,128]{2,1,0:T(8,128)(2,1)S(1)} %bitcast.54, ...), custom_call_target="tpu_custom_call" | custom-call | tf_op jit(solution)/shard_map/pallas_call | solution.py:72
  181.5 1.9 collective-permute-start.12
  183.4 2.6 %collective-permute-done.12 = bf16[2048,256]{1,0:T(8,128)(2,1)S(1)} collective-permute-done((bf16[2048,256]{1,0:T(8,128)(2,1)S(1)}, bf16[2048,256]{1,0:T(8,128)(2,1)S(1)}, u32[]{:S(2)}, u32[]{:S(2)}) %collective-permute-start.12) | collective-permute-done | bytes 1048608 | tf_op jit(solution)/shard_map/ppermute | solution.py:158
  186.0 0.3 add_convert_fusion
  186.3 17.0 %all_to_all.30 = bf16[4,512,256]{2,1,0:T(8,128)(2,1)S(1)} all-to-all(bf16[4,512,256]{2,1,0:T(8,128)(2,1)S(1)} %bitcast.57), channel_id=1, replica_groups=mesh['zl'=4,'x'=4,'c'=2,'y'=8,'zh'=3] {'x'}, dimensions={0} | all-to-all | bytes 2097152 | tf_op jit(solution)/shard_map/all_to_all | solution.py:87
  203.3 0.3 reduce_sum.44
  203.6 12.6 %all_to_all.31 = bf16[4,128,256]{2,1,0:T(8,128)(2,1)S(1)} all-to-all(bf16[4,128,256]{2,1,0:T(8,128)(2,1)S(1)} %bitcast.58), channel_id=1, replica_groups=mesh['zl'=4,'x'=4,'c'=2,'y'=8,'zh'=3] {'zl'}, dimensions={0} | all-to-all | bytes 524288 | tf_op jit(solution)/shard_map/all_to_all | solution.py:87
  216.3 0.8 convolution_convert_fusion
  (13 shorter events, 0.2 us)
Async XLA Ops:
  0.6 0.9 copy-start
  0.6 42.1 %copy-start.6 = (s32[1,1,128]{2,1,0:T(1,128)S(1)}, s32[1,1,128]{2,1,0:T(1,128)}, u32[]{:S(2)}) copy-start(s32[1,1,128]{2,1,0:T(1,128)} %param.15) | copy-start | bytes 1540
  0.7 44.0 %copy-start.3 = (s32[1,1,128]{2,1,0:T(1,128)S(1)}, s32[1,1,128]{2,1,0:T(1,128)}, u32[]{:S(2)}) copy-start(s32[1,1,128]{2,1,0:T(1,128)} %param.14) | copy-start | bytes 1540
  18.9 14.9 %collective-permute-start = (bf16[512,256]{1,0:T(8,128)(2,1)S(1)}, bf16[512,256]{1,0:T(8,128)(2,1)S(1)}, u32[]{:S(2)}, u32[]{:S(2)}) collective-permute-start(bf16[512,256]{1,0:T(8,128)(2,1)S(1)} %all_gather.3), channel_id=1, source_target_pairs={{0,48},{48,96},{96,144},{144,0},{1,49},{49,97},{97,145},{145,1},{2... | collective-permute-start | bytes 786440 | tf_op jit(solution)/shard_map/ppermute | solution.py:126
  22.3 13.9 %collective-permute-start.1 = (bf16[512,256]{1,0:T(8,128)(2,1)S(1)}, bf16[512,256]{1,0:T(8,128)(2,1)S(1)}, u32[]{:S(2)}, u32[]{:S(2)}) collective-permute-start(bf16[512,256]{1,0:T(8,128)(2,1)S(1)} %all_gather.3), channel_id=1, source_target_pairs={{0,96},{48,144},{96,0},{144,48},{1,97},{49,145},{97,1},{145,49},{2... | collective-permute-start | bytes 786440 | tf_op jit(solution)/shard_map/ppermute | solution.py:126
  31.8 8.3 %collective-permute-start.2 = (bf16[512,256]{1,0:T(8,128)(2,1)S(1)}, bf16[512,256]{1,0:T(8,128)(2,1)S(1)}, u32[]{:S(2)}, u32[]{:S(2)}) collective-permute-start(bf16[512,256]{1,0:T(8,128)(2,1)S(1)} %all_gather.3), channel_id=1, source_target_pairs={{0,144},{48,0},{96,48},{144,96},{1,145},{49,1},{97,49},{145,97},{2... | collective-permute-start | bytes 786440 | tf_op jit(solution)/shard_map/ppermute | solution.py:126
  40.1 4.6 %collective-permute-start.3 = (bf16[2048,256]{1,0:T(8,128)(2,1)S(1)}, bf16[2048,256]{1,0:T(8,128)(2,1)S(1)}, u32[]{:S(2)}, u32[]{:S(2)}) collective-permute-start(bf16[2048,256]{1,0:T(8,128)(2,1)S(1)} %constant_dynamic-update-slice_fusion.near_ref), channel_id=1, source_target_pairs={{0,24},{24,0},{1,25},{25,1},{2,26},{26,2},{3,27},{27,3},{4,28},{28... | collective-permute-start | bytes 3145736 | tf_op jit(solution)/shard_map/ppermute | solution.py:128
  44.7 2.2 %copy-start.1 = (bf16[1,1,128,128,128]{4,3,2,1,0:T(8,128)(2,1)S(1)}, bf16[1,1,128,128,128]{4,3,2,1,0:T(8,128)(2,1)}, u32[]{:S(2)}) copy-start(bf16[1,1,128,128,128]{4,3,2,1,0:T(8,128)(2,1)} %param.13) | copy-start | bytes 12582916
  56.2 57.9 %copy-start.4 = (bf16[128,256]{1,0:T(8,128)(2,1)S(1)}, bf16[128,256]{1,0:T(8,128)(2,1)}, u32[]{:S(2)}) copy-start(bf16[128,256]{1,0:T(8,128)(2,1)} %param.17) | copy-start | bytes 196612
  56.2 57.9 %copy-start.5 = (f32[256]{0:T(256)S(1)}, f32[256]{0:T(256)}, u32[]{:S(2)}) copy-start(f32[256]{0:T(256)} %param.12) | copy-start | bytes 3076
  56.2 36.8 %all-to-all-start = ((bf16[8,3,80,256]{3,2,1,0:T(8,128)(2,1)}), bf16[8,3,80,256]{3,2,1,0:T(8,128)(2,1)S(1)}, u32[]{:S(2)}, u32[]{:S(2)}) async-start(bf16[8,3,80,256]{3,2,1,0:T(8,128)(2,1)} %get-tuple-element.8), calls=%async_computation | async-start | bytes 1966080 | tf_op jit(solution)/shard_map/all_to_all | solution.py:87
  59.9 27.7 %collective-permute-start.6 = (bf16[8,48,256]{2,1,0:T(8,128)(2,1)S(1)}, bf16[8,48,256]{2,1,0:T(8,128)(2,1)S(1)}, u32[]{:S(2)}, u32[]{:S(2)}) collective-permute-start(bf16[8,48,256]{2,1,0:T(8,128)(2,1)S(1)} %get-tuple-element.10), channel_id=1, source_target_pairs={{0,1},{1,2},{2,0},{3,4},{4,5},{5,3},{6,7},{7,8},{8,6},{9,10},{10,1... | collective-permute-start | bytes 589832 | tf_op jit(solution)/shard_map/ppermute | solution.py:95
  70.6 21.6 %collective-permute-start.7 = (bf16[8,48,256]{2,1,0:T(8,128)(2,1)S(1)}, bf16[8,48,256]{2,1,0:T(8,128)(2,1)S(1)}, u32[]{:S(2)}, u32[]{:S(2)}) collective-permute-start(bf16[8,48,256]{2,1,0:T(8,128)(2,1)S(1)} %get-tuple-element.11), channel_id=1, source_target_pairs={{0,2},{1,0},{2,1},{3,5},{4,3},{5,4},{6,8},{7,6},{8,7},{9,11},{10,9... | collective-permute-start | bytes 589832 | tf_op jit(solution)/shard_map/ppermute | solution.py:95
  93.0 17.1 %all-to-all-start.1 = ((bf16[8,48,256]{2,1,0:T(8,128)(2,1)}), bf16[8,48,256]{2,1,0:T(8,128)(2,1)S(1)}, u32[]{:S(2)}, u32[]{:S(2)}) async-start(bf16[8,48,256]{2,1,0:T(8,128)(2,1)} %add_convert_fusion.1), calls=%async_computation.1 | async-start | bytes 393216 | tf_op jit(solution)/shard_map/all_to_all | solution.py:87
  100.1 10.0 %collective-permute-start.4 = (bf16[80,256]{1,0:T(8,128)(2,1)S(1)}, bf16[80,256]{1,0:T(8,128)(2,1)S(1)}, u32[]{:S(2)}, u32[]{:S(2)}) collective-permute-start(bf16[80,256]{1,0:T(8,128)(2,1)S(1)} %get-tuple-element.20), channel_id=1, source_target_pairs={{0,1},{1,2},{2,0},{3,4},{4,5},{5,3},{6,7},{7,8},{8,6},{9,10},{10,1... | collective-permute-start | bytes 122888 | tf_op jit(solution)/shard_map/ppermute | solution.py:95
  104.3 9.8 %collective-permute-start.5 = (bf16[80,256]{1,0:T(8,128)(2,1)S(1)}, bf16[80,256]{1,0:T(8,128)(2,1)S(1)}, u32[]{:S(2)}, u32[]{:S(2)}) collective-permute-start(bf16[80,256]{1,0:T(8,128)(2,1)S(1)} %get-tuple-element.21), channel_id=1, source_target_pairs={{0,2},{1,0},{2,1},{3,5},{4,3},{5,4},{6,8},{7,6},{8,7},{9,11},{10,9... | collective-permute-start | bytes 122888 | tf_op jit(solution)/shard_map/ppermute | solution.py:95
  115.6 21.5 %all-to-all-start.3 = ((bf16[8,48,256]{2,1,0:T(8,128)(2,1)}), bf16[8,48,256]{2,1,0:T(8,128)(2,1)S(1)}, u32[]{:S(2)}, u32[]{:S(2)}) async-start(bf16[8,48,256]{2,1,0:T(8,128)(2,1)} %broadcast_in_dim.8), calls=%async_computation.3 | async-start | bytes 393216 | tf_op jit(solution)/shard_map/all_to_all | solution.py:87
  122.9 9.8 %collective-permute-start.8 = (bf16[80,256]{1,0:T(8,128)(2,1)S(1)}, bf16[80,256]{1,0:T(8,128)(2,1)S(1)}, u32[]{:S(2)}, u32[]{:S(2)}) collective-permute-start(bf16[80,256]{1,0:T(8,128)(2,1)S(1)} %get-tuple-element.23), channel_id=1, source_target_pairs={{0,1},{1,2},{2,0},{3,4},{4,5},{5,3},{6,7},{7,8},{8,6},{9,10},{10,1... | collective-permute-start | bytes 122888 | tf_op jit(solution)/shard_map/ppermute | solution.py:100
  127.3 9.8 %collective-permute-start.9 = (bf16[80,256]{1,0:T(8,128)(2,1)S(1)}, bf16[80,256]{1,0:T(8,128)(2,1)S(1)}, u32[]{:S(2)}, u32[]{:S(2)}) collective-permute-start(bf16[80,256]{1,0:T(8,128)(2,1)S(1)} %get-tuple-element.23), channel_id=1, source_target_pairs={{0,2},{1,0},{2,1},{3,5},{4,3},{5,4},{6,8},{7,6},{8,7},{9,11},{10,9... | collective-permute-start | bytes 122888 | tf_op jit(solution)/shard_map/ppermute | solution.py:100
  138.2 31.4 %all-to-all-start.2 = ((bf16[8,3,80,256]{3,2,1,0:T(8,128)(2,1)}), bf16[8,3,80,256]{3,2,1,0:T(8,128)(2,1)S(1)}, u32[]{:S(2)}, u32[]{:S(2)}) async-start(bf16[8,3,80,256]{3,2,1,0:T(8,128)(2,1)} %broadcast_in_dim.7), calls=%async_computation.2 | async-start | bytes 1966080 | tf_op jit(solution)/shard_map/all_to_all | solution.py:87
  145.4 12.0 %collective-permute-start.11 = (bf16[8,48,256]{2,1,0:T(8,128)(2,1)S(1)}, bf16[8,48,256]{2,1,0:T(8,128)(2,1)S(1)}, u32[]{:S(2)}, u32[]{:S(2)}) collective-permute-start(bf16[8,48,256]{2,1,0:T(8,128)(2,1)S(1)} %all-to-all-done.3.rest_0_), channel_id=1, source_target_pairs={{0,2},{1,0},{2,1},{3,5},{4,3},{5,4},{6,8},{7,6},{8,7},{9,11},{10,9... | collective-permute-start | bytes 589832 | tf_op jit(solution)/shard_map/ppermute | solution.py:100
  150.8 15.4 %collective-permute-start.10 = (bf16[8,48,256]{2,1,0:T(8,128)(2,1)S(1)}, bf16[8,48,256]{2,1,0:T(8,128)(2,1)S(1)}, u32[]{:S(2)}, u32[]{:S(2)}) collective-permute-start(bf16[8,48,256]{2,1,0:T(8,128)(2,1)S(1)} %all-to-all-done.3.rest_0_), channel_id=1, source_target_pairs={{0,1},{1,2},{2,0},{3,4},{4,5},{5,3},{6,7},{7,8},{8,6},{9,10},{10,1... | collective-permute-start | bytes 589832 | tf_op jit(solution)/shard_map/ppermute | solution.py:100
  169.5 2.2 %copy-start.2 = (bf16[1,1,128,128,128]{4,3,2,1,0:T(8,128)(2,1)S(1)}, bf16[1,1,128,128,128]{4,3,2,1,0:T(8,128)(2,1)}, u32[]{:S(2)}) copy-start(bf16[1,1,128,128,128]{4,3,2,1,0:T(8,128)(2,1)} %param.13) | copy-start | bytes 12582916
  181.5 4.6 %collective-permute-start.12 = (bf16[2048,256]{1,0:T(8,128)(2,1)S(1)}, bf16[2048,256]{1,0:T(8,128)(2,1)S(1)}, u32[]{:S(2)}, u32[]{:S(2)}) collective-permute-start(bf16[2048,256]{1,0:T(8,128)(2,1)S(1)} %get-tuple-element.13), channel_id=1, source_target_pairs={{0,24},{24,0},{1,25},{25,1},{2,26},{26,2},{3,27},{27,3},{4,28},{28... | collective-permute-start | bytes 3145736 | tf_op jit(solution)/shard_map/ppermute | solution.py:158

commit v3 on v2

v3 whole, which is shorter than its diff:
```python
import functools

import jax
import jax.numpy as jnp
from jax import lax
from jax.experimental import pallas as pl
from jax.experimental.pallas import tpu as pltpu
from jax.sharding import Mesh
from jax.sharding import PartitionSpec as P

ZL, X, C, Y, ZH = 4, 4, 2, 8, 3
BF, F32 = jnp.bfloat16, jnp.float32
NODE_AXES = ("zl", "x", "c", "y", "zh")
UNROLL = 4
PARTS = 4


def fetch(tiles_ref, tiles, sems):
    size = tiles.shape[0] // PARTS
    copies = []
    for part in range(PARTS):
        slots = pl.ds(part * size, size)
        copies.append(pltpu.make_async_copy(tiles_ref.at[slots], tiles.at[slots], sems.at[part]))
        copies[-1].start()
    return copies


def accumulate(count_ref, pick_ref, place_ref, tiles, copies, src, acc, transposed):
    edge = tiles.shape[-1]
    size = tiles.shape[0] // PARTS
    dims = (((0,), (0,)), ((), ())) if transposed else (((1,), (0,)), ((), ()))
    acc[...] = jnp.zeros_like(acc)

    for part in range(PARTS):
        copies[part].wait()

        def step(s, carry, first=part * size):
            products = []
            for u in range(UNROLL):
                t = first + s * UNROLL + u
                block = src[pl.ds(pl.multiple_of(pick_ref[t] * edge, edge), edge), :]
                products.append(lax.dot_general(tiles[t], block, dims, preferred_element_type=F32))
            for u in range(UNROLL):
                q = place_ref[first + s * UNROLL + u]
                acc[pl.ds(pl.multiple_of(q * edge, edge), edge), :] += products[u]
            return carry

        live = jnp.clip(count_ref[0] - part * size, 0, size)
        lax.fori_loop(0, live // UNROLL, step, 0)


def forward_kernel(
    count_ref, pick_ref, place_ref, at_ref, tiles_ref, near_ref, far_ref, out, src, acc, tiles, sems
):
    copies = fetch(tiles_ref, tiles, sems)
    half = near_ref.shape[0]
    edge = tiles.shape[-1]
    src[:half] = near_ref[...]
    src[half:] = far_ref[...]
    accumulate(count_ref, pick_ref, place_ref, tiles, copies, src, acc, False)
    for y in range(Y):
        for k in range(ZH):
            base = pl.multiple_of((y * ZH + (at_ref[0] + k) % ZH) * edge, edge)
            out[y, k] = acc[pl.ds(base, edge), :].astype(BF)


def backward_kernel(count_ref, pick_ref, place_ref, at_ref, tiles_ref, *rest):
    same, (next_a, next_b, near_ref, far_ref, src, acc, tiles, sems) = rest[: Y // 2], rest[Y // 2 :]
    copies = fetch(tiles_ref, tiles, sems)
    edge = tiles.shape[-1]
    cut = edge // 2
    for j in range(Y // 2):
        for k in range(ZH):
            z = (at_ref[0] + ZH - k) % ZH
            base, base_a, base_b = [
                pl.multiple_of(((at_ref[1 + i] + Y - 2 * j) % Y * ZH + z) * edge, edge) for i in range(3)
            ]
            src[pl.ds(base, edge), :] = same[j][k]
            src[pl.ds(base_a, cut), :] = next_a[j, k]
            src[pl.ds(base_b + cut, cut), :] = next_b[j, k]
    accumulate(count_ref, pick_ref, place_ref, tiles, copies, src, acc, True)
    half = near_ref.shape[0]
    near_ref[...] = acc[:half, :].astype(BF)
    far_ref[...] = acc[half:, :].astype(BF)


SMEM = pl.BlockSpec(memory_space=pltpu.SMEM)
VMEM = pl.BlockSpec(memory_space=pltpu.VMEM)
HBM = pl.BlockSpec(memory_space=pltpu.HBM)


def call(kernel, outs, src_rows, acc_rows, feat, *args):
    tiles = args[4]
    return pl.pallas_call(
        kernel,
        out_shape=tuple(jax.ShapeDtypeStruct(s, BF) for s in outs),
        in_specs=[SMEM] * 4 + [HBM] + [VMEM] * (len(args) - 5),
        out_specs=tuple(VMEM for _ in outs),
        scratch_shapes=[
            pltpu.VMEM((src_rows, feat), BF),
            pltpu.VMEM((acc_rows, feat), F32),
            pltpu.VMEM(tiles.shape, BF),
            pltpu.SemaphoreType.DMA((PARTS,)),
        ],
        compiler_params=pltpu.CompilerParams(vmem_limit_bytes=40 * 1024 * 1024),
    )(*args)


def shift(n, k):
    return [(i, (i + k) % n) for i in range(n)]


def swap(value, axis):
    return lax.all_to_all(value, axis, 0, 0, tiled=True)


def spread(value, axis, size):
    return swap(jnp.broadcast_to(value[None], (size,) + value.shape), axis)


def collect(pieces):
    moved = [pieces[0]] + [lax.ppermute(pieces[k], "zh", shift(ZH, k)) for k in range(1, ZH)]
    return sum(piece.astype(F32) for piece in moved)


def share(value, axis, size, stride):
    return [value] + [lax.ppermute(value, axis, shift(size, k)) for k in range(stride, size, stride)]


def total(value):
    return value.astype(F32).sum(0)


def body(
    features, degrees, weight, bias_term, tile_weights, tile_rows, tile_columns, tile_count, cotangent
):
    tiles = tile_weights[0, 0]
    rows, columns = tile_rows[0, 0], tile_columns[0, 0]
    count = tile_count[0]
    n, feat = features.shape
    my_y = lax.axis_index("y").astype(jnp.int32)
    my_zh = lax.axis_index("zh").astype(jnp.int32)
    odd = my_y % 2
    at = jnp.stack([my_zh, my_y, my_y + 1 - 2 * odd, (my_y + Y - 1 + 2 * odd) % Y])
    block_zl, block_x, block_c = columns // (X * C), columns // C % X, columns % C
    other = (block_c != lax.axis_index("c")).astype(jnp.int32)
    column_at = (other * X + block_x) * ZL + block_zl
    inv_root = lax.rsqrt(degrees.astype(F32))[:, None]
    hidden = jnp.dot(features, weight, preferred_element_type=F32)
    scaled = (hidden * inv_root).astype(BF)

    near = spread(spread(scaled, "zl", ZL), "x", X).reshape(X * ZL * n, feat)
    far = lax.ppermute(near, "c", shift(C, 1))
    (part,) = call(
        forward_kernel, [(Y, ZH, n, feat)], C * X * ZL * n, Y * ZH * n, feat,
        count, column_at, rows, at, tiles, near, far,
    )
    along_y = total(swap(part, "y")).astype(BF)
    own_rows = collect([along_y[k] for k in range(ZH)])

    preact = inv_root * (own_rows + scaled.astype(F32)) + bias_term[None, :]
    sigmoid_value = jax.nn.sigmoid(preact)
    activations = (preact * sigmoid_value).astype(BF)
    slope_value = sigmoid_value * (1.0 + preact * (1.0 - sigmoid_value))
    upstream = (cotangent.astype(F32) * slope_value * inv_root).astype(BF)

    mine = jnp.stack(share(upstream, "zh", ZH, 1))
    same = share(mine, "y", Y, 2)
    gathered = jnp.stack(same)
    next_a = lax.ppermute(gathered[:, :, : n // 2], "y", [(i, i ^ 1) for i in range(Y)])
    next_b = lax.ppermute(
        gathered[:, :, n // 2 :], "y", [(i, (i + 1 if i % 2 else i - 1) % Y) for i in range(Y)]
    )
    half = (X * ZL * n, feat)
    own_half, other_half = call(
        backward_kernel, [half, half], Y * ZH * n, C * X * ZL * n, feat,
        count, rows, column_at, at, tiles, *same, next_a, next_b,
    )
    other_half = lax.ppermute(other_half, "c", shift(C, 1))
    both = (own_half.astype(F32) + other_half.astype(F32)).astype(BF).reshape(X, ZL * n, feat)
    along_x = total(swap(both, "x")).astype(BF).reshape(ZL, n, feat)
    own_back = total(swap(along_x, "zl"))
    grad_hidden = (inv_root * (own_back + upstream.astype(F32))).astype(BF)
    feature_grad = jnp.einsum("nf,gf->ng", grad_hidden, weight, preferred_element_type=F32)
    return activations, feature_grad.astype(BF)


def solution(mesh):
    fine = Mesh(mesh.devices.reshape(ZL, X, C, Y, ZH), NODE_AXES)
    gr, gc = ("zl", "x", "c"), ("y", "zh")
    nodes = P(NODE_AXES, None)

    return jax.shard_map(
        body,
        mesh=fine,
        in_specs=(
            nodes, P(NODE_AXES), P(), P(), P(gr, gc, None, None, None), P(gr, gc, None), P(gr, gc, None),
            P(gr, gc), nodes,
        ),
        out_specs=(nodes, nodes),
        check_vma=False,
    )
```

time: 218 us -> 223 us (1.023)
  the two profiles are of different devices: /device:TPU:2 before, /device:TPU:8 now
where the time goes in v3:
time: 223 us; the launch traced here: 222 us
  blocking collectives  112 us (50%)
  waiting for transfers between devices  43.9 us (20%)
  starting transfers between devices  38.9 us (17%)
  Pallas kernels  18.8 us (8%)
  local copies, waits for them, and re-layouts  2.64 us (1%)
  other arithmetic  2.52 us (1%)
    all_to_all x5, blocking collectives, swap(): return lax.all_to_all(value, axis, 0, 0, tiled=True)  112 us
    ppermute x5, waiting for transfers between devices, share(): lax.ppermute(value, axis, shift(size, k))  19.7 us
    ppermute x5, starting transfers between devices, share(): lax.ppermute(value, axis, shift(size, k))  19.2 us
    pallas_call x2, Pallas kernels, call(): pl.pallas_call(kernel, out_shape=tuple((jax.ShapeDtypeStruct(s, BF) for s...  18.8 us
    ppermute x2, waiting for transfers between devices, collect(): lax.ppermute(pieces[k], 'zh', shift(ZH, k))  10.7 us
    ppermute x2, starting transfers between devices, collect(): lax.ppermute(pieces[k], 'zh', shift(ZH, k))  10.1 us
    ppermute x1, waiting for transfers between devices, body(): lax.ppermute(gathered[:, :, n // 2:], 'y', [(i, (i + 1 if i % 2 else i -...  7.08 us
  transfers between devices with their start and end apart: 11, of which 11 were waited for; matrix products, arithmetic and copies ran while one was open for 0% of the time, Pallas kernels for 0%

profile of v3, /device:TPU:8, one launch (start us, length us, event | category | flops | bytes accessed | tf_op | source)
XLA Modules:
  0.0 221.9 jit_solution(12840448379810488553)
XLA Ops:
  0.6 0.0 copy-start
  0.6 0.7 convert_rsqrt_fusion
  1.3 0.2 copy-done
  1.6 1.0 fusion
  2.6 0.0 copy-start.6
  2.6 0.0 copy-start.3
  2.6 15.9 %all_to_all.25 = bf16[4,128,256]{2,1,0:T(8,128)(2,1)S(1)} all-to-all(bf16[4,128,256]{2,1,0:T(8,128)(2,1)S(1)} %broadcast_in_dim.4), channel_id=1, replica_groups=mesh['zl'=4,'x'=4,'c'=2,'y'=8,'zh'=3] {'zl'}, dimensions={0} | all-to-all | bytes 524288 | tf_op jit(solution)/shard_map/all_to_all | solution.py:114
  18.5 0.1 broadcast_in_dim.5
  18.6 16.9 %all_to_all.26 = bf16[4,4,128,256]{3,2,1,0:T(8,128)(2,1)S(1)} all-to-all(bf16[4,4,128,256]{3,2,1,0:T(8,128)(2,1)S(1)} %broadcast_in_dim.5), channel_id=1, replica_groups=mesh['zl'=4,'x'=4,'c'=2,'y'=8,'zh'=3] {'x'}, dimensions={0} | all-to-all | bytes 2097152 | tf_op jit(solution)/shard_map/all_to_all | solution.py:114
  35.6 1.9 collective-permute-start
  38.2 0.1 pad_add_fusion.at_ref
  38.2 0.0 copy-done.6
  38.3 1.8 collective-permute-done.far_ref
  40.1 0.0 copy-done.3
  40.1 0.0 copy-start.1
  40.1 2.2 copy-done.1
  42.3 8.8 %shard_map.104 = bf16[8,3,128,256]{3,2,1,0:T(8,128)(2,1)S(1)} custom-call(s32[1]{0:T(128)} %bitcast.52.count_ref, s32[128]{0:T(128)S(1)} %multiply_add_fusion.pick_ref.place_ref, s32[128]{0:T(128)S(1)} %bitcast.61, s32[4]{0:T(128)S(1)} %pad_add_fusion.at_ref, bf16[128,128,128]{2,1,0:T(8,128)(2,1)S(1)} %bitcast.54, bf16[2048,256]{1,0:T(8,128)(2,1)S(1)} %bitcast.57, ...), custom_call_target="tpu_custom_call" | custom-call | tf_op jit(solution)/shard_map/pallas_call | solution.py:94
  51.1 0.0 copy-start.4
  51.1 0.0 copy-start.5
  51.1 44.0 %all_to_all.27 = bf16[8,3,128,256]{3,2,1,0:T(8,128)(2,1)S(1)} all-to-all(bf16[8,3,128,256]{3,2,1,0:T(8,128)(2,1)S(1)} %shard_map.104), channel_id=1, replica_groups=mesh['zl'=4,'x'=4,'c'=2,'y'=8,'zh'=3] {'y'}, dimensions={0} | all-to-all | bytes 3145728 | tf_op jit(solution)/shard_map/all_to_all | solution.py:114
  95.1 0.3 reduce_sum.33
  95.4 7.6 %collective-permute-start.1 = (bf16[128,256]{1,0:T(8,128)(2,1)S(1)}, bf16[128,256]{1,0:T(8,128)(2,1)S(1)}, u32[]{:S(2)}, u32[]{:S(2)}) collective-permute-start(bf16[128,256]{1,0:T(8,128)(2,1)S(1)} %get-tuple-element.12), channel_id=1, source_target_pairs={{0,1},{1,2},{2,0},{3,4},{4,5},{5,3},{6,7},{7,8},{8,6},{9,10},{10,1... | collective-permute-start | bytes 196616 | tf_op jit(solution)/shard_map/ppermute | solution.py:122
  103.1 0.0 copy-start.2
  103.1 2.5 %collective-permute-start.2 = (bf16[128,256]{1,0:T(8,128)(2,1)S(1)}, bf16[128,256]{1,0:T(8,128)(2,1)S(1)}, u32[]{:S(2)}, u32[]{:S(2)}) collective-permute-start(bf16[128,256]{1,0:T(8,128)(2,1)S(1)} %get-tuple-element.13), channel_id=1, source_target_pairs={{0,2},{1,0},{2,1},{3,5},{4,3},{5,4},{6,8},{7,6},{8,7},{9,11},{10,9... | collective-permute-start | bytes 196616 | tf_op jit(solution)/shard_map/ppermute | solution.py:122
  105.5 0.2 collective-permute-done.1
  105.7 10.5 %collective-permute-done.2 = bf16[128,256]{1,0:T(8,128)(2,1)S(1)} collective-permute-done((bf16[128,256]{1,0:T(8,128)(2,1)S(1)}, bf16[128,256]{1,0:T(8,128)(2,1)S(1)}, u32[]{:S(2)}, u32[]{:S(2)}) %collective-permute-start.2) | collective-permute-done | bytes 65568 | tf_op jit(solution)/shard_map/ppermute | solution.py:122
  116.2 0.0 copy-done.4
  116.2 0.0 copy-done.5
  116.2 0.8 multiply_convert_fusion.1
  117.0 1.9 collective-permute-start.4
  118.9 7.8 %collective-permute-start.3 = (bf16[128,256]{1,0:T(8,128)(2,1)S(1)}, bf16[128,256]{1,0:T(8,128)(2,1)S(1)}, u32[]{:S(2)}, u32[]{:S(2)}) collective-permute-start(bf16[128,256]{1,0:T(8,128)(2,1)S(1)} %get-tuple-element.8), channel_id=1, source_target_pairs={{0,1},{1,2},{2,0},{3,4},{4,5},{5,3},{6,7},{7,8},{8,6},{9,10},{10,1... | collective-permute-start | bytes 196616 | tf_op jit(solution)/shard_map/ppermute | solution.py:127
  126.7 0.6 collective-permute-done.4
  127.3 3.3 %collective-permute-done.3 = bf16[128,256]{1,0:T(8,128)(2,1)S(1)} collective-permute-done((bf16[128,256]{1,0:T(8,128)(2,1)S(1)}, bf16[128,256]{1,0:T(8,128)(2,1)S(1)}, u32[]{:S(2)}, u32[]{:S(2)}) %collective-permute-start.3) | collective-permute-done | bytes 65568 | tf_op jit(solution)/shard_map/ppermute | solution.py:127
  130.6 1.9 collective-permute-start.7
  132.5 5.6 %collective-permute-start.6 = (bf16[3,128,256]{2,1,0:T(8,128)(2,1)S(1)}, bf16[3,128,256]{2,1,0:T(8,128)(2,1)S(1)}, u32[]{:S(2)}, u32[]{:S(2)}) collective-permute-start(bf16[3,128,256]{2,1,0:T(8,128)(2,1)S(1)} %get-tuple-element.11.rest_0_), channel_id=1, source_target_pairs={{0,12},{3,15},{6,18},{9,21},{12,0},{15,3},{18,6},{21,9},{1,13},{4,... | collective-permute-start | bytes 589832 | tf_op jit(solution)/shard_map/ppermute | solution.py:127
  138.2 1.9 collective-permute-start.5
  140.1 3.4 %collective-permute-done.7.rest_3_ = bf16[3,128,256]{2,1,0:T(8,128)(2,1)S(1)} collective-permute-done((bf16[3,128,256]{2,1,0:T(8,128)(2,1)S(1)}, bf16[3,128,256]{2,1,0:T(8,128)(2,1)S(1)}, u32[]{:S(2)}, u32[]{:S(2)}) %collective-permute-start.7) | collective-permute-done | bytes 196640 | tf_op jit(solution)/shard_map/ppermute | solution.py:127
  143.5 8.8 %collective-permute-done.6.rest_2_ = bf16[3,128,256]{2,1,0:T(8,128)(2,1)S(1)} collective-permute-done((bf16[3,128,256]{2,1,0:T(8,128)(2,1)S(1)}, bf16[3,128,256]{2,1,0:T(8,128)(2,1)S(1)}, u32[]{:S(2)}, u32[]{:S(2)}) %collective-permute-start.6) | collective-permute-done | bytes 196640 | tf_op jit(solution)/shard_map/ppermute | solution.py:127
  152.3 3.7 %collective-permute-done.5.rest_1_ = bf16[3,128,256]{2,1,0:T(8,128)(2,1)S(1)} collective-permute-done((bf16[3,128,256]{2,1,0:T(8,128)(2,1)S(1)}, bf16[3,128,256]{2,1,0:T(8,128)(2,1)S(1)}, u32[]{:S(2)}, u32[]{:S(2)}) %collective-permute-start.5) | collective-permute-done | bytes 196640 | tf_op jit(solution)/shard_map/ppermute | solution.py:127
  156.0 0.1 pad_maximum_fusion
  156.1 0.1 fusion.9
  156.2 1.9 collective-permute-start.9
  158.1 3.9 %collective-permute-start.8 = (bf16[4,3,64,256]{3,2,1,0:T(8,128)(2,1)S(1)}, bf16[4,3,64,256]{3,2,1,0:T(8,128)(2,1)S(1)}, u32[]{:S(2)}, u32[]{:S(2)}) collective-permute-start(bf16[4,3,64,256]{3,2,1,0:T(8,128)(2,1)S(1)} %get-tuple-element.7), channel_id=1, source_target_pairs={{0,3},{3,0},{6,9},{9,6},{12,15},{15,12},{18,21},{21,18},{1,4},{4,1... | collective-permute-start | bytes 1179656 | tf_op jit(solution)/shard_map/ppermute | solution.py:170
  162.0 7.1 %collective-permute-done.9.rest_5_ = bf16[4,3,64,256]{3,2,1,0:T(8,128)(2,1)S(1)} collective-permute-done((bf16[4,3,64,256]{3,2,1,0:T(8,128)(2,1)S(1)}, bf16[4,3,64,256]{3,2,1,0:T(8,128)(2,1)S(1)}, u32[]{:S(2)}, u32[]{:S(2)}) %collective-permute-start.9) | collective-permute-done | bytes 393248 | tf_op jit(solution)/shard_map/ppermute | solution.py:171
  169.1 1.9 collective-permute-done.8.rest_4_
  171.1 0.0 copy-done.2
  171.1 10.0 %shard_map.105 = (bf16[2048,256]{1,0:T(8,128)(2,1)S(1)}, bf16[2048,256]{1,0:T(8,128)(2,1)S(1)}) custom-call(s32[1]{0:T(128)} %bitcast.53.count_ref, s32[128]{0:T(128)S(1)} %bitcast.62, s32[128]{0:T(128)S(1)} %multiply_add_fusion.pick_ref.place_ref, s32[4]{0:T(128)S(1)} %pad_add_fusion.at_ref, bf16[128,128,128]{2,1,0:T(8,128)(2,1)S(1)} %bitcast.55, ...), custom_call_target="tpu_custom_call" | custom-call | tf_op jit(solution)/shard_map/pallas_call | solution.py:94
  181.1 1.9 collective-permute-start.10
  183.0 2.6 %collective-permute-done.10 = bf16[2048,256]{1,0:T(8,128)(2,1)S(1)} collective-permute-done((bf16[2048,256]{1,0:T(8,128)(2,1)S(1)}, bf16[2048,256]{1,0:T(8,128)(2,1)S(1)}, u32[]{:S(2)}, u32[]{:S(2)}) %collective-permute-start.10) | collective-permute-done | bytes 1048608 | tf_op jit(solution)/shard_map/ppermute | solution.py:179
  185.6 0.3 add_convert_fusion
  185.9 24.0 %all_to_all.28 = bf16[4,512,256]{2,1,0:T(8,128)(2,1)S(1)} all-to-all(bf16[4,512,256]{2,1,0:T(8,128)(2,1)S(1)} %bitcast.63), channel_id=1, replica_groups=mesh['zl'=4,'x'=4,'c'=2,'y'=8,'zh'=3] {'x'}, dimensions={0} | all-to-all | bytes 2097152 | tf_op jit(solution)/shard_map/all_to_all | solution.py:114
  209.9 0.3 reduce_sum.34
  210.1 10.9 %all_to_all.29 = bf16[4,128,256]{2,1,0:T(8,128)(2,1)S(1)} all-to-all(bf16[4,128,256]{2,1,0:T(8,128)(2,1)S(1)} %bitcast.64), channel_id=1, replica_groups=mesh['zl'=4,'x'=4,'c'=2,'y'=8,'zh'=3] {'zl'}, dimensions={0} | all-to-all | bytes 524288 | tf_op jit(solution)/shard_map/all_to_all | solution.py:114
  221.1 0.8 convolution_convert_fusion
  (5 shorter events, 0.1 us)
Async XLA Ops:
  0.6 0.9 copy-start
  2.6 35.7 %copy-start.6 = (s32[1,1,128]{2,1,0:T(1,128)S(1)}, s32[1,1,128]{2,1,0:T(1,128)}, u32[]{:S(2)}) copy-start(s32[1,1,128]{2,1,0:T(1,128)} %param.15) | copy-start | bytes 1540
  2.6 37.5 %copy-start.3 = (s32[1,1,128]{2,1,0:T(1,128)S(1)}, s32[1,1,128]{2,1,0:T(1,128)}, u32[]{:S(2)}) copy-start(s32[1,1,128]{2,1,0:T(1,128)} %param.14) | copy-start | bytes 1540
  35.6 4.5 %collective-permute-start = (bf16[2048,256]{1,0:T(8,128)(2,1)S(1)}, bf16[2048,256]{1,0:T(8,128)(2,1)S(1)}, u32[]{:S(2)}, u32[]{:S(2)}) collective-permute-start(bf16[2048,256]{1,0:T(8,128)(2,1)S(1)} %bitcast.56), channel_id=1, source_target_pairs={{0,24},{24,0},{1,25},{25,1},{2,26},{26,2},{3,27},{27,3},{4,28},{28... | collective-permute-start | bytes 3145736 | tf_op jit(solution)/shard_map/ppermute | solution.py:153
  40.1 2.2 copy-start.1
  51.1 65.1 %copy-start.4 = (bf16[128,256]{1,0:T(8,128)(2,1)S(1)}, bf16[128,256]{1,0:T(8,128)(2,1)}, u32[]{:S(2)}) copy-start(bf16[128,256]{1,0:T(8,128)(2,1)} %param.17) | copy-start | bytes 196612
  51.1 65.1 %copy-start.5 = (f32[256]{0:T(256)S(1)}, f32[256]{0:T(256)}, u32[]{:S(2)}) copy-start(f32[256]{0:T(256)} %param.12) | copy-start | bytes 3076
  95.4 10.3 %collective-permute-start.1 = (bf16[128,256]{1,0:T(8,128)(2,1)S(1)}, bf16[128,256]{1,0:T(8,128)(2,1)S(1)}, u32[]{:S(2)}, u32[]{:S(2)}) collective-permute-start(bf16[128,256]{1,0:T(8,128)(2,1)S(1)} %get-tuple-element.12), channel_id=1, source_target_pairs={{0,1},{1,2},{2,0},{3,4},{4,5},{5,3},{6,7},{7,8},{8,6},{9,10},{10,1... | collective-permute-start | bytes 196616 | tf_op jit(solution)/shard_map/ppermute | solution.py:122
  103.1 68.0 %copy-start.2 = (bf16[1,1,128,128,128]{4,3,2,1,0:T(8,128)(2,1)S(1)}, bf16[1,1,128,128,128]{4,3,2,1,0:T(8,128)(2,1)}, u32[]{:S(2)}) copy-start(bf16[1,1,128,128,128]{4,3,2,1,0:T(8,128)(2,1)} %param.13) | copy-start | bytes 12582916
  103.1 13.1 %collective-permute-start.2 = (bf16[128,256]{1,0:T(8,128)(2,1)S(1)}, bf16[128,256]{1,0:T(8,128)(2,1)S(1)}, u32[]{:S(2)}, u32[]{:S(2)}) collective-permute-start(bf16[128,256]{1,0:T(8,128)(2,1)S(1)} %get-tuple-element.13), channel_id=1, source_target_pairs={{0,2},{1,0},{2,1},{3,5},{4,3},{5,4},{6,8},{7,6},{8,7},{9,11},{10,9... | collective-permute-start | bytes 196616 | tf_op jit(solution)/shard_map/ppermute | solution.py:122
  117.0 10.3 %collective-permute-start.4 = (bf16[128,256]{1,0:T(8,128)(2,1)S(1)}, bf16[128,256]{1,0:T(8,128)(2,1)S(1)}, u32[]{:S(2)}, u32[]{:S(2)}) collective-permute-start(bf16[128,256]{1,0:T(8,128)(2,1)S(1)} %get-tuple-element.8), channel_id=1, source_target_pairs={{0,2},{1,0},{2,1},{3,5},{4,3},{5,4},{6,8},{7,6},{8,7},{9,11},{10,9... | collective-permute-start | bytes 196616 | tf_op jit(solution)/shard_map/ppermute | solution.py:127
  118.9 11.7 %collective-permute-start.3 = (bf16[128,256]{1,0:T(8,128)(2,1)S(1)}, bf16[128,256]{1,0:T(8,128)(2,1)S(1)}, u32[]{:S(2)}, u32[]{:S(2)}) collective-permute-start(bf16[128,256]{1,0:T(8,128)(2,1)S(1)} %get-tuple-element.8), channel_id=1, source_target_pairs={{0,1},{1,2},{2,0},{3,4},{4,5},{5,3},{6,7},{7,8},{8,6},{9,10},{10,1... | collective-permute-start | bytes 196616 | tf_op jit(solution)/shard_map/ppermute | solution.py:127
  130.6 12.9 %collective-permute-start.7 = (bf16[3,128,256]{2,1,0:T(8,128)(2,1)S(1)}, bf16[3,128,256]{2,1,0:T(8,128)(2,1)S(1)}, u32[]{:S(2)}, u32[]{:S(2)}) collective-permute-start(bf16[3,128,256]{2,1,0:T(8,128)(2,1)S(1)} %get-tuple-element.11.rest_0_), channel_id=1, source_target_pairs={{0,18},{3,21},{6,0},{9,3},{12,6},{15,9},{18,12},{21,15},{1,19},{4,... | collective-permute-start | bytes 589832 | tf_op jit(solution)/shard_map/ppermute | solution.py:127
  132.5 19.7 %collective-permute-start.6 = (bf16[3,128,256]{2,1,0:T(8,128)(2,1)S(1)}, bf16[3,128,256]{2,1,0:T(8,128)(2,1)S(1)}, u32[]{:S(2)}, u32[]{:S(2)}) collective-permute-start(bf16[3,128,256]{2,1,0:T(8,128)(2,1)S(1)} %get-tuple-element.11.rest_0_), channel_id=1, source_target_pairs={{0,12},{3,15},{6,18},{9,21},{12,0},{15,3},{18,6},{21,9},{1,13},{4,... | collective-permute-start | bytes 589832 | tf_op jit(solution)/shard_map/ppermute | solution.py:127
  138.2 17.9 %collective-permute-start.5 = (bf16[3,128,256]{2,1,0:T(8,128)(2,1)S(1)}, bf16[3,128,256]{2,1,0:T(8,128)(2,1)S(1)}, u32[]{:S(2)}, u32[]{:S(2)}) collective-permute-start(bf16[3,128,256]{2,1,0:T(8,128)(2,1)S(1)} %get-tuple-element.11.rest_0_), channel_id=1, source_target_pairs={{0,6},{3,9},{6,12},{9,15},{12,18},{15,21},{18,0},{21,3},{1,7},{4,1... | collective-permute-start | bytes 589832 | tf_op jit(solution)/shard_map/ppermute | solution.py:127
  156.2 12.9 %collective-permute-start.9 = (bf16[4,3,64,256]{3,2,1,0:T(8,128)(2,1)S(1)}, bf16[4,3,64,256]{3,2,1,0:T(8,128)(2,1)S(1)}, u32[]{:S(2)}, u32[]{:S(2)}) collective-permute-start(bf16[4,3,64,256]{3,2,1,0:T(8,128)(2,1)S(1)} %get-tuple-element.6), channel_id=1, source_target_pairs={{0,21},{3,6},{6,3},{9,12},{12,9},{15,18},{18,15},{21,0},{1,22},{4,... | collective-permute-start | bytes 1179656 | tf_op jit(solution)/shard_map/ppermute | solution.py:171
  158.1 12.9 %collective-permute-start.8 = (bf16[4,3,64,256]{3,2,1,0:T(8,128)(2,1)S(1)}, bf16[4,3,64,256]{3,2,1,0:T(8,128)(2,1)S(1)}, u32[]{:S(2)}, u32[]{:S(2)}) collective-permute-start(bf16[4,3,64,256]{3,2,1,0:T(8,128)(2,1)S(1)} %get-tuple-element.7), channel_id=1, source_target_pairs={{0,3},{3,0},{6,9},{9,6},{12,15},{15,12},{18,21},{21,18},{1,4},{4,1... | collective-permute-start | bytes 1179656 | tf_op jit(solution)/shard_map/ppermute | solution.py:170
  181.1 4.6 %collective-permute-start.10 = (bf16[2048,256]{1,0:T(8,128)(2,1)S(1)}, bf16[2048,256]{1,0:T(8,128)(2,1)S(1)}, u32[]{:S(2)}, u32[]{:S(2)}) collective-permute-start(bf16[2048,256]{1,0:T(8,128)(2,1)S(1)} %get-tuple-element.5), channel_id=1, source_target_pairs={{0,24},{24,0},{1,25},{25,1},{2,26},{26,2},{3,27},{27,3},{4,28},{28... | collective-permute-start | bytes 3145736 | tf_op jit(solution)/shard_map/ppermute | solution.py:179

commit v4 on v2

v4 whole, which is shorter than its diff:
```python
import jax
import jax.numpy as jnp
from jax import lax
from jax.experimental import pallas as pl
from jax.experimental.pallas import tpu as pltpu
from jax.sharding import Mesh
from jax.sharding import PartitionSpec as P

ZL, X, C, Y, ZH = 4, 4, 2, 8, 3
BF, F32 = jnp.bfloat16, jnp.float32
NODE_AXES = ("zl", "x", "c", "y", "zh")
UNROLL = 16


def accumulate(count_ref, pick_ref, place_ref, tiles_ref, src, acc, transposed):
    edge = tiles_ref.shape[-1]
    dims = (((0,), (0,)), ((), ())) if transposed else (((1,), (0,)), ((), ()))
    acc[...] = jnp.zeros_like(acc)

    def step(s, carry):
        for u in range(UNROLL):
            t = s * UNROLL + u
            block = src[pl.ds(pl.multiple_of(pick_ref[t] * edge, edge), edge), :]
            product = lax.dot_general(tiles_ref[t], block, dims, preferred_element_type=F32)
            acc[pl.ds(pl.multiple_of(place_ref[t] * edge, edge), edge), :] += product
        return carry

    lax.fori_loop(0, count_ref[0] // UNROLL, step, 0)


def forward_kernel(count_ref, pick_ref, place_ref, zh_ref, tiles_ref, near_ref, far_ref, out, src, acc):
    half = near_ref.shape[0]
    edge = tiles_ref.shape[-1]
    src[:half] = near_ref[...]
    src[half:] = far_ref[...]
    accumulate(count_ref, pick_ref, place_ref, tiles_ref, src, acc, False)
    for y in range(Y):
        for k in range(ZH):
            base = pl.multiple_of((y * ZH + (zh_ref[0] + k) % ZH) * edge, edge)
            out[y, k] = acc[pl.ds(base, edge), :].astype(BF)


def backward_kernel(count_ref, pick_ref, place_ref, zh_ref, tiles_ref, ups_ref, near_ref, far_ref, src, acc):
    edge = tiles_ref.shape[-1]
    for y in range(Y):
        for k in range(ZH):
            base = pl.multiple_of((y * ZH + (zh_ref[0] + ZH - k) % ZH) * edge, edge)
            src[pl.ds(base, edge), :] = ups_ref[y, k]
    accumulate(count_ref, pick_ref, place_ref, tiles_ref, src, acc, True)
    half = near_ref.shape[0]
    near_ref[...] = acc[:half, :].astype(BF)
    far_ref[...] = acc[half:, :].astype(BF)


SMEM = pl.BlockSpec(memory_space=pltpu.SMEM)
VMEM = pl.BlockSpec(memory_space=pltpu.VMEM)


def call(kernel, outs, src_rows, acc_rows, *args):
    feat = outs[0][-1]
    return pl.pallas_call(
        kernel,
        out_shape=tuple(jax.ShapeDtypeStruct(s, BF) for s in outs),
        in_specs=[SMEM] * 4 + [VMEM] * (len(args) - 4),
        out_specs=tuple(VMEM for _ in outs),
        scratch_shapes=[pltpu.VMEM((src_rows, feat), BF), pltpu.VMEM((acc_rows, feat), F32)],
        compiler_params=pltpu.CompilerParams(vmem_limit_bytes=24 * 1024 * 1024),
    )(*args)


def shift(n, k):
    return [(i, (i + k) % n) for i in range(n)]


def swap(value, axis):
    return lax.all_to_all(value, axis, 0, 0, tiled=True)


def spread(value, axis, size):
    return swap(jnp.broadcast_to(value[None], (size,) + value.shape), axis)


def collect(pieces, axis, step):
    size = len(pieces)
    moved = [lax.ppermute(pieces[k], axis, shift(size, step * k)) for k in range(1, size)]
    return sum((piece.astype(F32) for piece in moved), pieces[0].astype(F32))


def share(value, axis, size):
    return [value] + [lax.ppermute(value, axis, shift(size, k)) for k in range(1, size)]


def total(value):
    return value.astype(F32).sum(0)


def body(
    features, degrees, weight, bias_term, tile_weights, tile_rows, tile_columns, tile_count, cotangent
):
    tiles = tile_weights[0, 0]
    rows, columns = tile_rows[0, 0], tile_columns[0, 0]
    count = tile_count[0]
    n, feat = features.shape
    wide = feat // 2
    parts = (slice(0, wide), slice(wide, feat))
    my_x = lax.axis_index("x").astype(jnp.int32)
    my_zh = lax.axis_index("zh").astype(jnp.int32)[None]
    block_zl, block_x, block_c = columns // (X * C), columns // C % X, columns % C
    other = (block_c != lax.axis_index("c")).astype(jnp.int32) * (X * ZL)
    fixed = other + block_x * ZL + block_zl
    moving = other + (my_x + X - block_x) % X * ZL + block_zl
    sources, targets, chip = C * X * ZL * n, Y * ZH * n, X * ZL * n

    inv_root = lax.rsqrt(degrees.astype(F32))[:, None]
    hidden = jnp.dot(features, weight, preferred_element_type=F32)
    scaled = (hidden * inv_root).astype(BF)

    def forward(near, at):
        far = lax.ppermute(near, "c", shift(C, 1))
        (out,) = call(
            forward_kernel, [(Y, ZH, n, wide)], sources, targets,
            count, at, rows, my_zh, tiles, near, far,
        )
        return out

    def middle(partial, part, cotangent, after):
        along_y = total(swap(partial, "y")).astype(BF)
        own_rows = collect([along_y[k] for k in range(ZH)], "zh", 1)
        own_rows, _ = lax.optimization_barrier((own_rows, after))
        preact = inv_root * (own_rows + scaled[:, part].astype(F32)) + bias_term[None, part]
        sigmoid_value = jax.nn.sigmoid(preact)
        activations = (preact * sigmoid_value).astype(BF)
        slope_value = sigmoid_value * (1.0 + preact * (1.0 - sigmoid_value))
        upstream = (cotangent[:, part].astype(F32) * slope_value * inv_root).astype(BF)
        return activations, upstream, jnp.stack(share(upstream, "zh", ZH))

    def backward(ups, at):
        own, others = call(
            backward_kernel, [(chip, wide)] * 2, targets, sources, count, rows, at, my_zh, tiles, ups
        )
        others = lax.ppermute(others, "c", shift(C, 1))
        return (own.astype(F32) + others.astype(F32)).astype(BF).reshape(X, ZL * n, wide)

    along_z = spread(scaled, "zl", ZL)
    along_z = [along_z[:, :, part].reshape(ZL * n, wide) for part in parts]
    partial_0 = forward(spread(along_z[0], "x", X).reshape(chip, wide), fixed)
    partial_0, along_z[1] = lax.optimization_barrier((partial_0, along_z[1]))
    partial_1 = forward(jnp.concatenate(share(along_z[1], "x", X), 0), moving)

    activations_0, upstream_0, along_0 = middle(partial_0, parts[0], cotangent, ())
    activations_1, upstream_1, along_1 = middle(partial_1, parts[1], cotangent, upstream_0)

    ups_0, along_1 = lax.optimization_barrier((spread(along_0, "y", Y), along_1))
    ups_1 = spread(along_1, "y", Y)
    sums = backward(ups_0, moving)
    back_0 = collect([sums[k] for k in range(X)], "x", -1).astype(BF)
    ups_1, back_0 = lax.optimization_barrier((ups_1, back_0))
    back_1 = total(swap(backward(ups_1, fixed), "x")).astype(BF)
    back = jnp.concatenate([back_0, back_1], 1).reshape(ZL, n, feat)
    own_back = total(swap(back, "zl"))
    upstream = jnp.concatenate([upstream_0, upstream_1], 1)
    grad_hidden = (inv_root * (own_back + upstream.astype(F32))).astype(BF)
    feature_grad = jnp.einsum("nf,gf->ng", grad_hidden, weight, preferred_element_type=F32)
    return jnp.concatenate([activations_0, activations_1], 1), feature_grad.astype(BF)


def solution(mesh):
    fine = Mesh(mesh.devices.reshape(ZL, X, C, Y, ZH), NODE_AXES)
    gr, gc = ("zl", "x", "c"), ("y", "zh")
    nodes = P(NODE_AXES, None)
    return jax.shard_map(
        body,
        mesh=fine,
        in_specs=(
            nodes, P(NODE_AXES), P(), P(), P(gr, gc, None, None, None), P(gr, gc, None), P(gr, gc, None),
            P(gr, gc), nodes,
        ),
        out_specs=(nodes, nodes),
        check_vma=False,
    )
```

time: 218 us -> 229 us (1.050)
  starting transfers between devices: 85.7 us -> 105 us
  Pallas kernels: 19.1 us -> 7.74 us
  local copies, waits for them, and re-layouts: 6.36 us -> 12 us
  blocking collectives: 46.1 us -> 43.2 us
    all_gather x1 -> x0, blocking collectives: 16.4 us -> none  [body(): along_z = lax.all_gather(scaled, 'zl', axis=0, tiled=True)]
    ppermute x13 -> x18, waiting for transfers between devices: 49.9 us -> 35.4 us  [the longest x7 17.8 us: share(): lax.ppermute(value, axis, shift(size, k))]
    all_to_all x2 -> x3, blocking collectives: 29.7 us -> 43.2 us  [swap(): return lax.all_to_all(value, axis, 0, 0, tiled=True)]
    all_to_all x4 -> x5, waiting for transfers between devices: 3.61 us -> 17 us  [swap(): return lax.all_to_all(value, axis, 0, 0, tiled=True)]
    all_to_all x4 -> x5, starting transfers between devices: 25.1 us -> 36.6 us  [swap(): return lax.all_to_all(value, axis, 0, 0, tiled=True)]
    pallas_call x2 -> x4, Pallas kernels: 19.1 us -> 7.74 us  [call(): pl.pallas_call(kernel, out_shape=tuple((jax.ShapeDtypeStruct(s, BF) for s...]
    ppermute x13 -> x18, starting transfers between devices: 60.5 us -> 68.4 us  [the longest x7 32 us: collect(): lax.ppermute(pieces[k], axis, shift(size, step * k))]
    unnamed x17 -> x21, local copies, waits for them, and re-layouts: 4.61 us -> 9.68 us
  transfers between devices with their start and end apart: 17 -> 23, of which waited for: 12 -> 16; matrix products, arithmetic and copies ran while one was open for 0% -> 1% of each run, Pallas kernels for 0% -> 1%
where the time goes in v4:
time: 229 us; the launch traced here: 228 us
  starting transfers between devices  105 us (46%)
  waiting for transfers between devices  52.4 us (23%)
  blocking collectives  43.2 us (19%)
  local copies, waits for them, and re-layouts  12 us (5%)
  Pallas kernels  7.74 us (3%)
  other arithmetic  3.74 us (2%)
    all_to_all x3, blocking collectives, swap(): return lax.all_to_all(value, axis, 0, 0, tiled=True)  43.2 us
    all_to_all x5, starting transfers between devices, swap(): return lax.all_to_all(value, axis, 0, 0, tiled=True)  36.6 us
    ppermute x7, starting transfers between devices, collect(): lax.ppermute(pieces[k], axis, shift(size, step * k))  32 us
    ppermute x7, starting transfers between devices, share(): lax.ppermute(value, axis, shift(size, k))  28.8 us
    ppermute x7, waiting for transfers between devices, share(): lax.ppermute(value, axis, shift(size, k))  17.8 us
    all_to_all x5, waiting for transfers between devices, swap(): return lax.all_to_all(value, axis, 0, 0, tiled=True)  17 us
    ppermute x7, waiting for transfers between devices, collect(): lax.ppermute(pieces[k], axis, shift(size, step * k))  13.4 us
    unnamed x21, local copies, waits for them, and re-layouts  9.68 us
  transfers between devices with their start and end apart: 23, of which 16 were waited for; matrix products, arithmetic and copies ran while one was open for 1% of the time, Pallas kernels for 1%

profile of v4, /device:TPU:2, one launch (start us, length us, event | category | flops | bytes accessed | tf_op | source)
XLA Modules:
  0.0 227.7 jit_solution(277161653403453117)
XLA Ops:
  0.6 0.7 convert_rsqrt_fusion
  1.3 0.2 copy-done
  1.6 1.0 fusion
  2.6 15.9 %all_to_all.40 = bf16[4,128,256]{2,1,0:T(8,128)(2,1)S(1)} all-to-all(bf16[4,128,256]{2,1,0:T(8,128)(2,1)S(1)} %broadcast_in_dim.13), channel_id=1, replica_groups=mesh['zl'=4,'x'=4,'c'=2,'y'=8,'zh'=3] {'zl'}, dimensions={0} | all-to-all | bytes 524288 | tf_op jit(solution)/shard_map/all_to_all | solution.py:76
  18.7 12.2 %all_to_all.41 = bf16[4,512,128]{2,1,0:T(8,128)(2,1)S(1)} all-to-all(bf16[4,512,128]{2,1,0:T(8,128)(2,1)S(1)} %broadcast_in_dim.15), channel_id=1, replica_groups=mesh['zl'=4,'x'=4,'c'=2,'y'=8,'zh'=3] {'x'}, dimensions={0} | all-to-all | bytes 1048576 | tf_op jit(solution)/shard_map/all_to_all | solution.py:76
  30.8 1.9 collective-permute-start
  33.4 0.7 add_add_fusion
  34.1 0.5 collective-permute-done.far_ref
  34.6 2.2 copy-done.1
  36.8 0.7 copy-done.5
  37.4 2.4 %shard_map.104 = bf16[8,3,128,128]{3,2,1,0:T(8,128)(2,1)} custom-call(s32[1]{0:T(128)} %bitcast.65.count_ref, s32[128]{0:T(128)S(1)} %get-tuple-element.24.pick_ref.place_ref, s32[128]{0:T(128)S(1)} %bitcast.75, s32[1]{0:T(128)} %bitcast.3.zh_ref, bf16[128,128,128]{2,1,0:T(8,128)(2,1)S(1)} %bitcast.69, bf16[2048,128]{1,0:T(8,128)(2,1)S(1)} %bitcast.74, ...), custom_call_target="tpu_custom_call" | custom-call | tf_op jit(solution)/shard_map/pallas_call | solution.py:61
  39.8 8.1 %all-to-all-start.2 = ((bf16[8,3,128,128]{3,2,1,0:T(8,128)(2,1)}), bf16[8,3,128,128]{3,2,1,0:T(8,128)(2,1)S(1)}, u32[]{:S(2)}, u32[]{:S(2)}) async-start(bf16[8,3,128,128]{3,2,1,0:T(8,128)(2,1)} %shard_map.104), calls=%async_computation.2 | async-start | bytes 1572864 | tf_op jit(solution)/shard_map/all_to_all | solution.py:76
  47.9 1.9 collective-permute-start.3
  49.8 5.4 %collective-permute-start.4 = (bf16[512,128]{1,0:T(8,128)(2,1)S(1)}, bf16[512,128]{1,0:T(8,128)(2,1)S(1)}, u32[]{:S(2)}, u32[]{:S(2)}) collective-permute-start(bf16[512,128]{1,0:T(8,128)(2,1)S(1)} %bitcast.82), channel_id=1, source_target_pairs={{0,96},{48,144},{96,0},{144,48},{1,97},{49,145},{97,1},{145,49},{2... | collective-permute-start | bytes 393224 | tf_op jit(solution)/shard_map/ppermute | solution.py:90
  55.3 1.9 collective-permute-start.5
  57.3 2.0 collective-permute-done.4
  59.3 2.8 %collective-permute-done.5 = bf16[512,128]{1,0:T(8,128)(2,1)S(1)} collective-permute-done((bf16[512,128]{1,0:T(8,128)(2,1)S(1)}, bf16[512,128]{1,0:T(8,128)(2,1)S(1)}, u32[]{:S(2)}, u32[]{:S(2)}) %collective-permute-start.5) | collective-permute-done | bytes 131104 | tf_op jit(solution)/shard_map/ppermute | solution.py:90
  62.2 1.9 collective-permute-start.6
  64.1 1.9 collective-permute-done.6.far_ref
  66.0 2.2 copy-done.2
  68.2 2.3 %shard_map.105 = bf16[8,3,128,128]{3,2,1,0:T(8,128)(2,1)} custom-call(s32[1]{0:T(128)} %bitcast.66.count_ref, s32[128]{0:T(128)S(1)} %fusion.9.pick_ref.place_ref, s32[128]{0:T(128)S(1)} %bitcast.76, s32[1]{0:T(128)} %bitcast.3.zh_ref, bf16[128,128,128]{2,1,0:T(8,128)(2,1)S(1)} %bitcast.70, bf16[2048,128]{1,0:T(8,128)(2,1)S(1)} %constant_dynamic-update-slice_fusion.near_ref, ...), custom_call_target="tpu_custom_call" | custom-call | tf_op jit(solution)/shard_map/pallas_call | solution.py:61
  70.5 9.1 %all-to-all-start.3 = ((bf16[8,3,128,128]{3,2,1,0:T(8,128)(2,1)}), bf16[8,3,128,128]{3,2,1,0:T(8,128)(2,1)S(1)}, u32[]{:S(2)}, u32[]{:S(2)}) async-start(bf16[8,3,128,128]{3,2,1,0:T(8,128)(2,1)} %shard_map.105), calls=%async_computation.3 | async-start | bytes 1572864 | tf_op jit(solution)/shard_map/all_to_all | solution.py:76
  79.7 9.5 %collective-permute-start.1 = (bf16[128,128]{1,0:T(8,128)(2,1)S(1)}, bf16[128,128]{1,0:T(8,128)(2,1)S(1)}, u32[]{:S(2)}, u32[]{:S(2)}) collective-permute-start(bf16[128,128]{1,0:T(8,128)(2,1)S(1)} %get-tuple-element.37), channel_id=1, source_target_pairs={{0,1},{1,2},{2,0},{3,4},{4,5},{5,3},{6,7},{7,8},{8,6},{9,10},{10,1... | collective-permute-start | bytes 98312 | tf_op jit(solution)/shard_map/ppermute | solution.py:85
  89.2 1.9 collective-permute-start.2
  91.1 7.8 %collective-permute-done.2 = bf16[128,128]{1,0:T(8,128)(2,1)S(1)} collective-permute-done((bf16[128,128]{1,0:T(8,128)(2,1)S(1)}, bf16[128,128]{1,0:T(8,128)(2,1)S(1)}, u32[]{:S(2)}, u32[]{:S(2)}) %collective-permute-start.2) | collective-permute-done | bytes 32800 | tf_op jit(solution)/shard_map/ppermute | solution.py:85
  98.9 0.1 multiply_convert_fusion.5
  99.1 4.7 %collective-permute-start.9 = (bf16[128,128]{1,0:T(8,128)(2,1)S(1)}, bf16[128,128]{1,0:T(8,128)(2,1)S(1)}, u32[]{:S(2)}, u32[]{:S(2)}) collective-permute-start(bf16[128,128]{1,0:T(8,128)(2,1)S(1)} %get-tuple-element.36), channel_id=1, source_target_pairs={{0,1},{1,2},{2,0},{3,4},{4,5},{5,3},{6,7},{7,8},{8,6},{9,10},{10,1... | collective-permute-start | bytes 98312 | tf_op jit(solution)/shard_map/ppermute | solution.py:90
  103.8 5.0 %collective-permute-start.10 = (bf16[128,128]{1,0:T(8,128)(2,1)S(1)}, bf16[128,128]{1,0:T(8,128)(2,1)S(1)}, u32[]{:S(2)}, u32[]{:S(2)}) collective-permute-start(bf16[128,128]{1,0:T(8,128)(2,1)S(1)} %get-tuple-element.36), channel_id=1, source_target_pairs={{0,2},{1,0},{2,1},{3,5},{4,3},{5,4},{6,8},{7,6},{8,7},{9,11},{10,9... | collective-permute-start | bytes 98312 | tf_op jit(solution)/shard_map/ppermute | solution.py:90
  108.9 5.1 %collective-permute-done.10 = bf16[128,128]{1,0:T(8,128)(2,1)S(1)} collective-permute-done((bf16[128,128]{1,0:T(8,128)(2,1)S(1)}, bf16[128,128]{1,0:T(8,128)(2,1)S(1)}, u32[]{:S(2)}, u32[]{:S(2)}) %collective-permute-start.10) | collective-permute-done | bytes 32800 | tf_op jit(solution)/shard_map/ppermute | solution.py:90
  114.0 1.1 broadcast_in_dim.16
  115.0 6.7 %all-to-all-start.4 = ((bf16[8,3,128,128]{3,2,1,0:T(8,128)(2,1)}), bf16[8,3,128,128]{3,2,1,0:T(8,128)(2,1)S(1)}, u32[]{:S(2)}, u32[]{:S(2)}) async-start(bf16[8,3,128,128]{3,2,1,0:T(8,128)(2,1)} %broadcast_in_dim.16), calls=%async_computation.4 | async-start | bytes 1572864 | tf_op jit(solution)/shard_map/all_to_all | solution.py:76
  121.7 0.1 reduce_sum.46
  121.8 2.5 %collective-permute-start.7 = (bf16[128,128]{1,0:T(8,128)(2,1)S(1)}, bf16[128,128]{1,0:T(8,128)(2,1)S(1)}, u32[]{:S(2)}, u32[]{:S(2)}) collective-permute-start(bf16[128,128]{1,0:T(8,128)(2,1)S(1)} %get-tuple-element.39), channel_id=1, source_target_pairs={{0,1},{1,2},{2,0},{3,4},{4,5},{5,3},{6,7},{7,8},{8,6},{9,10},{10,1... | collective-permute-start | bytes 98312 | tf_op jit(solution)/shard_map/ppermute | solution.py:85
  124.3 7.3 %collective-permute-start.8 = (bf16[128,128]{1,0:T(8,128)(2,1)S(1)}, bf16[128,128]{1,0:T(8,128)(2,1)S(1)}, u32[]{:S(2)}, u32[]{:S(2)}) collective-permute-start(bf16[128,128]{1,0:T(8,128)(2,1)S(1)} %get-tuple-element.40), channel_id=1, source_target_pairs={{0,2},{1,0},{2,1},{3,5},{4,3},{5,4},{6,8},{7,6},{8,7},{9,11},{10,9... | collective-permute-start | bytes 98312 | tf_op jit(solution)/shard_map/ppermute | solution.py:85
  131.6 0.7 collective-permute-done.7
  132.3 1.8 collective-permute-done.8
  134.1 0.1 multiply_convert_fusion.2
  134.2 7.8 %collective-permute-start.11 = (bf16[128,128]{1,0:T(8,128)(2,1)S(1)}, bf16[128,128]{1,0:T(8,128)(2,1)S(1)}, u32[]{:S(2)}, u32[]{:S(2)}) collective-permute-start(bf16[128,128]{1,0:T(8,128)(2,1)S(1)} %get-tuple-element.33), channel_id=1, source_target_pairs={{0,1},{1,2},{2,0},{3,4},{4,5},{5,3},{6,7},{7,8},{8,6},{9,10},{10,1... | collective-permute-start | bytes 98312 | tf_op jit(solution)/shard_map/ppermute | solution.py:90
  142.0 1.9 collective-permute-start.12
  143.9 0.2 collective-permute-done.11
  144.1 7.6 %collective-permute-done.12 = bf16[128,128]{1,0:T(8,128)(2,1)S(1)} collective-permute-done((bf16[128,128]{1,0:T(8,128)(2,1)S(1)}, bf16[128,128]{1,0:T(8,128)(2,1)S(1)}, u32[]{:S(2)}, u32[]{:S(2)}) %collective-permute-start.12) | collective-permute-done | bytes 32800 | tf_op jit(solution)/shard_map/ppermute | solution.py:90
  151.8 2.2 copy-done.3
  153.9 1.5 shard_map.106
  155.5 1.9 collective-permute-start.13
  157.4 1.1 broadcast_in_dim.17
  158.5 9.3 %all-to-all-start.5 = ((bf16[8,3,128,128]{3,2,1,0:T(8,128)(2,1)}), bf16[8,3,128,128]{3,2,1,0:T(8,128)(2,1)S(1)}, u32[]{:S(2)}, u32[]{:S(2)}) async-start(bf16[8,3,128,128]{3,2,1,0:T(8,128)(2,1)} %broadcast_in_dim.17), calls=%async_computation.5 | async-start | bytes 1572864 | tf_op jit(solution)/shard_map/all_to_all | solution.py:76
  167.8 0.1 add_convert_fusion.1
  168.0 1.9 collective-permute-start.14
  169.9 4.4 %collective-permute-start.15 = (bf16[512,128]{1,0:T(8,128)(2,1)S(1)}, bf16[512,128]{1,0:T(8,128)(2,1)S(1)}, u32[]{:S(2)}, u32[]{:S(2)}) collective-permute-start(bf16[512,128]{1,0:T(8,128)(2,1)S(1)} %get-tuple-element.30), channel_id=1, source_target_pairs={{0,96},{48,144},{96,0},{144,48},{1,97},{49,145},{97,1},{145,49},{2... | collective-permute-start | bytes 393224 | tf_op jit(solution)/shard_map/ppermute | solution.py:85
  174.3 4.5 %collective-permute-start.16 = (bf16[512,128]{1,0:T(8,128)(2,1)S(1)}, bf16[512,128]{1,0:T(8,128)(2,1)S(1)}, u32[]{:S(2)}, u32[]{:S(2)}) collective-permute-start(bf16[512,128]{1,0:T(8,128)(2,1)S(1)} %get-tuple-element.29), channel_id=1, source_target_pairs={{0,48},{48,96},{96,144},{144,0},{1,49},{49,97},{97,145},{145,1},{2... | collective-permute-start | bytes 393224 | tf_op jit(solution)/shard_map/ppermute | solution.py:85
  178.8 0.2 collective-permute-done.15
  179.0 3.0 %collective-permute-done.16 = bf16[512,128]{1,0:T(8,128)(2,1)S(1)} collective-permute-done((bf16[512,128]{1,0:T(8,128)(2,1)S(1)}, bf16[512,128]{1,0:T(8,128)(2,1)S(1)}, u32[]{:S(2)}, u32[]{:S(2)}) %collective-permute-start.16) | collective-permute-done | bytes 131104 | tf_op jit(solution)/shard_map/ppermute | solution.py:85
  182.1 9.5 %all-to-all-done.5.ups_ref = bf16[8,3,128,128]{3,2,1,0:T(8,128)(2,1)S(1)} async-done(((bf16[8,3,128,128]{3,2,1,0:T(8,128)(2,1)}), bf16[8,3,128,128]{3,2,1,0:T(8,128)(2,1)S(1)}, u32[]{:S(2)}, u32[]{:S(2)}) %all-to-all-start.5) | async-done | bytes 786464 | tf_op jit(solution)/shard_map/all_to_all | solution.py:76
  191.6 2.2 copy-done.4
  193.8 1.5 shard_map.107
  195.3 1.9 collective-permute-start.17
  197.3 1.8 collective-permute-done.17
  199.2 0.1 add_convert_fusion
  199.3 15.1 %all_to_all.42 = bf16[4,512,128]{2,1,0:T(8,128)(2,1)S(1)} all-to-all(bf16[4,512,128]{2,1,0:T(8,128)(2,1)S(1)} %bitcast.79), channel_id=1, replica_groups=mesh['zl'=4,'x'=4,'c'=2,'y'=8,'zh'=3] {'x'}, dimensions={0} | all-to-all | bytes 1048576 | tf_op jit(solution)/shard_map/all_to_all | solution.py:76
  214.5 0.7 pad_maximum_fusion
  215.2 3.4 %all-to-all-start.7 = ((bf16[4,128,256]{2,1,0:T(8,128)(2,1)}), bf16[4,128,256]{2,1,0:T(8,128)(2,1)S(1)}, u32[]{:S(2)}, u32[]{:S(2)}) async-start(bf16[4,128,256]{2,1,0:T(8,128)(2,1)} %bitcast.21), calls=%async_computation.7 | async-start | bytes 524288 | tf_op jit(solution)/shard_map/all_to_all | solution.py:76
  218.7 0.6 pad_maximum_fusion.3
  219.3 7.5 %all-to-all-done.7 = bf16[4,128,256]{2,1,0:T(8,128)(2,1)S(1)} async-done(((bf16[4,128,256]{2,1,0:T(8,128)(2,1)}), bf16[4,128,256]{2,1,0:T(8,128)(2,1)S(1)}, u32[]{:S(2)}, u32[]{:S(2)}) %all-to-all-start.7) | async-done | bytes 262176 | tf_op jit(solution)/shard_map/all_to_all | solution.py:76
  226.8 0.8 convolution_convert_fusion
  (40 shorter events, 0.7 us)
Async XLA Ops:
  0.6 0.9 copy-start
  30.8 3.8 %collective-permute-start = (bf16[2048,128]{1,0:T(8,128)(2,1)S(1)}, bf16[2048,128]{1,0:T(8,128)(2,1)S(1)}, u32[]{:S(2)}, u32[]{:S(2)}) collective-permute-start(bf16[2048,128]{1,0:T(8,128)(2,1)S(1)} %bitcast.73), channel_id=1, source_target_pairs={{0,24},{24,0},{1,25},{25,1},{2,26},{26,2},{3,27},{27,3},{4,28},{28... | collective-permute-start | bytes 1572872 | tf_op jit(solution)/shard_map/ppermute | solution.py:119
  34.6 2.2 copy-start.1
  36.8 0.7 copy-start.5
  37.4 28.5 %copy-start.6 = (s32[1,1,128]{2,1,0:T(1,128)S(1)}, s32[1,1,128]{2,1,0:T(1,128)}, u32[]{:S(2)}) copy-start(s32[1,1,128]{2,1,0:T(1,128)} %param.14) | copy-start | bytes 1540
  39.8 30.7 %all-to-all-start.2 = ((bf16[8,3,128,128]{3,2,1,0:T(8,128)(2,1)}), bf16[8,3,128,128]{3,2,1,0:T(8,128)(2,1)S(1)}, u32[]{:S(2)}, u32[]{:S(2)}) async-start(bf16[8,3,128,128]{3,2,1,0:T(8,128)(2,1)} %shard_map.104), calls=%async_computation.2 | async-start | bytes 1572864 | tf_op jit(solution)/shard_map/all_to_all | solution.py:76
  47.9 9.3 %collective-permute-start.3 = (bf16[512,128]{1,0:T(8,128)(2,1)S(1)}, bf16[512,128]{1,0:T(8,128)(2,1)S(1)}, u32[]{:S(2)}, u32[]{:S(2)}) collective-permute-start(bf16[512,128]{1,0:T(8,128)(2,1)S(1)} %bitcast.81), channel_id=1, source_target_pairs={{0,48},{48,96},{96,144},{144,0},{1,49},{49,97},{97,145},{145,1},{2... | collective-permute-start | bytes 393224 | tf_op jit(solution)/shard_map/ppermute | solution.py:90
  49.8 9.5 %collective-permute-start.4 = (bf16[512,128]{1,0:T(8,128)(2,1)S(1)}, bf16[512,128]{1,0:T(8,128)(2,1)S(1)}, u32[]{:S(2)}, u32[]{:S(2)}) collective-permute-start(bf16[512,128]{1,0:T(8,128)(2,1)S(1)} %bitcast.82), channel_id=1, source_target_pairs={{0,96},{48,144},{96,0},{144,48},{1,97},{49,145},{97,1},{145,49},{2... | collective-permute-start | bytes 393224 | tf_op jit(solution)/shard_map/ppermute | solution.py:90
  55.3 6.9 %collective-permute-start.5 = (bf16[512,128]{1,0:T(8,128)(2,1)S(1)}, bf16[512,128]{1,0:T(8,128)(2,1)S(1)}, u32[]{:S(2)}, u32[]{:S(2)}) collective-permute-start(bf16[512,128]{1,0:T(8,128)(2,1)S(1)} %bitcast.84), channel_id=1, source_target_pairs={{0,144},{48,0},{96,48},{144,96},{1,145},{49,1},{97,49},{145,97},{2... | collective-permute-start | bytes 393224 | tf_op jit(solution)/shard_map/ppermute | solution.py:90
  62.2 3.8 %collective-permute-start.6 = (bf16[2048,128]{1,0:T(8,128)(2,1)S(1)}, bf16[2048,128]{1,0:T(8,128)(2,1)S(1)}, u32[]{:S(2)}, u32[]{:S(2)}) collective-permute-start(bf16[2048,128]{1,0:T(8,128)(2,1)S(1)} %constant_dynamic-update-slice_fusion.near_ref), channel_id=1, source_target_pairs={{0,24},{24,0},{1,25},{25,1},{2,26},{26,2},{3,27},{27,3},{4,28},{28... | collective-permute-start | bytes 1572872 | tf_op jit(solution)/shard_map/ppermute | solution.py:119
  66.0 2.2 copy-start.2
  68.2 22.9 %copy-start.8 = (f32[256]{0:T(256)S(1)}, f32[256]{0:T(256)}, u32[]{:S(2)}) copy-start(f32[256]{0:T(256)} %param.12) | copy-start | bytes 3076
  68.2 30.8 %copy-start.7 = (bf16[128,256]{1,0:T(8,128)(2,1)S(1)}, bf16[128,256]{1,0:T(8,128)(2,1)}, u32[]{:S(2)}) copy-start(bf16[128,256]{1,0:T(8,128)(2,1)} %param.17) | copy-start | bytes 196612
  70.5 43.5 %all-to-all-start.3 = ((bf16[8,3,128,128]{3,2,1,0:T(8,128)(2,1)}), bf16[8,3,128,128]{3,2,1,0:T(8,128)(2,1)S(1)}, u32[]{:S(2)}, u32[]{:S(2)}) async-start(bf16[8,3,128,128]{3,2,1,0:T(8,128)(2,1)} %shard_map.105), calls=%async_computation.3 | async-start | bytes 1572864 | tf_op jit(solution)/shard_map/all_to_all | solution.py:76
  79.7 11.4 %collective-permute-start.1 = (bf16[128,128]{1,0:T(8,128)(2,1)S(1)}, bf16[128,128]{1,0:T(8,128)(2,1)S(1)}, u32[]{:S(2)}, u32[]{:S(2)}) collective-permute-start(bf16[128,128]{1,0:T(8,128)(2,1)S(1)} %get-tuple-element.37), channel_id=1, source_target_pairs={{0,1},{1,2},{2,0},{3,4},{4,5},{5,3},{6,7},{7,8},{8,6},{9,10},{10,1... | collective-permute-start | bytes 98312 | tf_op jit(solution)/shard_map/ppermute | solution.py:85
  89.2 9.7 %collective-permute-start.2 = (bf16[128,128]{1,0:T(8,128)(2,1)S(1)}, bf16[128,128]{1,0:T(8,128)(2,1)S(1)}, u32[]{:S(2)}, u32[]{:S(2)}) collective-permute-start(bf16[128,128]{1,0:T(8,128)(2,1)S(1)} %get-tuple-element.38), channel_id=1, source_target_pairs={{0,2},{1,0},{2,1},{3,5},{4,3},{5,4},{6,8},{7,6},{8,7},{9,11},{10,9... | collective-permute-start | bytes 98312 | tf_op jit(solution)/shard_map/ppermute | solution.py:85
  99.1 9.8 %collective-permute-start.9 = (bf16[128,128]{1,0:T(8,128)(2,1)S(1)}, bf16[128,128]{1,0:T(8,128)(2,1)S(1)}, u32[]{:S(2)}, u32[]{:S(2)}) collective-permute-start(bf16[128,128]{1,0:T(8,128)(2,1)S(1)} %get-tuple-element.36), channel_id=1, source_target_pairs={{0,1},{1,2},{2,0},{3,4},{4,5},{5,3},{6,7},{7,8},{8,6},{9,10},{10,1... | collective-permute-start | bytes 98312 | tf_op jit(solution)/shard_map/ppermute | solution.py:90
  103.8 10.2 %collective-permute-start.10 = (bf16[128,128]{1,0:T(8,128)(2,1)S(1)}, bf16[128,128]{1,0:T(8,128)(2,1)S(1)}, u32[]{:S(2)}, u32[]{:S(2)}) collective-permute-start(bf16[128,128]{1,0:T(8,128)(2,1)S(1)} %get-tuple-element.36), channel_id=1, source_target_pairs={{0,2},{1,0},{2,1},{3,5},{4,3},{5,4},{6,8},{7,6},{8,7},{9,11},{10,9... | collective-permute-start | bytes 98312 | tf_op jit(solution)/shard_map/ppermute | solution.py:90
  115.0 36.7 %all-to-all-start.4 = ((bf16[8,3,128,128]{3,2,1,0:T(8,128)(2,1)}), bf16[8,3,128,128]{3,2,1,0:T(8,128)(2,1)S(1)}, u32[]{:S(2)}, u32[]{:S(2)}) async-start(bf16[8,3,128,128]{3,2,1,0:T(8,128)(2,1)} %broadcast_in_dim.16), calls=%async_computation.4 | async-start | bytes 1572864 | tf_op jit(solution)/shard_map/all_to_all | solution.py:76
  121.8 10.4 %collective-permute-start.7 = (bf16[128,128]{1,0:T(8,128)(2,1)S(1)}, bf16[128,128]{1,0:T(8,128)(2,1)S(1)}, u32[]{:S(2)}, u32[]{:S(2)}) collective-permute-start(bf16[128,128]{1,0:T(8,128)(2,1)S(1)} %get-tuple-element.39), channel_id=1, source_target_pairs={{0,1},{1,2},{2,0},{3,4},{4,5},{5,3},{6,7},{7,8},{8,6},{9,10},{10,1... | collective-permute-start | bytes 98312 | tf_op jit(solution)/shard_map/ppermute | solution.py:85
  124.3 9.7 %collective-permute-start.8 = (bf16[128,128]{1,0:T(8,128)(2,1)S(1)}, bf16[128,128]{1,0:T(8,128)(2,1)S(1)}, u32[]{:S(2)}, u32[]{:S(2)}) collective-permute-start(bf16[128,128]{1,0:T(8,128)(2,1)S(1)} %get-tuple-element.40), channel_id=1, source_target_pairs={{0,2},{1,0},{2,1},{3,5},{4,3},{5,4},{6,8},{7,6},{8,7},{9,11},{10,9... | collective-permute-start | bytes 98312 | tf_op jit(solution)/shard_map/ppermute | solution.py:85
  134.2 10.0 %collective-permute-start.11 = (bf16[128,128]{1,0:T(8,128)(2,1)S(1)}, bf16[128,128]{1,0:T(8,128)(2,1)S(1)}, u32[]{:S(2)}, u32[]{:S(2)}) collective-permute-start(bf16[128,128]{1,0:T(8,128)(2,1)S(1)} %get-tuple-element.33), channel_id=1, source_target_pairs={{0,1},{1,2},{2,0},{3,4},{4,5},{5,3},{6,7},{7,8},{8,6},{9,10},{10,1... | collective-permute-start | bytes 98312 | tf_op jit(solution)/shard_map/ppermute | solution.py:90
  142.0 9.7 %collective-permute-start.12 = (bf16[128,128]{1,0:T(8,128)(2,1)S(1)}, bf16[128,128]{1,0:T(8,128)(2,1)S(1)}, u32[]{:S(2)}, u32[]{:S(2)}) collective-permute-start(bf16[128,128]{1,0:T(8,128)(2,1)S(1)} %get-tuple-element.33), channel_id=1, source_target_pairs={{0,2},{1,0},{2,1},{3,5},{4,3},{5,4},{6,8},{7,6},{8,7},{9,11},{10,9... | collective-permute-start | bytes 98312 | tf_op jit(solution)/shard_map/ppermute | solution.py:90
  151.8 2.2 copy-start.3
  155.5 12.3 %collective-permute-start.13 = (bf16[2048,128]{1,0:T(8,128)(2,1)S(1)}, bf16[2048,128]{1,0:T(8,128)(2,1)S(1)}, u32[]{:S(2)}, u32[]{:S(2)}) collective-permute-start(bf16[2048,128]{1,0:T(8,128)(2,1)S(1)} %get-tuple-element.19), channel_id=1, source_target_pairs={{0,24},{24,0},{1,25},{25,1},{2,26},{26,2},{3,27},{27,3},{4,28},{28... | collective-permute-start | bytes 1572872 | tf_op jit(solution)/shard_map/ppermute | solution.py:141
  158.5 33.1 %all-to-all-start.5 = ((bf16[8,3,128,128]{3,2,1,0:T(8,128)(2,1)}), bf16[8,3,128,128]{3,2,1,0:T(8,128)(2,1)S(1)}, u32[]{:S(2)}, u32[]{:S(2)}) async-start(bf16[8,3,128,128]{3,2,1,0:T(8,128)(2,1)} %broadcast_in_dim.17), calls=%async_computation.5 | async-start | bytes 1572864 | tf_op jit(solution)/shard_map/all_to_all | solution.py:76
  168.0 10.9 %collective-permute-start.14 = (bf16[512,128]{1,0:T(8,128)(2,1)S(1)}, bf16[512,128]{1,0:T(8,128)(2,1)S(1)}, u32[]{:S(2)}, u32[]{:S(2)}) collective-permute-start(bf16[512,128]{1,0:T(8,128)(2,1)S(1)} %get-tuple-element.28), channel_id=1, source_target_pairs={{0,144},{48,0},{96,48},{144,96},{1,145},{49,1},{97,49},{145,97},{2... | collective-permute-start | bytes 393224 | tf_op jit(solution)/shard_map/ppermute | solution.py:85
  169.9 9.1 %collective-permute-start.15 = (bf16[512,128]{1,0:T(8,128)(2,1)S(1)}, bf16[512,128]{1,0:T(8,128)(2,1)S(1)}, u32[]{:S(2)}, u32[]{:S(2)}) collective-permute-start(bf16[512,128]{1,0:T(8,128)(2,1)S(1)} %get-tuple-element.30), channel_id=1, source_target_pairs={{0,96},{48,144},{96,0},{144,48},{1,97},{49,145},{97,1},{145,49},{2... | collective-permute-start | bytes 393224 | tf_op jit(solution)/shard_map/ppermute | solution.py:85
  174.3 7.7 %collective-permute-start.16 = (bf16[512,128]{1,0:T(8,128)(2,1)S(1)}, bf16[512,128]{1,0:T(8,128)(2,1)S(1)}, u32[]{:S(2)}, u32[]{:S(2)}) collective-permute-start(bf16[512,128]{1,0:T(8,128)(2,1)S(1)} %get-tuple-element.29), channel_id=1, source_target_pairs={{0,48},{48,96},{96,144},{144,0},{1,49},{49,97},{97,145},{145,1},{2... | collective-permute-start | bytes 393224 | tf_op jit(solution)/shard_map/ppermute | solution.py:85
  191.6 2.2 copy-start.4
  195.3 3.8 %collective-permute-start.17 = (bf16[2048,128]{1,0:T(8,128)(2,1)S(1)}, bf16[2048,128]{1,0:T(8,128)(2,1)S(1)}, u32[]{:S(2)}, u32[]{:S(2)}) collective-permute-start(bf16[2048,128]{1,0:T(8,128)(2,1)S(1)} %get-tuple-element.23), channel_id=1, source_target_pairs={{0,24},{24,0},{1,25},{25,1},{2,26},{26,2},{3,27},{27,3},{4,28},{28... | collective-permute-start | bytes 1572872 | tf_op jit(solution)/shard_map/ppermute | solution.py:141
  215.2 11.6 %all-to-all-start.7 = ((bf16[4,128,256]{2,1,0:T(8,128)(2,1)}), bf16[4,128,256]{2,1,0:T(8,128)(2,1)S(1)}, u32[]{:S(2)}, u32[]{:S(2)}) async-start(bf16[4,128,256]{2,1,0:T(8,128)(2,1)} %bitcast.21), calls=%async_computation.7 | async-start | bytes 524288 | tf_op jit(solution)/shard_map/all_to_all | solution.py:76

commit v5 on v3

v5 whole, which is shorter than its diff:
```python
import jax
import jax.numpy as jnp
from jax import lax
from jax.experimental import pallas as pl
from jax.experimental.pallas import tpu as pltpu
from jax.sharding import Mesh
from jax.sharding import PartitionSpec as P

ZL, X, C, Y, ZH = 4, 4, 2, 8, 3
BF, F32 = jnp.bfloat16, jnp.float32
NODE_AXES = ("zl", "x", "c", "y", "zh")
UNROLL = 16
PARTS = 4


def fetch(tiles_ref, tiles, sems):
    size = tiles.shape[0] // PARTS
    copies = []
    for part in range(PARTS):
        slots = pl.ds(part * size, size)
        copies.append(pltpu.make_async_copy(tiles_ref.at[slots], tiles.at[slots], sems.at[part]))
        copies[-1].start()
    return copies


def accumulate(count_ref, pick_ref, place_ref, tiles, copies, src, acc, transposed):
    edge = tiles.shape[-1]
    size = tiles.shape[0] // PARTS
    dims = (((0,), (0,)), ((), ())) if transposed else (((1,), (0,)), ((), ()))
    acc[...] = jnp.zeros_like(acc)

    for part in range(PARTS):
        copies[part].wait()

        def step(s, carry, first=part * size):
            for u in range(UNROLL):
                t = first + s * UNROLL + u
                block = src[pl.ds(pl.multiple_of(pick_ref[t] * edge, edge), edge), :]
                product = lax.dot_general(tiles[t], block, dims, preferred_element_type=F32)
                acc[pl.ds(pl.multiple_of(place_ref[t] * edge, edge), edge), :] += product
            return carry

        live = jnp.clip(count_ref[0] - part * size, 0, size)
        lax.fori_loop(0, live // UNROLL, step, 0)


def forward_kernel(
    count_ref, pick_ref, place_ref, zh_ref, tiles_ref, near_ref, far_ref, out, src, acc, tiles, sems
):
    copies = fetch(tiles_ref, tiles, sems)
    half = near_ref.shape[0]
    edge = tiles.shape[-1]
    src[:half] = near_ref[...]
    src[half:] = far_ref[...]
    accumulate(count_ref, pick_ref, place_ref, tiles, copies, src, acc, False)
    for y in range(Y):
        for k in range(ZH):
            base = pl.multiple_of((y * ZH + (zh_ref[0] + k) % ZH) * edge, edge)
            out[y, k] = acc[pl.ds(base, edge), :].astype(BF)


def backward_kernel(
    count_ref, pick_ref, place_ref, zh_ref, tiles_ref, ups_ref, near_ref, far_ref, src, acc, tiles, sems
):
    copies = fetch(tiles_ref, tiles, sems)
    edge = tiles.shape[-1]
    for y in range(Y):
        for k in range(ZH):
            base = pl.multiple_of((y * ZH + (zh_ref[0] + k) % ZH) * edge, edge)
            src[pl.ds(base, edge), :] = ups_ref[y, k]
    accumulate(count_ref, pick_ref, place_ref, tiles, copies, src, acc, True)
    half = near_ref.shape[0]
    near_ref[...] = acc[:half, :].astype(BF)
    far_ref[...] = acc[half:, :].astype(BF)


SMEM = pl.BlockSpec(memory_space=pltpu.SMEM)
VMEM = pl.BlockSpec(memory_space=pltpu.VMEM)
HBM = pl.BlockSpec(memory_space=pltpu.HBM)


def call(kernel, outs, src_rows, acc_rows, *args):
    feat = outs[0][-1]
    tiles = args[4]
    return pl.pallas_call(
        kernel,
        out_shape=tuple(jax.ShapeDtypeStruct(s, BF) for s in outs),
        in_specs=[SMEM] * 4 + [HBM] + [VMEM] * (len(args) - 5),
        out_specs=tuple(VMEM for _ in outs),
        scratch_shapes=[
            pltpu.VMEM((src_rows, feat), BF),
            pltpu.VMEM((acc_rows, feat), F32),
            pltpu.VMEM(tiles.shape, BF),
            pltpu.SemaphoreType.DMA((PARTS,)),
        ],
        compiler_params=pltpu.CompilerParams(vmem_limit_bytes=40 * 1024 * 1024),
    )(*args)


def shift(n, k):
    return [(i, (i + k) % n) for i in range(n)]


def swap(value, axis):
    return lax.all_to_all(value, axis, 0, 0, tiled=True)


def spread(value, axis, size):
    return swap(jnp.broadcast_to(value[None], (size,) + value.shape), axis)


def share(value, axis, size):
    return [value] + [lax.ppermute(value, axis, shift(size, k)) for k in range(1, size)]


def total(value):
    return value.astype(F32).sum(0)


def body(
    features, degrees, weight, bias_term, tile_weights, tile_rows, tile_columns, tile_count, cotangent
):
    tiles = tile_weights[0, 0]
    rows, columns = tile_rows[0, 0], tile_columns[0, 0]
    count = tile_count[0]
    n, feat = features.shape
    my_zh = lax.axis_index("zh").astype(jnp.int32)[None]
    other = (columns % C != lax.axis_index("c")).astype(jnp.int32)
    column_at = other * (ZL * X) + columns // C
    sources, targets, chip = C * ZL * X * n, Y * ZH * n, ZL * X * n

    degree = degrees.astype(F32)[:, None]
    inv_root = lax.rsqrt(degree)
    hidden = jnp.dot(features, weight, preferred_element_type=F32)
    scaled = (hidden * inv_root).astype(BF)

    near = spread(scaled, ("zl", "x"), ZL * X).reshape(chip, feat)
    far = lax.ppermute(near, "c", shift(C, 1))
    (partial,) = call(
        forward_kernel, [(Y, ZH, n, feat)], sources, targets,
        count, column_at, rows, my_zh, tiles, near, far,
    )
    along_y = total(swap(partial, "y")).astype(BF)
    shared = share(along_y, "zh", ZH)
    own_rows = sum(
        jnp.concatenate([shared[j][(k + j) % ZH] for k in range(ZH)], 0).astype(F32) for j in range(ZH)
    )
    beside = jnp.concatenate([cotangent, scaled, jnp.broadcast_to(degree.astype(BF), (n, n))], 1)
    beside = share(beside, "zh", ZH)
    beside = jnp.concatenate([beside[-k % ZH] for k in range(ZH)], 0).astype(F32)
    cotangents, scales = beside[:, :feat], beside[:, feat : 2 * feat]
    roots = lax.rsqrt(beside[:, 2 * feat : 2 * feat + 1])

    preact = roots * (own_rows + scales) + bias_term[None, :]
    sigmoid_value = jax.nn.sigmoid(preact)
    activations = (preact * sigmoid_value)[:n].astype(BF)
    slope_value = sigmoid_value * (1.0 + preact * (1.0 - sigmoid_value))
    upstream = (cotangents * slope_value * roots).astype(BF)

    ups = spread(upstream.reshape(ZH, n, feat), "y", Y)
    own, others = call(
        backward_kernel, [(chip, feat)] * 2, targets, sources, count, rows, column_at, my_zh, tiles, ups
    )
    others = lax.ppermute(others, "c", shift(C, 1))
    back = (own.astype(F32) + others.astype(F32)).astype(BF).reshape(ZL * X, n, feat)
    own_back = total(swap(back, ("zl", "x")))
    grad_hidden = (inv_root * (own_back + upstream[:n].astype(F32))).astype(BF)
    feature_grad = jnp.einsum("nf,gf->ng", grad_hidden, weight, preferred_element_type=F32)
    return activations, feature_grad.astype(BF)


def solution(mesh):
    fine = Mesh(mesh.devices.reshape(ZL, X, C, Y, ZH), NODE_AXES)
    gr, gc = ("zl", "x", "c"), ("y", "zh")
    nodes = P(NODE_AXES, None)
    return jax.shard_map(
        body,
        mesh=fine,
        in_specs=(
            nodes, P(NODE_AXES), P(), P(), P(gr, gc, None, None, None), P(gr, gc, None), P(gr, gc, None),
            P(gr, gc), nodes,
        ),
        out_specs=(nodes, nodes),
        check_vma=False,
    )
```

time: 223 us -> 219 us (0.982)
  the two profiles are of different devices: /device:TPU:8 before, /device:TPU:64 now
where the time goes in v5:
time: 219 us
  blocking collectives  77.3 us (35%)
  waiting for transfers between devices  72.9 us (33%)
  starting transfers between devices  50.9 us (23%)
  Pallas kernels  7.72 us (4%)
  other arithmetic  3.67 us (2%)
  local copies, waits for them, and re-layouts  2.76 us (1%)
    all_to_all x2, blocking collectives, swap(): return lax.all_to_all(value, axis, 0, 0, tiled=True)  77.3 us
    all_to_all x2, waiting for transfers between devices, swap(): return lax.all_to_all(value, axis, 0, 0, tiled=True)  37.7 us
    ppermute x4, waiting for transfers between devices, share(): lax.ppermute(value, axis, shift(size, k))  30.6 us
    ppermute x4, starting transfers between devices, share(): lax.ppermute(value, axis, shift(size, k))  29.3 us
    all_to_all x2, starting transfers between devices, swap(): return lax.all_to_all(value, axis, 0, 0, tiled=True)  17.8 us
    pallas_call x2, Pallas kernels, call(): pl.pallas_call(kernel, out_shape=tuple((jax.ShapeDtypeStruct(s, BF) for s...  7.72 us
  transfers between devices with their start and end apart: 8, of which 8 were waited for; matrix products, arithmetic and copies ran while one was open for 0% of the time, Pallas kernels for 0%

profile of v5, /device:TPU:64, one launch (start us, length us, event | category | flops | bytes accessed | tf_op | source)
XLA Modules:
  0.0 218.6 jit_solution(7030519871958794976)
XLA Ops:
  0.6 0.0 copy-start
  0.6 0.0 copy-start.6
  0.7 0.0 copy-start.3
  0.7 0.7 convert_rsqrt_fusion.1
  1.4 0.2 copy-done
  1.5 1.0 fusion
  2.5 0.1 broadcast_in_dim.12
  2.7 35.3 %all_to_all.20 = bf16[16,128,256]{2,1,0:T(8,128)(2,1)S(1)} all-to-all(bf16[16,128,256]{2,1,0:T(8,128)(2,1)S(1)} %broadcast_in_dim.12), channel_id=1, replica_groups=mesh['zl'=4,'x'=4,'c'=2,'y'=8,'zh'=3] {'zl','x'}, dimensions={0} | all-to-all | bytes 2097152 | tf_op jit(solution)/shard_map/all_to_all | solution.py:105
  37.9 1.9 collective-permute-start.2
  40.5 0.0 copy-done.6
  40.5 1.9 collective-permute-done.2.far_ref
  42.4 0.0 copy-done.3
  42.5 0.0 copy-start.1
  42.5 2.2 %copy-done.1 = bf16[1,1,128,128,128]{4,3,2,1,0:T(8,128)(2,1)S(1)} copy-done((bf16[1,1,128,128,128]{4,3,2,1,0:T(8,128)(2,1)S(1)}, bf16[1,1,128,128,128]{4,3,2,1,0:T(8,128)(2,1)}, u32[]{:S(2)}) %copy-start.1) | copy-done | bytes 4194328
  44.6 4.3 %shard_map.104 = bf16[8,3,128,256]{3,2,1,0:T(8,128)(2,1)} custom-call(s32[1]{0:T(128)} %bitcast.41.count_ref, s32[128]{0:T(128)S(1)} %fusion.7.pick_ref.place_ref, s32[128]{0:T(128)S(1)} %bitcast.47, s32[1]{0:T(128)} %bitcast.3.zh_ref, bf16[128,128,128]{2,1,0:T(8,128)(2,1)S(1)} %bitcast.43, bf16[2048,256]{1,0:T(8,128)(2,1)S(1)} %bitcast.46, ...), custom_call_target="tpu_custom_call" | custom-call | tf_op jit(solution)/shard_map/pallas_call | solution.py:85
  49.0 0.0 copy-start.7
  49.0 0.0 copy-start.4
  49.0 7.2 %all-to-all-start.1 = ((bf16[8,3,128,256]{3,2,1,0:T(8,128)(2,1)}), bf16[8,3,128,256]{3,2,1,0:T(8,128)(2,1)S(1)}, u32[]{:S(2)}, u32[]{:S(2)}) async-start(bf16[8,3,128,256]{3,2,1,0:T(8,128)(2,1)} %shard_map.104), calls=%async_computation.1 | async-start | bytes 3145728 | tf_op jit(solution)/shard_map/all_to_all | solution.py:105
  56.2 0.0 copy-done.7
  56.2 0.0 copy-start.5
  56.2 0.1 broadcast_in_dim.10
  56.3 0.0 copy-done.4
  56.3 12.4 %collective-permute-start.1 = (bf16[128,640]{1,0:T(8,128)(2,1)S(1)}, bf16[128,640]{1,0:T(8,128)(2,1)S(1)}, u32[]{:S(2)}, u32[]{:S(2)}) collective-permute-start(bf16[128,640]{1,0:T(8,128)(2,1)S(1)} %pad_maximum_fusion.4), channel_id=1, source_target_pairs={{0,1},{1,2},{2,0},{3,4},{4,5},{5,3},{6,7},{7,8},{8,6},{9,10},{10,1... | collective-permute-start | bytes 491528 | tf_op jit(solution)/shard_map/ppermute | solution.py:113
  68.7 2.4 %collective-permute-start = (bf16[128,640]{1,0:T(8,128)(2,1)S(1)}, bf16[128,640]{1,0:T(8,128)(2,1)S(1)}, u32[]{:S(2)}, u32[]{:S(2)}) collective-permute-start(bf16[128,640]{1,0:T(8,128)(2,1)S(1)} %pad_maximum_fusion.4), channel_id=1, source_target_pairs={{0,2},{1,0},{2,1},{3,5},{4,3},{5,4},{6,8},{7,6},{8,7},{9,11},{10,9... | collective-permute-start | bytes 491528 | tf_op jit(solution)/shard_map/ppermute | solution.py:113
  71.1 10.6 %collective-permute-done.1 = bf16[128,640]{1,0:T(8,128)(2,1)S(1)} collective-permute-done((bf16[128,640]{1,0:T(8,128)(2,1)S(1)}, bf16[128,640]{1,0:T(8,128)(2,1)S(1)}, u32[]{:S(2)}, u32[]{:S(2)}) %collective-permute-start.1) | collective-permute-done | bytes 163872 | tf_op jit(solution)/shard_map/ppermute | solution.py:113
  81.7 3.5 %collective-permute-done = bf16[128,640]{1,0:T(8,128)(2,1)S(1)} collective-permute-done((bf16[128,640]{1,0:T(8,128)(2,1)S(1)}, bf16[128,640]{1,0:T(8,128)(2,1)S(1)}, u32[]{:S(2)}, u32[]{:S(2)}) %collective-permute-start) | collective-permute-done | bytes 163872 | tf_op jit(solution)/shard_map/ppermute | solution.py:113
  85.1 0.2 fusion.3
  85.3 12.2 %all-to-all-done.1 = bf16[8,3,128,256]{3,2,1,0:T(8,128)(2,1)S(1)} async-done(((bf16[8,3,128,256]{3,2,1,0:T(8,128)(2,1)}), bf16[8,3,128,256]{3,2,1,0:T(8,128)(2,1)S(1)}, u32[]{:S(2)}, u32[]{:S(2)}) %all-to-all-start.1) | async-done | bytes 1572896 | tf_op jit(solution)/shard_map/all_to_all | solution.py:105
  97.5 0.3 reduce_sum.21
  97.8 12.6 %collective-permute-start.4 = (bf16[3,128,256]{2,1,0:T(8,128)(2,1)S(1)}, bf16[3,128,256]{2,1,0:T(8,128)(2,1)S(1)}, u32[]{:S(2)}, u32[]{:S(2)}) collective-permute-start(bf16[3,128,256]{2,1,0:T(8,128)(2,1)S(1)} %reduce_sum.21), channel_id=1, source_target_pairs={{0,2},{1,0},{2,1},{3,5},{4,3},{5,4},{6,8},{7,6},{8,7},{9,11},{10,9... | collective-permute-start | bytes 589832 | tf_op jit(solution)/shard_map/ppermute | solution.py:113
  110.4 1.9 collective-permute-start.3
  112.4 13.0 %collective-permute-done.4 = bf16[3,128,256]{2,1,0:T(8,128)(2,1)S(1)} collective-permute-done((bf16[3,128,256]{2,1,0:T(8,128)(2,1)S(1)}, bf16[3,128,256]{2,1,0:T(8,128)(2,1)S(1)}, u32[]{:S(2)}, u32[]{:S(2)}) %collective-permute-start.4) | collective-permute-done | bytes 196640 | tf_op jit(solution)/shard_map/ppermute | solution.py:113
  125.4 3.5 %collective-permute-done.3 = bf16[3,128,256]{2,1,0:T(8,128)(2,1)S(1)} collective-permute-done((bf16[3,128,256]{2,1,0:T(8,128)(2,1)S(1)}, bf16[3,128,256]{2,1,0:T(8,128)(2,1)S(1)}, u32[]{:S(2)}, u32[]{:S(2)}) %collective-permute-start.3) | collective-permute-done | bytes 196640 | tf_op jit(solution)/shard_map/ppermute | solution.py:113
  129.0 0.0 copy-done.5
  129.0 0.3 multiply_convert_fusion
  129.3 0.0 copy-start.2
  129.3 0.2 broadcast_in_dim.27
  129.5 42.1 %all_to_all.21.ups_ref = bf16[8,3,128,256]{3,2,1,0:T(8,128)(2,1)S(1)} all-to-all(bf16[8,3,128,256]{3,2,1,0:T(8,128)(2,1)S(1)} %broadcast_in_dim.27), channel_id=1, replica_groups=mesh['zl'=4,'x'=4,'c'=2,'y'=8,'zh'=3] {'y'}, dimensions={0} | all-to-all | bytes 3145728 | tf_op jit(solution)/shard_map/all_to_all | solution.py:105
  171.5 0.0 copy-done.2
  171.5 3.4 %shard_map.105 = (bf16[2048,256]{1,0:T(8,128)(2,1)S(1)}, bf16[2048,256]{1,0:T(8,128)(2,1)S(1)}) custom-call(s32[1]{0:T(128)} %bitcast.42.count_ref, s32[128]{0:T(128)S(1)} %bitcast.48, s32[128]{0:T(128)S(1)} %fusion.7.pick_ref.place_ref, s32[1]{0:T(128)} %bitcast.3.zh_ref, bf16[128,128,128]{2,1,0:T(8,128)(2,1)S(1)} %bitcast.44, ...), custom_call_target="tpu_custom_call" | custom-call | tf_op jit(solution)/shard_map/pallas_call | solution.py:85
  174.9 1.9 collective-permute-start.5
  176.8 2.6 %collective-permute-done.5 = bf16[2048,256]{1,0:T(8,128)(2,1)S(1)} collective-permute-done((bf16[2048,256]{1,0:T(8,128)(2,1)S(1)}, bf16[2048,256]{1,0:T(8,128)(2,1)S(1)}, u32[]{:S(2)}, u32[]{:S(2)}) %collective-permute-start.5) | collective-permute-done | bytes 1048608 | tf_op jit(solution)/shard_map/ppermute | solution.py:164
  179.5 1.3 add_convert_fusion
  180.8 10.6 %all-to-all-start.3 = ((bf16[16,128,256]{2,1,0:T(8,128)(2,1)}), bf16[16,128,256]{2,1,0:T(8,128)(2,1)S(1)}, u32[]{:S(2)}, u32[]{:S(2)}) async-start(bf16[16,128,256]{2,1,0:T(8,128)(2,1)} %bitcast.16), calls=%async_computation.3 | async-start | bytes 2097152 | tf_op jit(solution)/shard_map/all_to_all | solution.py:105
  191.4 0.1 add_divide_fusion
  191.5 0.6 fusion.4
  192.1 25.5 %all-to-all-done.3 = bf16[16,128,256]{2,1,0:T(8,128)(2,1)S(1)} async-done(((bf16[16,128,256]{2,1,0:T(8,128)(2,1)}), bf16[16,128,256]{2,1,0:T(8,128)(2,1)S(1)}, u32[]{:S(2)}, u32[]{:S(2)}) %all-to-all-start.3) | async-done | bytes 1048608 | tf_op jit(solution)/shard_map/all_to_all | solution.py:105
  217.6 0.1 convert_reduce_fusion
  217.8 0.8 convolution_convert_fusion
  (6 shorter events, 0.1 us)
Async XLA Ops:
  0.6 0.9 copy-start
  0.6 39.8 %copy-start.6 = (s32[1,1,128]{2,1,0:T(1,128)S(1)}, s32[1,1,128]{2,1,0:T(1,128)}, u32[]{:S(2)}) copy-start(s32[1,1,128]{2,1,0:T(1,128)} %param.15) | copy-start | bytes 1540
  0.7 41.8 %copy-start.3 = (s32[1,1,128]{2,1,0:T(1,128)S(1)}, s32[1,1,128]{2,1,0:T(1,128)}, u32[]{:S(2)}) copy-start(s32[1,1,128]{2,1,0:T(1,128)} %param.14) | copy-start | bytes 1540
  37.9 4.5 %collective-permute-start.2 = (bf16[2048,256]{1,0:T(8,128)(2,1)S(1)}, bf16[2048,256]{1,0:T(8,128)(2,1)S(1)}, u32[]{:S(2)}, u32[]{:S(2)}) collective-permute-start(bf16[2048,256]{1,0:T(8,128)(2,1)S(1)} %bitcast.45), channel_id=1, source_target_pairs={{0,24},{24,0},{1,25},{25,1},{2,26},{26,2},{3,27},{27,3},{4,28},{28... | collective-permute-start | bytes 3145736 | tf_op jit(solution)/shard_map/ppermute | solution.py:138
  42.5 2.2 %copy-start.1 = (bf16[1,1,128,128,128]{4,3,2,1,0:T(8,128)(2,1)S(1)}, bf16[1,1,128,128,128]{4,3,2,1,0:T(8,128)(2,1)}, u32[]{:S(2)}) copy-start(bf16[1,1,128,128,128]{4,3,2,1,0:T(8,128)(2,1)} %param.13) | copy-start | bytes 12582916
  49.0 7.2 %copy-start.7 = (s32[128]{0:T(128)S(1)}, s32[128]{0:T(128)}, u32[]{:S(2)}) copy-start(s32[128]{0:T(128)} %param.10) | copy-start | bytes 1540
  49.0 7.3 %copy-start.4 = (bf16[128,256]{1,0:T(8,128)(2,1)S(1)}, bf16[128,256]{1,0:T(8,128)(2,1)}, u32[]{:S(2)}) copy-start(bf16[128,256]{1,0:T(8,128)(2,1)} %param.17) | copy-start | bytes 196612
  49.0 48.5 %all-to-all-start.1 = ((bf16[8,3,128,256]{3,2,1,0:T(8,128)(2,1)}), bf16[8,3,128,256]{3,2,1,0:T(8,128)(2,1)S(1)}, u32[]{:S(2)}, u32[]{:S(2)}) async-start(bf16[8,3,128,256]{3,2,1,0:T(8,128)(2,1)} %shard_map.104), calls=%async_computation.1 | async-start | bytes 3145728 | tf_op jit(solution)/shard_map/all_to_all | solution.py:105
  56.2 72.8 %copy-start.5 = (f32[256]{0:T(256)S(1)}, f32[256]{0:T(256)}, u32[]{:S(2)}) copy-start(f32[256]{0:T(256)} %param.12) | copy-start | bytes 3076
  56.3 25.3 %collective-permute-start.1 = (bf16[128,640]{1,0:T(8,128)(2,1)S(1)}, bf16[128,640]{1,0:T(8,128)(2,1)S(1)}, u32[]{:S(2)}, u32[]{:S(2)}) collective-permute-start(bf16[128,640]{1,0:T(8,128)(2,1)S(1)} %pad_maximum_fusion.4), channel_id=1, source_target_pairs={{0,1},{1,2},{2,0},{3,4},{4,5},{5,3},{6,7},{7,8},{8,6},{9,10},{10,1... | collective-permute-start | bytes 491528 | tf_op jit(solution)/shard_map/ppermute | solution.py:113
  68.7 16.4 %collective-permute-start = (bf16[128,640]{1,0:T(8,128)(2,1)S(1)}, bf16[128,640]{1,0:T(8,128)(2,1)S(1)}, u32[]{:S(2)}, u32[]{:S(2)}) collective-permute-start(bf16[128,640]{1,0:T(8,128)(2,1)S(1)} %pad_maximum_fusion.4), channel_id=1, source_target_pairs={{0,2},{1,0},{2,1},{3,5},{4,3},{5,4},{6,8},{7,6},{8,7},{9,11},{10,9... | collective-permute-start | bytes 491528 | tf_op jit(solution)/shard_map/ppermute | solution.py:113
  97.8 27.6 %collective-permute-start.4 = (bf16[3,128,256]{2,1,0:T(8,128)(2,1)S(1)}, bf16[3,128,256]{2,1,0:T(8,128)(2,1)S(1)}, u32[]{:S(2)}, u32[]{:S(2)}) collective-permute-start(bf16[3,128,256]{2,1,0:T(8,128)(2,1)S(1)} %reduce_sum.21), channel_id=1, source_target_pairs={{0,2},{1,0},{2,1},{3,5},{4,3},{5,4},{6,8},{7,6},{8,7},{9,11},{10,9... | collective-permute-start | bytes 589832 | tf_op jit(solution)/shard_map/ppermute | solution.py:113
  110.4 18.5 %collective-permute-start.3 = (bf16[3,128,256]{2,1,0:T(8,128)(2,1)S(1)}, bf16[3,128,256]{2,1,0:T(8,128)(2,1)S(1)}, u32[]{:S(2)}, u32[]{:S(2)}) collective-permute-start(bf16[3,128,256]{2,1,0:T(8,128)(2,1)S(1)} %reduce_sum.21), channel_id=1, source_target_pairs={{0,1},{1,2},{2,0},{3,4},{4,5},{5,3},{6,7},{7,8},{8,6},{9,10},{10,1... | collective-permute-start | bytes 589832 | tf_op jit(solution)/shard_map/ppermute | solution.py:113
  129.3 42.2 %copy-start.2 = (bf16[1,1,128,128,128]{4,3,2,1,0:T(8,128)(2,1)S(1)}, bf16[1,1,128,128,128]{4,3,2,1,0:T(8,128)(2,1)}, u32[]{:S(2)}) copy-start(bf16[1,1,128,128,128]{4,3,2,1,0:T(8,128)(2,1)} %param.13) | copy-start | bytes 12582916
  174.9 4.6 %collective-permute-start.5 = (bf16[2048,256]{1,0:T(8,128)(2,1)S(1)}, bf16[2048,256]{1,0:T(8,128)(2,1)S(1)}, u32[]{:S(2)}, u32[]{:S(2)}) collective-permute-start(bf16[2048,256]{1,0:T(8,128)(2,1)S(1)} %get-tuple-element.5), channel_id=1, source_target_pairs={{0,24},{24,0},{1,25},{25,1},{2,26},{26,2},{3,27},{27,3},{4,28},{28... | collective-permute-start | bytes 3145736 | tf_op jit(solution)/shard_map/ppermute | solution.py:164
  180.8 36.9 %all-to-all-start.3 = ((bf16[16,128,256]{2,1,0:T(8,128)(2,1)}), bf16[16,128,256]{2,1,0:T(8,128)(2,1)S(1)}, u32[]{:S(2)}, u32[]{:S(2)}) async-start(bf16[16,128,256]{2,1,0:T(8,128)(2,1)} %bitcast.16), calls=%async_computation.3 | async-start | bytes 2097152 | tf_op jit(solution)/shard_map/all_to_all | solution.py:105

commit v6 on v4

--- a/solution.py
+++ b/solution.py
@@ -44,12 +44,48 @@
     edge = tiles_ref.shape[-1]
     for y in range(Y):
         for k in range(ZH):
-            base = pl.multiple_of((y * ZH + (zh_ref[0] + ZH - k) % ZH) * edge, edge)
+            base = pl.multiple_of((y * ZH + (zh_ref[0] + k) % ZH) * edge, edge)
             src[pl.ds(base, edge), :] = ups_ref[y, k]
     accumulate(count_ref, pick_ref, place_ref, tiles_ref, src, acc, True)
     half = near_ref.shape[0]
     near_ref[...] = acc[:half, :].astype(BF)
     far_ref[...] = acc[half:, :].astype(BF)
+
+
+def pack_kernel(along_y_ref, scaled_ref, cotangent_ref, degree_ref, out):
+    n = scaled_ref.shape[0]
+    for k in range(ZH):
+        summed = along_y_ref[0, k].astype(F32)
+        for y in range(1, Y):
+            summed += along_y_ref[y, k].astype(F32)
+        if k == 0:
+            summed += scaled_ref[...].astype(F32)
+        out[k * n : (k + 1) * n, :] = summed.astype(BF)
+    out[ZH * n : (ZH + 1) * n, :] = cotangent_ref[...]
+    out[(ZH + 1) * n :, :] = degree_ref[...]
+
+
+def middle_kernel(own_ref, back_1_ref, back_2_ref, bias_ref, activations_ref, upstream_ref, copies_ref):
+    shared = (own_ref, back_1_ref, back_2_ref)
+    n, wide = activations_ref.shape
+    for k in range(ZH):
+        gathered = shared[0][k * n : (k + 1) * n, :].astype(F32)
+        for j in range(1, ZH):
+            first = (k + j) % ZH * n
+            gathered += shared[j][first : first + n, :].astype(F32)
+        beside = shared[-k % ZH]
+        degree = beside[(ZH + 1) * n :, :].astype(F32)[:1]
+        root = lax.rsqrt(jnp.broadcast_to(degree, (wide, n)).T)
+        preact = root * gathered + bias_ref[...]
+        sigmoid_value = jax.nn.sigmoid(preact)
+        slope_value = sigmoid_value * (1.0 + preact * (1.0 - sigmoid_value))
+        cotangents = beside[ZH * n : (ZH + 1) * n, :].astype(F32)
+        upstream = (cotangents * slope_value * root).astype(BF)
+        if k == 0:
+            activations_ref[...] = (preact * sigmoid_value).astype(BF)
+            upstream_ref[...] = upstream
+        for y in range(Y):
+            copies_ref[y, k] = upstream
 
 
 SMEM = pl.BlockSpec(memory_space=pltpu.SMEM)
@@ -68,6 +104,16 @@
     )(*args)
 
 
+def call_small(kernel, outs, *args):
+    return pl.pallas_call(
+        kernel,
+        out_shape=tuple(jax.ShapeDtypeStruct(s, BF) for s in outs),
+        in_specs=[VMEM] * len(args),
+        out_specs=tuple(VMEM for _ in outs),
+        compiler_params=pltpu.CompilerParams(vmem_limit_bytes=24 * 1024 * 1024),
+    )(*args)
+
+
 def shift(n, k):
     return [(i, (i + k) % n) for i in range(n)]
 
@@ -80,9 +126,9 @@
     return swap(jnp.broadcast_to(value[None], (size,) + value.shape), axis)
 
 
-def collect(pieces, axis, step):
+def collect(pieces, axis):
     size = len(pieces)
-    moved = [lax.ppermute(pieces[k], axis, shift(size, step * k)) for k in range(1, size)]
+    moved = [lax.ppermute(pieces[k], axis, shift(size, -k)) for k in range(1, size)]
     return sum((piece.astype(F32) for piece in moved), pieces[0].astype(F32))
 
 
@@ -123,16 +169,15 @@
         )
         return out
 
-    def middle(partial, part, cotangent, after):
-        along_y = total(swap(partial, "y")).astype(BF)
-        own_rows = collect([along_y[k] for k in range(ZH)], "zh", 1)
-        own_rows, _ = lax.optimization_barrier((own_rows, after))
-        preact = inv_root * (own_rows + scaled[:, part].astype(F32)) + bias_term[None, part]
-        sigmoid_value = jax.nn.sigmoid(preact)
-        activations = (preact * sigmoid_value).astype(BF)
-        slope_value = sigmoid_value * (1.0 + preact * (1.0 - sigmoid_value))
-        upstream = (cotangent[:, part].astype(F32) * slope_value * inv_root).astype(BF)
-        return activations, upstream, jnp.stack(share(upstream, "zh", ZH))
+    degree_rows = jnp.pad(degrees.astype(BF)[None], ((0, 15), (0, 0)))
+
+    def middle(partial, part, after):
+        beside, _ = lax.optimization_barrier(((scaled[:, part], cotangent[:, part], degree_rows), after))
+        (mine,) = call_small(pack_kernel, [((ZH + 1) * n + 16, wide)], swap(partial, "y"), *beside)
+        shared = share(mine, "zh", ZH)
+        return call_small(
+            middle_kernel, [(n, wide), (n, wide), (Y, ZH, n, wide)], *shared, bias_term[None, part]
+        )
 
     def backward(ups, at):
         own, others = call(
@@ -147,13 +192,13 @@
     partial_0, along_z[1] = lax.optimization_barrier((partial_0, along_z[1]))
     partial_1 = forward(jnp.concatenate(share(along_z[1], "x", X), 0), moving)
 
-    activations_0, upstream_0, along_0 = middle(partial_0, parts[0], cotangent, ())
-    activations_1, upstream_1, along_1 = middle(partial_1, parts[1], cotangent, upstream_0)
-
-    ups_0, along_1 = lax.optimization_barrier((spread(along_0, "y", Y), along_1))
-    ups_1 = spread(along_1, "y", Y)
+    activations_0, upstream_0, along_0 = middle(partial_0, parts[0], ())
+    activations_1, upstream_1, along_1 = middle(partial_1, parts[1], upstream_0)
+
+    ups_0, along_1 = lax.optimization_barrier((swap(along_0, "y"), along_1))
+    ups_1 = swap(along_1, "y")
     sums = backward(ups_0, moving)
-    back_0 = collect([sums[k] for k in range(X)], "x", -1).astype(BF)
+    back_0 = collect([sums[k] for k in range(X)], "x").astype(BF)
     ups_1, back_0 = lax.optimization_barrier((ups_1, back_0))
     back_1 = total(swap(backward(ups_1, fixed), "x")).astype(BF)
     back = jnp.concatenate([back_0, back_1], 1).reshape(ZL, n, feat)

time: 229 us -> 212 us (0.926)
  the two profiles are of different devices: /device:TPU:2 before, /device:TPU:8 now
where the time goes in v6:
time: 212 us; the launch traced here: 211 us
  starting transfers between devices  80.6 us (38%)
  waiting for transfers between devices  54.9 us (26%)
  blocking collectives  40.6 us (19%)
  Pallas kernels  18.2 us (9%)
  local copies, waits for them, and re-layouts  9.9 us (5%)
  other arithmetic  3.23 us (2%)
    all_to_all x3, blocking collectives, swap(): return lax.all_to_all(value, axis, 0, 0, tiled=True)  40.6 us
    ppermute x7, starting transfers between devices, share(): lax.ppermute(value, axis, shift(size, k))  34 us
    all_to_all x5, starting transfers between devices, swap(): return lax.all_to_all(value, axis, 0, 0, tiled=True)  30 us
    ppermute x7, waiting for transfers between devices, share(): lax.ppermute(value, axis, shift(size, k))  29.6 us
    all_to_all x5, waiting for transfers between devices, swap(): return lax.all_to_all(value, axis, 0, 0, tiled=True)  16.3 us
    pallas_call x4, Pallas kernels, call(): pl.pallas_call(kernel, out_shape=tuple((jax.ShapeDtypeStruct(s, BF) for s...  15.7 us
    unnamed x23, local copies, waits for them, and re-layouts  9.7 us
    ppermute x3, starting transfers between devices, collect(): lax.ppermute(pieces[k], axis, shift(size, -k))  8.97 us
  transfers between devices with their start and end apart: 19, of which 13 were waited for; matrix products, arithmetic and copies ran while one was open for 1% of the time, Pallas kernels for 3%

profile of v6, /device:TPU:8, one launch (start us, length us, event | category | flops | bytes accessed | tf_op | source)
XLA Modules:
  0.0 210.8 jit_solution(15757200622722275519)
XLA Ops:
  0.6 0.0 copy-start
  0.6 0.7 convert_rsqrt_fusion
  1.3 0.2 copy-done
  1.6 1.0 fusion
  2.6 15.9 %all_to_all.40 = bf16[4,128,256]{2,1,0:T(8,128)(2,1)S(1)} all-to-all(bf16[4,128,256]{2,1,0:T(8,128)(2,1)S(1)} %broadcast_in_dim.27), channel_id=1, replica_groups=mesh['zl'=4,'x'=4,'c'=2,'y'=8,'zh'=3] {'zl'}, dimensions={0} | all-to-all | bytes 524288 | tf_op jit(solution)/shard_map/all_to_all | solution.py:122
  18.6 0.1 broadcast_in_dim.29
  18.6 12.2 %all_to_all.41 = bf16[4,512,128]{2,1,0:T(8,128)(2,1)S(1)} all-to-all(bf16[4,512,128]{2,1,0:T(8,128)(2,1)S(1)} %broadcast_in_dim.29), channel_id=1, replica_groups=mesh['zl'=4,'x'=4,'c'=2,'y'=8,'zh'=3] {'x'}, dimensions={0} | all-to-all | bytes 1048576 | tf_op jit(solution)/shard_map/all_to_all | solution.py:122
  30.8 1.9 collective-permute-start
  33.4 0.7 add_add_fusion
  34.1 0.5 collective-permute-done.far_ref
  34.6 2.2 %copy-done.1 = bf16[1,1,128,128,128]{4,3,2,1,0:T(8,128)(2,1)S(1)} copy-done((bf16[1,1,128,128,128]{4,3,2,1,0:T(8,128)(2,1)S(1)}, bf16[1,1,128,128,128]{4,3,2,1,0:T(8,128)(2,1)}, u32[]{:S(2)}) %copy-start.1) | copy-done | bytes 4194328
  36.8 0.7 copy-done.5
  37.5 4.3 %shard_map.104 = bf16[8,3,128,128]{3,2,1,0:T(8,128)(2,1)} custom-call(s32[1]{0:T(128)} %bitcast.47.count_ref, s32[128]{0:T(128)S(1)} %get-tuple-element.46.pick_ref.place_ref, s32[128]{0:T(128)S(1)} %bitcast.57, s32[1]{0:T(128)} %bitcast.3.zh_ref, bf16[128,128,128]{2,1,0:T(8,128)(2,1)S(1)} %bitcast.51, bf16[2048,128]{1,0:T(8,128)(2,1)S(1)} %bitcast.56, ...), custom_call_target="tpu_custom_call" | custom-call | tf_op jit(solution)/shard_map/pallas_call | solution.py:97
  41.7 6.8 %all-to-all-start.2 = ((bf16[8,3,128,128]{3,2,1,0:T(8,128)(2,1)}), bf16[8,3,128,128]{3,2,1,0:T(8,128)(2,1)S(1)}, u32[]{:S(2)}, u32[]{:S(2)}) async-start(bf16[8,3,128,128]{3,2,1,0:T(8,128)(2,1)} %shard_map.104), calls=%async_computation.2 | async-start | bytes 1572864 | tf_op jit(solution)/shard_map/all_to_all | solution.py:122
  48.5 3.2 %collective-permute-start.3 = (bf16[512,128]{1,0:T(8,128)(2,1)S(1)}, bf16[512,128]{1,0:T(8,128)(2,1)S(1)}, u32[]{:S(2)}, u32[]{:S(2)}) collective-permute-start(bf16[512,128]{1,0:T(8,128)(2,1)S(1)} %bitcast.63), channel_id=1, source_target_pairs={{0,48},{48,96},{96,144},{144,0},{1,49},{49,97},{97,145},{145,1},{2... | collective-permute-start | bytes 393224 | tf_op jit(solution)/shard_map/ppermute | solution.py:136
  51.8 2.7 %collective-permute-start.4 = (bf16[512,128]{1,0:T(8,128)(2,1)S(1)}, bf16[512,128]{1,0:T(8,128)(2,1)S(1)}, u32[]{:S(2)}, u32[]{:S(2)}) collective-permute-start(bf16[512,128]{1,0:T(8,128)(2,1)S(1)} %bitcast.64), channel_id=1, source_target_pairs={{0,96},{48,144},{96,0},{144,48},{1,97},{49,145},{97,1},{145,49},{2... | collective-permute-start | bytes 393224 | tf_op jit(solution)/shard_map/ppermute | solution.py:136
  54.5 0.0 copy-start.9
  54.5 3.8 %collective-permute-start.5 = (bf16[512,128]{1,0:T(8,128)(2,1)S(1)}, bf16[512,128]{1,0:T(8,128)(2,1)S(1)}, u32[]{:S(2)}, u32[]{:S(2)}) collective-permute-start(bf16[512,128]{1,0:T(8,128)(2,1)S(1)} %bitcast.66), channel_id=1, source_target_pairs={{0,144},{48,0},{96,48},{144,96},{1,145},{49,1},{97,49},{145,97},{2... | collective-permute-start | bytes 393224 | tf_op jit(solution)/shard_map/ppermute | solution.py:136
  58.3 0.0 copy-start.7
  58.3 1.8 collective-permute-done.4
  60.1 2.0 collective-permute-done.5
  62.2 1.9 collective-permute-start.6
  64.1 1.9 collective-permute-done.6.far_ref
  66.0 2.2 %copy-done.2 = bf16[1,1,128,128,128]{4,3,2,1,0:T(8,128)(2,1)S(1)} copy-done((bf16[1,1,128,128,128]{4,3,2,1,0:T(8,128)(2,1)S(1)}, bf16[1,1,128,128,128]{4,3,2,1,0:T(8,128)(2,1)}, u32[]{:S(2)}) %copy-start.2) | copy-done | bytes 4194328
  68.2 4.2 %shard_map.107 = bf16[8,3,128,128]{3,2,1,0:T(8,128)(2,1)} custom-call(s32[1]{0:T(128)} %bitcast.48.count_ref, s32[128]{0:T(128)S(1)} %fusion.7.pick_ref.place_ref, s32[128]{0:T(128)S(1)} %bitcast.58, s32[1]{0:T(128)} %bitcast.3.zh_ref, bf16[128,128,128]{2,1,0:T(8,128)(2,1)S(1)} %bitcast.52, bf16[2048,128]{1,0:T(8,128)(2,1)S(1)} %constant_dynamic-update-slice_fusion.near_ref, ...), custom_call_target="tpu_custom_call" | custom-call | tf_op jit(solution)/shard_map/pallas_call | solution.py:97
  72.3 0.0 all-to-all-done.2.along_y_ref
  72.3 6.3 %all-to-all-start.3 = ((bf16[8,3,128,128]{3,2,1,0:T(8,128)(2,1)}), bf16[8,3,128,128]{3,2,1,0:T(8,128)(2,1)S(1)}, u32[]{:S(2)}, u32[]{:S(2)}) async-start(bf16[8,3,128,128]{3,2,1,0:T(8,128)(2,1)} %shard_map.107), calls=%async_computation.3 | async-start | bytes 1572864 | tf_op jit(solution)/shard_map/all_to_all | solution.py:122
  78.7 0.1 shard_map.105.own_ref
  78.8 10.6 %collective-permute-start.1 = (bf16[528,128]{1,0:T(8,128)(2,1)S(1)}, bf16[528,128]{1,0:T(8,128)(2,1)S(1)}, u32[]{:S(2)}, u32[]{:S(2)}) collective-permute-start(bf16[528,128]{1,0:T(8,128)(2,1)S(1)} %shard_map.105.own_ref), channel_id=1, source_target_pairs={{0,1},{1,2},{2,0},{3,4},{4,5},{5,3},{6,7},{7,8},{8,6},{9,10},{10,1... | collective-permute-start | bytes 405512 | tf_op jit(solution)/shard_map/ppermute | solution.py:136
  89.4 3.2 %collective-permute-start.2 = (bf16[528,128]{1,0:T(8,128)(2,1)S(1)}, bf16[528,128]{1,0:T(8,128)(2,1)S(1)}, u32[]{:S(2)}, u32[]{:S(2)}) collective-permute-start(bf16[528,128]{1,0:T(8,128)(2,1)S(1)} %shard_map.105.own_ref), channel_id=1, source_target_pairs={{0,2},{1,0},{2,1},{3,5},{4,3},{5,4},{6,8},{7,6},{8,7},{9,11},{10,9... | collective-permute-start | bytes 405512 | tf_op jit(solution)/shard_map/ppermute | solution.py:136
  92.6 1.2 collective-permute-done.1.back_1_ref
  93.9 11.5 %collective-permute-done.2.back_2_ref = bf16[528,128]{1,0:T(8,128)(2,1)S(1)} collective-permute-done((bf16[528,128]{1,0:T(8,128)(2,1)S(1)}, bf16[528,128]{1,0:T(8,128)(2,1)S(1)}, u32[]{:S(2)}, u32[]{:S(2)}) %collective-permute-start.2) | collective-permute-done | bytes 135200 | tf_op jit(solution)/shard_map/ppermute | solution.py:136
  105.4 1.1 shard_map.106
  106.5 7.2 %all-to-all-start.4 = ((bf16[8,3,128,128]{3,2,1,0:T(8,128)(2,1)}), bf16[8,3,128,128]{3,2,1,0:T(8,128)(2,1)S(1)}, u32[]{:S(2)}, u32[]{:S(2)}) async-start(bf16[8,3,128,128]{3,2,1,0:T(8,128)(2,1)} %get-tuple-element.35), calls=%async_computation.4 | async-start | bytes 1572864 | tf_op jit(solution)/shard_map/all_to_all | solution.py:122
  113.7 0.1 shard_map.108.own_ref
  113.8 8.6 %collective-permute-start.7 = (bf16[528,128]{1,0:T(8,128)(2,1)S(1)}, bf16[528,128]{1,0:T(8,128)(2,1)S(1)}, u32[]{:S(2)}, u32[]{:S(2)}) collective-permute-start(bf16[528,128]{1,0:T(8,128)(2,1)S(1)} %shard_map.108.own_ref), channel_id=1, source_target_pairs={{0,1},{1,2},{2,0},{3,4},{4,5},{5,3},{6,7},{7,8},{8,6},{9,10},{10,1... | collective-permute-start | bytes 405512 | tf_op jit(solution)/shard_map/ppermute | solution.py:136
  122.4 1.9 collective-permute-start.8
  124.3 4.5 %collective-permute-done.7.back_1_ref = bf16[528,128]{1,0:T(8,128)(2,1)S(1)} collective-permute-done((bf16[528,128]{1,0:T(8,128)(2,1)S(1)}, bf16[528,128]{1,0:T(8,128)(2,1)S(1)}, u32[]{:S(2)}, u32[]{:S(2)}) %collective-permute-start.7) | collective-permute-done | bytes 135200 | tf_op jit(solution)/shard_map/ppermute | solution.py:136
  128.8 8.5 %collective-permute-done.8.back_2_ref = bf16[528,128]{1,0:T(8,128)(2,1)S(1)} collective-permute-done((bf16[528,128]{1,0:T(8,128)(2,1)S(1)}, bf16[528,128]{1,0:T(8,128)(2,1)S(1)}, u32[]{:S(2)}, u32[]{:S(2)}) %collective-permute-start.8) | collective-permute-done | bytes 135200 | tf_op jit(solution)/shard_map/ppermute | solution.py:136
  137.4 1.1 shard_map.109
  138.5 2.2 %copy-done.3 = bf16[1,1,128,128,128]{4,3,2,1,0:T(8,128)(2,1)S(1)} copy-done((bf16[1,1,128,128,128]{4,3,2,1,0:T(8,128)(2,1)S(1)}, bf16[1,1,128,128,128]{4,3,2,1,0:T(8,128)(2,1)}, u32[]{:S(2)}) %copy-start.3) | copy-done | bytes 4194328
  140.7 3.6 %shard_map.110 = (bf16[2048,128]{1,0:T(8,128)(2,1)S(1)}, bf16[2048,128]{1,0:T(8,128)(2,1)S(1)}) custom-call(s32[1]{0:T(128)} %bitcast.49.count_ref, s32[128]{0:T(128)S(1)} %bitcast.59, s32[128]{0:T(128)S(1)} %fusion.7.pick_ref.place_ref, s32[1]{0:T(128)} %bitcast.3.zh_ref, bf16[128,128,128]{2,1,0:T(8,128)(2,1)S(1)} %bitcast.53, ...), custom_call_target="tpu_custom_call" | custom-call | tf_op jit(solution)/shard_map/pallas_call | solution.py:97
  144.3 1.9 collective-permute-start.9
  146.2 6.3 %all-to-all-start.5 = ((bf16[8,3,128,128]{3,2,1,0:T(8,128)(2,1)}), bf16[8,3,128,128]{3,2,1,0:T(8,128)(2,1)S(1)}, u32[]{:S(2)}, u32[]{:S(2)}) async-start(bf16[8,3,128,128]{3,2,1,0:T(8,128)(2,1)} %get-tuple-element.37), calls=%async_computation.5 | async-start | bytes 1572864 | tf_op jit(solution)/shard_map/all_to_all | solution.py:122
  152.6 0.1 add_convert_fusion.1
  152.7 1.9 collective-permute-start.12
  154.7 1.9 collective-permute-start.11
  156.6 5.1 %collective-permute-start.10 = (bf16[512,128]{1,0:T(8,128)(2,1)S(1)}, bf16[512,128]{1,0:T(8,128)(2,1)S(1)}, u32[]{:S(2)}, u32[]{:S(2)}) collective-permute-start(bf16[512,128]{1,0:T(8,128)(2,1)S(1)} %get-tuple-element.50), channel_id=1, source_target_pairs={{0,144},{48,0},{96,48},{144,96},{1,145},{49,1},{97,49},{145,97},{2... | collective-permute-start | bytes 393224 | tf_op jit(solution)/shard_map/ppermute | solution.py:131
  161.7 2.3 %collective-permute-done.12 = bf16[512,128]{1,0:T(8,128)(2,1)S(1)} collective-permute-done((bf16[512,128]{1,0:T(8,128)(2,1)S(1)}, bf16[512,128]{1,0:T(8,128)(2,1)S(1)}, u32[]{:S(2)}, u32[]{:S(2)}) %collective-permute-start.12) | collective-permute-done | bytes 131104 | tf_op jit(solution)/shard_map/ppermute | solution.py:131
  164.0 2.5 %collective-permute-done.10 = bf16[512,128]{1,0:T(8,128)(2,1)S(1)} collective-permute-done((bf16[512,128]{1,0:T(8,128)(2,1)S(1)}, bf16[512,128]{1,0:T(8,128)(2,1)S(1)}, u32[]{:S(2)}, u32[]{:S(2)}) %collective-permute-start.10) | collective-permute-done | bytes 131104 | tf_op jit(solution)/shard_map/ppermute | solution.py:131
  166.5 0.1 add_convert_fusion.2
  166.6 8.3 %all-to-all-done.5.ups_ref = bf16[8,3,128,128]{3,2,1,0:T(8,128)(2,1)S(1)} async-done(((bf16[8,3,128,128]{3,2,1,0:T(8,128)(2,1)}), bf16[8,3,128,128]{3,2,1,0:T(8,128)(2,1)S(1)}, u32[]{:S(2)}, u32[]{:S(2)}) %all-to-all-start.5) | async-done | bytes 786464 | tf_op jit(solution)/shard_map/all_to_all | solution.py:122
  174.9 2.2 %copy-done.4 = bf16[1,1,128,128,128]{4,3,2,1,0:T(8,128)(2,1)S(1)} copy-done((bf16[1,1,128,128,128]{4,3,2,1,0:T(8,128)(2,1)S(1)}, bf16[1,1,128,128,128]{4,3,2,1,0:T(8,128)(2,1)}, u32[]{:S(2)}) %copy-start.4) | copy-done | bytes 4194328
  177.1 3.6 %shard_map.111 = (bf16[2048,128]{1,0:T(8,128)(2,1)S(1)}, bf16[2048,128]{1,0:T(8,128)(2,1)S(1)}) custom-call(s32[1]{0:T(128)} %bitcast.50.count_ref, s32[128]{0:T(128)S(1)} %bitcast.60, s32[128]{0:T(128)S(1)} %get-tuple-element.46.pick_ref.place_ref, s32[1]{0:T(128)} %bitcast.3.zh_ref, bf16[128,128,128]{2,1,0:T(8,128)(2,1)S(1)} %bitcast.54, ...), custom_call_target="tpu_custom_call" | custom-call | tf_op jit(solution)/shard_map/pallas_call | solution.py:97
  180.7 1.9 collective-permute-start.13
  182.6 1.9 collective-permute-done.13
  184.5 0.1 add_convert_fusion
  184.7 12.5 %all_to_all.42 = bf16[4,512,128]{2,1,0:T(8,128)(2,1)S(1)} all-to-all(bf16[4,512,128]{2,1,0:T(8,128)(2,1)S(1)} %bitcast.61), channel_id=1, replica_groups=mesh['zl'=4,'x'=4,'c'=2,'y'=8,'zh'=3] {'x'}, dimensions={0} | all-to-all | bytes 1048576 | tf_op jit(solution)/shard_map/all_to_all | solution.py:122
  197.1 0.1 reduce_sum.21
  197.2 0.7 pad_maximum_fusion
  197.9 3.4 %all-to-all-start.7 = ((bf16[4,128,256]{2,1,0:T(8,128)(2,1)}), bf16[4,128,256]{2,1,0:T(8,128)(2,1)S(1)}, u32[]{:S(2)}, u32[]{:S(2)}) async-start(bf16[4,128,256]{2,1,0:T(8,128)(2,1)} %bitcast.12), calls=%async_computation.7 | async-start | bytes 524288 | tf_op jit(solution)/shard_map/all_to_all | solution.py:122
  201.3 0.6 pad_maximum_fusion.1
  202.0 8.0 %all-to-all-done.7 = bf16[4,128,256]{2,1,0:T(8,128)(2,1)S(1)} async-done(((bf16[4,128,256]{2,1,0:T(8,128)(2,1)}), bf16[4,128,256]{2,1,0:T(8,128)(2,1)S(1)}, u32[]{:S(2)}, u32[]{:S(2)}) %all-to-all-start.7) | async-done | bytes 262176 | tf_op jit(solution)/shard_map/all_to_all | solution.py:122
  210.0 0.8 convolution_convert_fusion
  (30 shorter events, 0.3 us)
Async XLA Ops:
  0.6 0.9 copy-start
  30.8 3.8 %collective-permute-start = (bf16[2048,128]{1,0:T(8,128)(2,1)S(1)}, bf16[2048,128]{1,0:T(8,128)(2,1)S(1)}, u32[]{:S(2)}, u32[]{:S(2)}) collective-permute-start(bf16[2048,128]{1,0:T(8,128)(2,1)S(1)} %bitcast.55), channel_id=1, source_target_pairs={{0,24},{24,0},{1,25},{25,1},{2,26},{26,2},{3,27},{27,3},{4,28},{28... | collective-permute-start | bytes 1572872 | tf_op jit(solution)/shard_map/ppermute | solution.py:165
  34.6 2.2 %copy-start.1 = (bf16[1,1,128,128,128]{4,3,2,1,0:T(8,128)(2,1)S(1)}, bf16[1,1,128,128,128]{4,3,2,1,0:T(8,128)(2,1)}, u32[]{:S(2)}) copy-start(bf16[1,1,128,128,128]{4,3,2,1,0:T(8,128)(2,1)} %param.13) | copy-start | bytes 12582916
  36.8 0.7 copy-start.5
  37.5 28.5 %copy-start.6 = (s32[1,1,128]{2,1,0:T(1,128)S(1)}, s32[1,1,128]{2,1,0:T(1,128)}, u32[]{:S(2)}) copy-start(s32[1,1,128]{2,1,0:T(1,128)} %param.14) | copy-start | bytes 1540
  41.7 30.6 %all-to-all-start.2 = ((bf16[8,3,128,128]{3,2,1,0:T(8,128)(2,1)}), bf16[8,3,128,128]{3,2,1,0:T(8,128)(2,1)S(1)}, u32[]{:S(2)}, u32[]{:S(2)}) async-start(bf16[8,3,128,128]{3,2,1,0:T(8,128)(2,1)} %shard_map.104), calls=%async_computation.2 | async-start | bytes 1572864 | tf_op jit(solution)/shard_map/all_to_all | solution.py:122
  48.5 9.8 %collective-permute-start.3 = (bf16[512,128]{1,0:T(8,128)(2,1)S(1)}, bf16[512,128]{1,0:T(8,128)(2,1)S(1)}, u32[]{:S(2)}, u32[]{:S(2)}) collective-permute-start(bf16[512,128]{1,0:T(8,128)(2,1)S(1)} %bitcast.63), channel_id=1, source_target_pairs={{0,48},{48,96},{96,144},{144,0},{1,49},{49,97},{97,145},{145,1},{2... | collective-permute-start | bytes 393224 | tf_op jit(solution)/shard_map/ppermute | solution.py:136
  51.8 8.4 %collective-permute-start.4 = (bf16[512,128]{1,0:T(8,128)(2,1)S(1)}, bf16[512,128]{1,0:T(8,128)(2,1)S(1)}, u32[]{:S(2)}, u32[]{:S(2)}) collective-permute-start(bf16[512,128]{1,0:T(8,128)(2,1)S(1)} %bitcast.64), channel_id=1, source_target_pairs={{0,96},{48,144},{96,0},{144,48},{1,97},{49,145},{97,1},{145,49},{2... | collective-permute-start | bytes 393224 | tf_op jit(solution)/shard_map/ppermute | solution.py:136
  54.5 24.1 %copy-start.9 = (s32[128]{0:T(128)S(1)}, s32[128]{0:T(128)}, u32[]{:S(2)}) copy-start(s32[128]{0:T(128)} %param.10) | copy-start | bytes 1540
  54.5 7.7 %collective-permute-start.5 = (bf16[512,128]{1,0:T(8,128)(2,1)S(1)}, bf16[512,128]{1,0:T(8,128)(2,1)S(1)}, u32[]{:S(2)}, u32[]{:S(2)}) collective-permute-start(bf16[512,128]{1,0:T(8,128)(2,1)S(1)} %bitcast.66), channel_id=1, source_target_pairs={{0,144},{48,0},{96,48},{144,96},{1,145},{49,1},{97,49},{145,97},{2... | collective-permute-start | bytes 393224 | tf_op jit(solution)/shard_map/ppermute | solution.py:136
  58.3 20.3 %copy-start.7 = (bf16[128,256]{1,0:T(8,128)(2,1)S(1)}, bf16[128,256]{1,0:T(8,128)(2,1)}, u32[]{:S(2)}) copy-start(bf16[128,256]{1,0:T(8,128)(2,1)} %param.17) | copy-start | bytes 196612
  62.2 3.8 %collective-permute-start.6 = (bf16[2048,128]{1,0:T(8,128)(2,1)S(1)}, bf16[2048,128]{1,0:T(8,128)(2,1)S(1)}, u32[]{:S(2)}, u32[]{:S(2)}) collective-permute-start(bf16[2048,128]{1,0:T(8,128)(2,1)S(1)} %constant_dynamic-update-slice_fusion.near_ref), channel_id=1, source_target_pairs={{0,24},{24,0},{1,25},{25,1},{2,26},{26,2},{3,27},{27,3},{4,28},{28... | collective-permute-start | bytes 1572872 | tf_op jit(solution)/shard_map/ppermute | solution.py:165
  66.0 2.2 %copy-start.2 = (bf16[1,1,128,128,128]{4,3,2,1,0:T(8,128)(2,1)S(1)}, bf16[1,1,128,128,128]{4,3,2,1,0:T(8,128)(2,1)}, u32[]{:S(2)}) copy-start(bf16[1,1,128,128,128]{4,3,2,1,0:T(8,128)(2,1)} %param.13) | copy-start | bytes 12582916
  68.2 24.4 %copy-start.8 = (f32[256]{0:T(256)S(1)}, f32[256]{0:T(256)}, u32[]{:S(2)}) copy-start(f32[256]{0:T(256)} %param.12) | copy-start | bytes 3076
  72.3 34.2 %all-to-all-start.3 = ((bf16[8,3,128,128]{3,2,1,0:T(8,128)(2,1)}), bf16[8,3,128,128]{3,2,1,0:T(8,128)(2,1)S(1)}, u32[]{:S(2)}, u32[]{:S(2)}) async-start(bf16[8,3,128,128]{3,2,1,0:T(8,128)(2,1)} %shard_map.107), calls=%async_computation.3 | async-start | bytes 1572864 | tf_op jit(solution)/shard_map/all_to_all | solution.py:122
  78.8 15.1 %collective-permute-start.1 = (bf16[528,128]{1,0:T(8,128)(2,1)S(1)}, bf16[528,128]{1,0:T(8,128)(2,1)S(1)}, u32[]{:S(2)}, u32[]{:S(2)}) collective-permute-start(bf16[528,128]{1,0:T(8,128)(2,1)S(1)} %shard_map.105.own_ref), channel_id=1, source_target_pairs={{0,1},{1,2},{2,0},{3,4},{4,5},{5,3},{6,7},{7,8},{8,6},{9,10},{10,1... | collective-permute-start | bytes 405512 | tf_op jit(solution)/shard_map/ppermute | solution.py:136
  89.4 16.0 %collective-permute-start.2 = (bf16[528,128]{1,0:T(8,128)(2,1)S(1)}, bf16[528,128]{1,0:T(8,128)(2,1)S(1)}, u32[]{:S(2)}, u32[]{:S(2)}) collective-permute-start(bf16[528,128]{1,0:T(8,128)(2,1)S(1)} %shard_map.105.own_ref), channel_id=1, source_target_pairs={{0,2},{1,0},{2,1},{3,5},{4,3},{5,4},{6,8},{7,6},{8,7},{9,11},{10,9... | collective-permute-start | bytes 405512 | tf_op jit(solution)/shard_map/ppermute | solution.py:136
  106.5 31.9 %all-to-all-start.4 = ((bf16[8,3,128,128]{3,2,1,0:T(8,128)(2,1)}), bf16[8,3,128,128]{3,2,1,0:T(8,128)(2,1)S(1)}, u32[]{:S(2)}, u32[]{:S(2)}) async-start(bf16[8,3,128,128]{3,2,1,0:T(8,128)(2,1)} %get-tuple-element.35), calls=%async_computation.4 | async-start | bytes 1572864 | tf_op jit(solution)/shard_map/all_to_all | solution.py:122
  113.8 15.0 %collective-permute-start.7 = (bf16[528,128]{1,0:T(8,128)(2,1)S(1)}, bf16[528,128]{1,0:T(8,128)(2,1)S(1)}, u32[]{:S(2)}, u32[]{:S(2)}) collective-permute-start(bf16[528,128]{1,0:T(8,128)(2,1)S(1)} %shard_map.108.own_ref), channel_id=1, source_target_pairs={{0,1},{1,2},{2,0},{3,4},{4,5},{5,3},{6,7},{7,8},{8,6},{9,10},{10,1... | collective-permute-start | bytes 405512 | tf_op jit(solution)/shard_map/ppermute | solution.py:136
  122.4 15.0 %collective-permute-start.8 = (bf16[528,128]{1,0:T(8,128)(2,1)S(1)}, bf16[528,128]{1,0:T(8,128)(2,1)S(1)}, u32[]{:S(2)}, u32[]{:S(2)}) collective-permute-start(bf16[528,128]{1,0:T(8,128)(2,1)S(1)} %shard_map.108.own_ref), channel_id=1, source_target_pairs={{0,2},{1,0},{2,1},{3,5},{4,3},{5,4},{6,8},{7,6},{8,7},{9,11},{10,9... | collective-permute-start | bytes 405512 | tf_op jit(solution)/shard_map/ppermute | solution.py:136
  138.5 2.2 %copy-start.3 = (bf16[1,1,128,128,128]{4,3,2,1,0:T(8,128)(2,1)S(1)}, bf16[1,1,128,128,128]{4,3,2,1,0:T(8,128)(2,1)}, u32[]{:S(2)}) copy-start(bf16[1,1,128,128,128]{4,3,2,1,0:T(8,128)(2,1)} %param.13) | copy-start | bytes 12582916
  144.3 8.2 %collective-permute-start.9 = (bf16[2048,128]{1,0:T(8,128)(2,1)S(1)}, bf16[2048,128]{1,0:T(8,128)(2,1)S(1)}, u32[]{:S(2)}, u32[]{:S(2)}) collective-permute-start(bf16[2048,128]{1,0:T(8,128)(2,1)S(1)} %get-tuple-element.40), channel_id=1, source_target_pairs={{0,24},{24,0},{1,25},{25,1},{2,26},{26,2},{3,27},{27,3},{4,28},{28... | collective-permute-start | bytes 1572872 | tf_op jit(solution)/shard_map/ppermute | solution.py:186
  146.2 28.6 %all-to-all-start.5 = ((bf16[8,3,128,128]{3,2,1,0:T(8,128)(2,1)}), bf16[8,3,128,128]{3,2,1,0:T(8,128)(2,1)S(1)}, u32[]{:S(2)}, u32[]{:S(2)}) async-start(bf16[8,3,128,128]{3,2,1,0:T(8,128)(2,1)} %get-tuple-element.37), calls=%async_computation.5 | async-start | bytes 1572864 | tf_op jit(solution)/shard_map/all_to_all | solution.py:122
  152.7 11.3 %collective-permute-start.12 = (bf16[512,128]{1,0:T(8,128)(2,1)S(1)}, bf16[512,128]{1,0:T(8,128)(2,1)S(1)}, u32[]{:S(2)}, u32[]{:S(2)}) collective-permute-start(bf16[512,128]{1,0:T(8,128)(2,1)S(1)} %get-tuple-element.51), channel_id=1, source_target_pairs={{0,48},{48,96},{96,144},{144,0},{1,49},{49,97},{97,145},{145,1},{2... | collective-permute-start | bytes 393224 | tf_op jit(solution)/shard_map/ppermute | solution.py:131
  154.7 9.3 %collective-permute-start.11 = (bf16[512,128]{1,0:T(8,128)(2,1)S(1)}, bf16[512,128]{1,0:T(8,128)(2,1)S(1)}, u32[]{:S(2)}, u32[]{:S(2)}) collective-permute-start(bf16[512,128]{1,0:T(8,128)(2,1)S(1)} %get-tuple-element.52), channel_id=1, source_target_pairs={{0,96},{48,144},{96,0},{144,48},{1,97},{49,145},{97,1},{145,49},{2... | collective-permute-start | bytes 393224 | tf_op jit(solution)/shard_map/ppermute | solution.py:131
  156.6 9.9 %collective-permute-start.10 = (bf16[512,128]{1,0:T(8,128)(2,1)S(1)}, bf16[512,128]{1,0:T(8,128)(2,1)S(1)}, u32[]{:S(2)}, u32[]{:S(2)}) collective-permute-start(bf16[512,128]{1,0:T(8,128)(2,1)S(1)} %get-tuple-element.50), channel_id=1, source_target_pairs={{0,144},{48,0},{96,48},{144,96},{1,145},{49,1},{97,49},{145,97},{2... | collective-permute-start | bytes 393224 | tf_op jit(solution)/shard_map/ppermute | solution.py:131
  174.9 2.2 %copy-start.4 = (bf16[1,1,128,128,128]{4,3,2,1,0:T(8,128)(2,1)S(1)}, bf16[1,1,128,128,128]{4,3,2,1,0:T(8,128)(2,1)}, u32[]{:S(2)}) copy-start(bf16[1,1,128,128,128]{4,3,2,1,0:T(8,128)(2,1)} %param.13) | copy-start | bytes 12582916
  180.7 3.8 %collective-permute-start.13 = (bf16[2048,128]{1,0:T(8,128)(2,1)S(1)}, bf16[2048,128]{1,0:T(8,128)(2,1)S(1)}, u32[]{:S(2)}, u32[]{:S(2)}) collective-permute-start(bf16[2048,128]{1,0:T(8,128)(2,1)S(1)} %get-tuple-element.44), channel_id=1, source_target_pairs={{0,24},{24,0},{1,25},{25,1},{2,26},{26,2},{3,27},{27,3},{4,28},{28... | collective-permute-start | bytes 1572872 | tf_op jit(solution)/shard_map/ppermute | solution.py:186
  197.9 12.0 %all-to-all-start.7 = ((bf16[4,128,256]{2,1,0:T(8,128)(2,1)}), bf16[4,128,256]{2,1,0:T(8,128)(2,1)S(1)}, u32[]{:S(2)}, u32[]{:S(2)}) async-start(bf16[4,128,256]{2,1,0:T(8,128)(2,1)} %bitcast.12), calls=%async_computation.7 | async-start | bytes 524288 | tf_op jit(solution)/shard_map/all_to_all | solution.py:122

commit v7 on v6

v7 whole, which is shorter than its diff:
```python
import functools

import jax
import jax.numpy as jnp
from jax import lax
from jax.experimental import pallas as pl
from jax.experimental.pallas import tpu as pltpu
from jax.sharding import Mesh
from jax.sharding import PartitionSpec as P

ZL, X, C, Y, ZH = 4, 4, 2, 8, 3
BF, F32 = jnp.bfloat16, jnp.float32
NODE_AXES = ("zl", "x", "c", "y", "zh")
UNROLL = 16


def accumulate(count_ref, pick_ref, place_ref, tiles_ref, src, acc, transposed):
    edge = tiles_ref.shape[-1]
    dims = (((0,), (0,)), ((), ())) if transposed else (((1,), (0,)), ((), ()))
    acc[...] = jnp.zeros_like(acc)

    def step(s, carry):
        for u in range(UNROLL):
            t = s * UNROLL + u
            block = src[pl.ds(pl.multiple_of(pick_ref[t] * edge, edge), edge), :]
            product = lax.dot_general(tiles_ref[t], block, dims, preferred_element_type=F32)
            acc[pl.ds(pl.multiple_of(place_ref[t] * edge, edge), edge), :] += product
        return carry

    lax.fori_loop(0, count_ref[0] // UNROLL, step, 0)


def forward_kernel(
    count_ref, pick_ref, place_ref, zh_ref, tiles_ref, near_ref, far_ref, out_0, out_1, src, acc
):
    half = near_ref.shape[0]
    edge = tiles_ref.shape[-1]
    wide = out_0.shape[-1]
    src[:half] = near_ref[...]
    src[half:] = far_ref[...]
    accumulate(count_ref, pick_ref, place_ref, tiles_ref, src, acc, False)
    for y in range(Y):
        for k in range(ZH):
            base = pl.multiple_of((y * ZH + (zh_ref[0] + k) % ZH) * edge, edge)
            out_0[y, k] = acc[pl.ds(base, edge), :wide].astype(BF)
            out_1[y, k] = acc[pl.ds(base, edge), wide:].astype(BF)


def backward_kernel(
    count_ref, pick_ref, place_ref, zh_ref, tiles_ref, ups_0, ups_1, near_ref, far_ref, src, acc
):
    edge = tiles_ref.shape[-1]
    wide = ups_0.shape[-1]
    for y in range(Y):
        for k in range(ZH):
            base = pl.multiple_of((y * ZH + (zh_ref[0] + k) % ZH) * edge, edge)
            src[pl.ds(base, edge), :wide] = ups_0[y, k]
            src[pl.ds(base, edge), wide:] = ups_1[y, k]
    accumulate(count_ref, pick_ref, place_ref, tiles_ref, src, acc, True)
    half = near_ref.shape[0]
    near_ref[...] = acc[:half, :].astype(BF)
    far_ref[...] = acc[half:, :].astype(BF)


def pack_kernel(h, along_y_ref, scaled_ref, out):
    n, wide = scaled_ref.shape[0], out.shape[-1]
    for k in range(ZH):
        summed = along_y_ref[0, k].astype(F32)
        for y in range(1, Y):
            summed += along_y_ref[y, k].astype(F32)
        if k == 0:
            summed += scaled_ref[:, h * wide : (h + 1) * wide].astype(F32)
        out[k * n : (k + 1) * n, :] = summed.astype(BF)


def middle_kernel(
    h, own_ref, back_1_ref, back_2_ref, beside_0, beside_1, beside_2, bias_ref,
    activations_ref, upstream_ref, copies_ref,
):
    shared = (own_ref, back_1_ref, back_2_ref)
    besides = (beside_0, beside_1, beside_2)
    n, wide = activations_ref.shape
    lanes = slice(h * wide, (h + 1) * wide)
    for k in range(ZH):
        gathered = shared[0][k * n : (k + 1) * n, :].astype(F32)
        for j in range(1, ZH):
            first = (k + j) % ZH * n
            gathered += shared[j][first : first + n, :].astype(F32)
        beside = besides[-k % ZH]
        degree = beside[n:, :n].astype(F32)[:1]
        root = lax.rsqrt(jnp.broadcast_to(degree, (wide, n)).T)
        preact = root * gathered + bias_ref[:, lanes]
        sigmoid_value = jax.nn.sigmoid(preact)
        slope_value = sigmoid_value * (1.0 + preact * (1.0 - sigmoid_value))
        cotangents = beside[:n, lanes].astype(F32)
        upstream = (cotangents * slope_value * root).astype(BF)
        if k == 0:
            activations_ref[...] = (preact * sigmoid_value).astype(BF)
            upstream_ref[...] = upstream
        for y in range(Y):
            copies_ref[y, k] = upstream


SMEM = pl.BlockSpec(memory_space=pltpu.SMEM)
VMEM = pl.BlockSpec(memory_space=pltpu.VMEM)


def call(kernel, outs, src_rows, acc_rows, feat, *args):
    return pl.pallas_call(
        kernel,
        out_shape=tuple(jax.ShapeDtypeStruct(s, BF) for s in outs),
        in_specs=[SMEM] * 4 + [VMEM] * (len(args) - 4),
        out_specs=tuple(VMEM for _ in outs),
        scratch_shapes=[pltpu.VMEM((src_rows, feat), BF), pltpu.VMEM((acc_rows, feat), F32)],
        compiler_params=pltpu.CompilerParams(vmem_limit_bytes=24 * 1024 * 1024),
    )(*args)


def call_small(kernel, outs, *args):
    return pl.pallas_call(
        kernel,
        out_shape=tuple(jax.ShapeDtypeStruct(s, BF) for s in outs),
        in_specs=[VMEM] * len(args),
        out_specs=tuple(VMEM for _ in outs),
        compiler_params=pltpu.CompilerParams(vmem_limit_bytes=24 * 1024 * 1024),
    )(*args)


def shift(n, k):
    return [(i, (i + k) % n) for i in range(n)]


def swap(value, axis):
    return lax.all_to_all(value, axis, 0, 0, tiled=True)


def spread(value, axis, size):
    return swap(jnp.broadcast_to(value[None], (size,) + value.shape), axis)


def share(value, axis, size):
    return [value] + [lax.ppermute(value, axis, shift(size, k)) for k in range(1, size)]


def total(value):
    return value.astype(F32).sum(0)


def body(
    features, degrees, weight, bias_term, tile_weights, tile_rows, tile_columns, tile_count, cotangent
):
    tiles = tile_weights[0, 0]
    rows, columns = tile_rows[0, 0], tile_columns[0, 0]
    count = tile_count[0]
    n, feat = features.shape
    wide = feat // 2
    my_zh = lax.axis_index("zh").astype(jnp.int32)[None]
    block_zl, block_x, block_c = columns // (X * C), columns // C % X, columns % C
    other = (block_c != lax.axis_index("c")).astype(jnp.int32)
    column_at = (other * X + block_x) * ZL + block_zl
    sources, targets, chip = C * X * ZL * n, Y * ZH * n, X * ZL * n

    inv_root = lax.rsqrt(degrees.astype(F32))[:, None]
    hidden = jnp.dot(features, weight, preferred_element_type=F32)
    scaled = (hidden * inv_root).astype(BF)

    near = spread(spread(scaled, "zl", ZL), "x", X).reshape(chip, feat)
    far = lax.ppermute(near, "c", shift(C, 1))
    partials = call(
        forward_kernel, [(Y, ZH, n, wide)] * 2, sources, targets, feat,
        count, column_at, rows, my_zh, tiles, near, far,
    )
    degree_rows = jnp.pad(degrees.astype(BF)[None], ((0, 15), (0, feat - n)))
    beside = jnp.concatenate([cotangent, degree_rows], 0)
    partials, beside = lax.optimization_barrier((partials, beside))
    beside = share(beside, "zh", ZH)

    def middle(along_y, h, after):
        along_y, _ = lax.optimization_barrier((along_y, after))
        (mine,) = call_small(functools.partial(pack_kernel, h), [(ZH * n, wide)], along_y, scaled)
        return call_small(
            functools.partial(middle_kernel, h), [(n, wide), (n, wide), (Y, ZH, n, wide)],
            *share(mine, "zh", ZH), *beside, bias_term[None],
        )

    along_y_0 = swap(partials[0], "y")
    along_y_0, partial_1, beside = lax.optimization_barrier((along_y_0, partials[1], beside))
    along_y_1 = swap(partial_1, "y")
    activations_0, upstream_0, along_0 = middle(along_y_0, 0, ())
    activations_1, upstream_1, along_1 = middle(along_y_1, 1, upstream_0)
    ups_0, along_1 = lax.optimization_barrier((swap(along_0, "y"), along_1))
    ups_1 = swap(along_1, "y")

    own, others = call(
        backward_kernel, [(chip, feat)] * 2, targets, sources, feat,
        count, rows, column_at, my_zh, tiles, ups_0, ups_1,
    )
    others = lax.ppermute(others, "c", shift(C, 1))
    back = (own.astype(F32) + others.astype(F32)).astype(BF).reshape(X, ZL * n, feat)
    back = total(swap(back, "x")).astype(BF).reshape(ZL, n, feat)
    own_back = total(swap(back, "zl"))
    upstream = jnp.concatenate([upstream_0, upstream_1], 1)
    grad_hidden = (inv_root * (own_back + upstream.astype(F32))).astype(BF)
    feature_grad = jnp.einsum("nf,gf->ng", grad_hidden, weight, preferred_element_type=F32)
    return jnp.concatenate([activations_0, activations_1], 1), feature_grad.astype(BF)


def solution(mesh):
    fine = Mesh(mesh.devices.reshape(ZL, X, C, Y, ZH), NODE_AXES)
    gr, gc = ("zl", "x", "c"), ("y", "zh")
    nodes = P(NODE_AXES, None)
    return jax.shard_map(
        body,
        mesh=fine,
        in_specs=(
            nodes, P(NODE_AXES), P(), P(), P(gr, gc, None, None, None), P(gr, gc, None), P(gr, gc, None),
            P(gr, gc), nodes,
        ),
        out_specs=(nodes, nodes),
        check_vma=False,
    )
```

time: 212 us -> 209 us (0.986)
  the two profiles are of different devices: /device:TPU:8 before, /device:TPU:2 now
where the time goes in v7:
time: 209 us; the launch traced here: 208 us
  blocking collectives  78 us (37%)
  starting transfers between devices  70.4 us (34%)
  waiting for transfers between devices  40.5 us (19%)
  Pallas kernels  8.74 us (4%)
  local copies, waits for them, and re-layouts  4.74 us (2%)
  other arithmetic  2.6 us (1%)
    all_to_all x4, blocking collectives, swap(): return lax.all_to_all(value, axis, 0, 0, tiled=True)  78 us
    ppermute x6, starting transfers between devices, share(): lax.ppermute(value, axis, shift(size, k))  33.5 us
    all_to_all x4, starting transfers between devices, swap(): return lax.all_to_all(value, axis, 0, 0, tiled=True)  33.1 us
    ppermute x6, waiting for transfers between devices, share(): lax.ppermute(value, axis, shift(size, k))  27.6 us
    all_to_all x4, waiting for transfers between devices, swap(): return lax.all_to_all(value, axis, 0, 0, tiled=True)  8.34 us
    pallas_call x2, Pallas kernels, call(): pl.pallas_call(kernel, out_shape=tuple((jax.ShapeDtypeStruct(s, BF) for s...  7.21 us
    unnamed x16, local copies, waits for them, and re-layouts  4.63 us
  transfers between devices with their start and end apart: 12, of which 11 were waited for; matrix products, arithmetic and copies ran while one was open for 0% of the time, Pallas kernels for 1%

profile of v7, /device:TPU:2, one launch (start us, length us, event | category | flops | bytes accessed | tf_op | source)
XLA Modules:
  0.0 208.3 jit_solution(6246793943175886168)
XLA Ops:
  0.6 0.0 copy-start
  0.6 0.7 convert_rsqrt_fusion
  1.3 0.2 copy-done
  1.6 1.0 fusion.scaled_ref
  2.6 0.0 copy-start.6
  2.6 0.0 copy-start.5
  2.6 0.0 copy-start.7
  2.6 0.0 copy-start.4
  2.6 15.9 %all_to_all.40 = bf16[4,128,256]{2,1,0:T(8,128)(2,1)S(1)} all-to-all(bf16[4,128,256]{2,1,0:T(8,128)(2,1)S(1)} %broadcast_in_dim.11), channel_id=1, replica_groups=mesh['zl'=4,'x'=4,'c'=2,'y'=8,'zh'=3] {'zl'}, dimensions={0} | all-to-all | bytes 524288 | tf_op jit(solution)/shard_map/all_to_all | solution.py:134
  18.6 0.1 broadcast_in_dim.12
  18.7 16.0 %all_to_all.41 = bf16[4,4,128,256]{3,2,1,0:T(8,128)(2,1)S(1)} all-to-all(bf16[4,4,128,256]{3,2,1,0:T(8,128)(2,1)S(1)} %broadcast_in_dim.12), channel_id=1, replica_groups=mesh['zl'=4,'x'=4,'c'=2,'y'=8,'zh'=3] {'x'}, dimensions={0} | all-to-all | bytes 2097152 | tf_op jit(solution)/shard_map/all_to_all | solution.py:134
  34.7 1.9 collective-permute-start
  37.2 0.0 copy-done.6
  37.3 0.0 copy-done.5
  37.3 0.0 copy-done.7
  37.3 1.9 collective-permute-done.far_ref
  39.2 0.0 copy-done.4
  39.2 0.0 copy-start.1
  39.2 2.2 %copy-done.1 = bf16[1,1,128,128,128]{4,3,2,1,0:T(8,128)(2,1)S(1)} copy-done((bf16[1,1,128,128,128]{4,3,2,1,0:T(8,128)(2,1)S(1)}, bf16[1,1,128,128,128]{4,3,2,1,0:T(8,128)(2,1)}, u32[]{:S(2)}) %copy-start.1) | copy-done | bytes 4194328
  41.4 4.0 %shard_map.104 = (bf16[8,3,128,128]{3,2,1,0:T(8,128)(2,1)}, bf16[8,3,128,128]{3,2,1,0:T(8,128)(2,1)}) custom-call(s32[1]{0:T(128)} %bitcast.31.count_ref, s32[128]{0:T(128)S(1)} %multiply_add_fusion.pick_ref.place_ref, s32[128]{0:T(128)S(1)} %bitcast.39, s32[1]{0:T(128)} %bitcast.3.zh_ref, bf16[128,128,128]{2,1,0:T(8,128)(2,1)S(1)} %bitcast.33, ...), custom_call_target="tpu_custom_call" | custom-call | tf_op jit(solution)/shard_map/pallas_call | solution.py:109
  45.4 0.0 copy-start.3
  45.4 9.0 %all-to-all-start.2 = ((bf16[8,3,128,128]{3,2,1,0:T(8,128)(2,1)}), bf16[8,3,128,128]{3,2,1,0:T(8,128)(2,1)S(1)}, u32[]{:S(2)}, u32[]{:S(2)}) async-start(bf16[8,3,128,128]{3,2,1,0:T(8,128)(2,1)} %get-tuple-element.25), calls=%async_computation.2 | async-start | bytes 1572864 | tf_op jit(solution)/shard_map/all_to_all | solution.py:134
  54.4 10.6 %collective-permute-start.1 = (bf16[144,256]{1,0:T(8,128)(2,1)S(1)}, bf16[144,256]{1,0:T(8,128)(2,1)S(1)}, u32[]{:S(2)}, u32[]{:S(2)}) collective-permute-start(bf16[144,256]{1,0:T(8,128)(2,1)S(1)} %fusion.2.beside_0), channel_id=1, source_target_pairs={{0,1},{1,2},{2,0},{3,4},{4,5},{5,3},{6,7},{7,8},{8,6},{9,10},{10,1... | collective-permute-start | bytes 221192 | tf_op jit(solution)/shard_map/ppermute | solution.py:142
  65.0 1.9 collective-permute-start.2
  66.9 3.1 %collective-permute-done.1.beside_1 = bf16[144,256]{1,0:T(8,128)(2,1)S(1)} collective-permute-done((bf16[144,256]{1,0:T(8,128)(2,1)S(1)}, bf16[144,256]{1,0:T(8,128)(2,1)S(1)}, u32[]{:S(2)}, u32[]{:S(2)}) %collective-permute-start.1) | collective-permute-done | bytes 73760 | tf_op jit(solution)/shard_map/ppermute | solution.py:142
  70.1 5.2 %collective-permute-done.2.beside_2 = bf16[144,256]{1,0:T(8,128)(2,1)S(1)} collective-permute-done((bf16[144,256]{1,0:T(8,128)(2,1)S(1)}, bf16[144,256]{1,0:T(8,128)(2,1)S(1)}, u32[]{:S(2)}, u32[]{:S(2)}) %collective-permute-start.2) | collective-permute-done | bytes 73760 | tf_op jit(solution)/shard_map/ppermute | solution.py:142
  75.3 0.8 all-to-all-done.2.along_y_ref
  76.1 6.3 %all-to-all-start.3 = ((bf16[8,3,128,128]{3,2,1,0:T(8,128)(2,1)}), bf16[8,3,128,128]{3,2,1,0:T(8,128)(2,1)S(1)}, u32[]{:S(2)}, u32[]{:S(2)}) async-start(bf16[8,3,128,128]{3,2,1,0:T(8,128)(2,1)} %get-tuple-element.33), calls=%async_computation.3 | async-start | bytes 1572864 | tf_op jit(solution)/shard_map/all_to_all | solution.py:134
  82.4 0.1 shard_map.105.own_ref
  82.5 7.9 %collective-permute-start.3 = (bf16[384,128]{1,0:T(8,128)(2,1)S(1)}, bf16[384,128]{1,0:T(8,128)(2,1)S(1)}, u32[]{:S(2)}, u32[]{:S(2)}) collective-permute-start(bf16[384,128]{1,0:T(8,128)(2,1)S(1)} %shard_map.105.own_ref), channel_id=1, source_target_pairs={{0,1},{1,2},{2,0},{3,4},{4,5},{5,3},{6,7},{7,8},{8,6},{9,10},{10,1... | collective-permute-start | bytes 294920 | tf_op jit(solution)/shard_map/ppermute | solution.py:142
  90.4 3.3 %collective-permute-start.4 = (bf16[384,128]{1,0:T(8,128)(2,1)S(1)}, bf16[384,128]{1,0:T(8,128)(2,1)S(1)}, u32[]{:S(2)}, u32[]{:S(2)}) collective-permute-start(bf16[384,128]{1,0:T(8,128)(2,1)S(1)} %shard_map.105.own_ref), channel_id=1, source_target_pairs={{0,2},{1,0},{2,1},{3,5},{4,3},{5,4},{6,8},{7,6},{8,7},{9,11},{10,9... | collective-permute-start | bytes 294920 | tf_op jit(solution)/shard_map/ppermute | solution.py:142
  93.7 1.3 collective-permute-done.3.back_1_ref
  95.0 8.6 %collective-permute-done.4.back_2_ref = bf16[384,128]{1,0:T(8,128)(2,1)S(1)} collective-permute-done((bf16[384,128]{1,0:T(8,128)(2,1)S(1)}, bf16[384,128]{1,0:T(8,128)(2,1)S(1)}, u32[]{:S(2)}, u32[]{:S(2)}) %collective-permute-start.4) | collective-permute-done | bytes 98336 | tf_op jit(solution)/shard_map/ppermute | solution.py:142
  103.7 0.0 copy-done.3
  103.7 1.1 shard_map.106
  104.8 0.0 all-to-all-done.3.along_y_ref
  104.8 6.8 %all-to-all-start.4 = ((bf16[8,3,128,128]{3,2,1,0:T(8,128)(2,1)}), bf16[8,3,128,128]{3,2,1,0:T(8,128)(2,1)S(1)}, u32[]{:S(2)}, u32[]{:S(2)}) async-start(bf16[8,3,128,128]{3,2,1,0:T(8,128)(2,1)} %get-tuple-element.37), calls=%async_computation.4 | async-start | bytes 1572864 | tf_op jit(solution)/shard_map/all_to_all | solution.py:134
  111.6 0.1 shard_map.107.own_ref
  111.7 7.1 %collective-permute-start.5 = (bf16[384,128]{1,0:T(8,128)(2,1)S(1)}, bf16[384,128]{1,0:T(8,128)(2,1)S(1)}, u32[]{:S(2)}, u32[]{:S(2)}) collective-permute-start(bf16[384,128]{1,0:T(8,128)(2,1)S(1)} %shard_map.107.own_ref), channel_id=1, source_target_pairs={{0,1},{1,2},{2,0},{3,4},{4,5},{5,3},{6,7},{7,8},{8,6},{9,10},{10,1... | collective-permute-start | bytes 294920 | tf_op jit(solution)/shard_map/ppermute | solution.py:142
  118.8 2.6 %collective-permute-start.6 = (bf16[384,128]{1,0:T(8,128)(2,1)S(1)}, bf16[384,128]{1,0:T(8,128)(2,1)S(1)}, u32[]{:S(2)}, u32[]{:S(2)}) collective-permute-start(bf16[384,128]{1,0:T(8,128)(2,1)S(1)} %shard_map.107.own_ref), channel_id=1, source_target_pairs={{0,2},{1,0},{2,1},{3,5},{4,3},{5,4},{6,8},{7,6},{8,7},{9,11},{10,9... | collective-permute-start | bytes 294920 | tf_op jit(solution)/shard_map/ppermute | solution.py:142
  121.5 0.7 collective-permute-done.5.back_1_ref
  122.2 8.6 %collective-permute-done.6.back_2_ref = bf16[384,128]{1,0:T(8,128)(2,1)S(1)} collective-permute-done((bf16[384,128]{1,0:T(8,128)(2,1)S(1)}, bf16[384,128]{1,0:T(8,128)(2,1)S(1)}, u32[]{:S(2)}, u32[]{:S(2)}) %collective-permute-start.6) | collective-permute-done | bytes 98336 | tf_op jit(solution)/shard_map/ppermute | solution.py:142
  130.8 0.2 shard_map.108
  131.1 0.2 all-to-all-done.4.ups_0
  131.3 29.1 %all_to_all.42.ups_1 = bf16[8,3,128,128]{3,2,1,0:T(8,128)(2,1)S(1)} all-to-all(bf16[8,3,128,128]{3,2,1,0:T(8,128)(2,1)S(1)} %get-tuple-element.40), channel_id=1, replica_groups=mesh['zl'=4,'x'=4,'c'=2,'y'=8,'zh'=3] {'y'}, dimensions={0} | all-to-all | bytes 1572864 | tf_op jit(solution)/shard_map/all_to_all | solution.py:134
  160.4 0.0 copy-start.2
  160.4 2.2 %copy-done.2 = bf16[1,1,128,128,128]{4,3,2,1,0:T(8,128)(2,1)S(1)} copy-done((bf16[1,1,128,128,128]{4,3,2,1,0:T(8,128)(2,1)S(1)}, bf16[1,1,128,128,128]{4,3,2,1,0:T(8,128)(2,1)}, u32[]{:S(2)}) %copy-start.2) | copy-done | bytes 4194328
  162.6 3.2 %shard_map.109 = (bf16[2048,256]{1,0:T(8,128)(2,1)S(1)}, bf16[2048,256]{1,0:T(8,128)(2,1)S(1)}) custom-call(s32[1]{0:T(128)} %bitcast.32.count_ref, s32[128]{0:T(128)S(1)} %bitcast.40, s32[128]{0:T(128)S(1)} %multiply_add_fusion.pick_ref.place_ref, s32[1]{0:T(128)} %bitcast.3.zh_ref, bf16[128,128,128]{2,1,0:T(8,128)(2,1)S(1)} %bitcast.34, ...), custom_call_target="tpu_custom_call" | custom-call | tf_op jit(solution)/shard_map/pallas_call | solution.py:109
  165.8 1.9 collective-permute-start.7
  167.7 2.6 %collective-permute-done.7 = bf16[2048,256]{1,0:T(8,128)(2,1)S(1)} collective-permute-done((bf16[2048,256]{1,0:T(8,128)(2,1)S(1)}, bf16[2048,256]{1,0:T(8,128)(2,1)S(1)}, u32[]{:S(2)}, u32[]{:S(2)}) %collective-permute-start.7) | collective-permute-done | bytes 1048608 | tf_op jit(solution)/shard_map/ppermute | solution.py:198
  170.4 0.3 add_convert_fusion
  170.7 17.0 %all_to_all.43 = bf16[4,512,256]{2,1,0:T(8,128)(2,1)S(1)} all-to-all(bf16[4,512,256]{2,1,0:T(8,128)(2,1)S(1)} %bitcast.41), channel_id=1, replica_groups=mesh['zl'=4,'x'=4,'c'=2,'y'=8,'zh'=3] {'x'}, dimensions={0} | all-to-all | bytes 2097152 | tf_op jit(solution)/shard_map/all_to_all | solution.py:134
  187.7 0.9 reduce_sum.21
  188.6 10.9 %all-to-all-start.7 = ((bf16[4,128,256]{2,1,0:T(8,128)(2,1)}), bf16[4,128,256]{2,1,0:T(8,128)(2,1)S(1)}, u32[]{:S(2)}, u32[]{:S(2)}) async-start(bf16[4,128,256]{2,1,0:T(8,128)(2,1)} %bitcast.9), calls=%async_computation.7 | async-start | bytes 524288 | tf_op jit(solution)/shard_map/all_to_all | solution.py:134
  199.5 0.6 pad_maximum_fusion
  200.2 7.3 %all-to-all-done.7 = bf16[4,128,256]{2,1,0:T(8,128)(2,1)S(1)} async-done(((bf16[4,128,256]{2,1,0:T(8,128)(2,1)}), bf16[4,128,256]{2,1,0:T(8,128)(2,1)S(1)}, u32[]{:S(2)}, u32[]{:S(2)}) %all-to-all-start.7) | async-done | bytes 262176 | tf_op jit(solution)/shard_map/all_to_all | solution.py:134
  207.5 0.8 convolution_convert_fusion
  (5 shorter events, 0.1 us)
Async XLA Ops:
  0.6 0.9 copy-start
  2.6 34.7 %copy-start.6 = (s32[128]{0:T(128)S(1)}, s32[128]{0:T(128)}, u32[]{:S(2)}) copy-start(s32[128]{0:T(128)} %param.10) | copy-start | bytes 1540
  2.6 34.7 %copy-start.5 = (bf16[128,256]{1,0:T(8,128)(2,1)S(1)}, bf16[128,256]{1,0:T(8,128)(2,1)}, u32[]{:S(2)}) copy-start(bf16[128,256]{1,0:T(8,128)(2,1)} %param.17) | copy-start | bytes 196612
  2.6 34.7 %copy-start.7 = (s32[1,1,128]{2,1,0:T(1,128)S(1)}, s32[1,1,128]{2,1,0:T(1,128)}, u32[]{:S(2)}) copy-start(s32[1,1,128]{2,1,0:T(1,128)} %param.15) | copy-start | bytes 1540
  2.6 36.6 %copy-start.4 = (s32[1,1,128]{2,1,0:T(1,128)S(1)}, s32[1,1,128]{2,1,0:T(1,128)}, u32[]{:S(2)}) copy-start(s32[1,1,128]{2,1,0:T(1,128)} %param.14) | copy-start | bytes 1540
  34.7 4.5 %collective-permute-start = (bf16[2048,256]{1,0:T(8,128)(2,1)S(1)}, bf16[2048,256]{1,0:T(8,128)(2,1)S(1)}, u32[]{:S(2)}, u32[]{:S(2)}) collective-permute-start(bf16[2048,256]{1,0:T(8,128)(2,1)S(1)} %bitcast.35), channel_id=1, source_target_pairs={{0,24},{24,0},{1,25},{25,1},{2,26},{26,2},{3,27},{27,3},{4,28},{28... | collective-permute-start | bytes 3145736 | tf_op jit(solution)/shard_map/ppermute | solution.py:168
  39.2 2.2 %copy-start.1 = (bf16[1,1,128,128,128]{4,3,2,1,0:T(8,128)(2,1)S(1)}, bf16[1,1,128,128,128]{4,3,2,1,0:T(8,128)(2,1)}, u32[]{:S(2)}) copy-start(bf16[1,1,128,128,128]{4,3,2,1,0:T(8,128)(2,1)} %param.13) | copy-start | bytes 12582916
  45.4 58.3 %copy-start.3 = (f32[256]{0:T(256)S(1)}, f32[256]{0:T(256)}, u32[]{:S(2)}) copy-start(f32[256]{0:T(256)} %param.12) | copy-start | bytes 3076
  45.4 30.7 %all-to-all-start.2 = ((bf16[8,3,128,128]{3,2,1,0:T(8,128)(2,1)}), bf16[8,3,128,128]{3,2,1,0:T(8,128)(2,1)S(1)}, u32[]{:S(2)}, u32[]{:S(2)}) async-start(bf16[8,3,128,128]{3,2,1,0:T(8,128)(2,1)} %get-tuple-element.25), calls=%async_computation.2 | async-start | bytes 1572864 | tf_op jit(solution)/shard_map/all_to_all | solution.py:134
  54.4 15.7 %collective-permute-start.1 = (bf16[144,256]{1,0:T(8,128)(2,1)S(1)}, bf16[144,256]{1,0:T(8,128)(2,1)S(1)}, u32[]{:S(2)}, u32[]{:S(2)}) collective-permute-start(bf16[144,256]{1,0:T(8,128)(2,1)S(1)} %fusion.2.beside_0), channel_id=1, source_target_pairs={{0,1},{1,2},{2,0},{3,4},{4,5},{5,3},{6,7},{7,8},{8,6},{9,10},{10,1... | collective-permute-start | bytes 221192 | tf_op jit(solution)/shard_map/ppermute | solution.py:142
  65.0 10.3 %collective-permute-start.2 = (bf16[144,256]{1,0:T(8,128)(2,1)S(1)}, bf16[144,256]{1,0:T(8,128)(2,1)S(1)}, u32[]{:S(2)}, u32[]{:S(2)}) collective-permute-start(bf16[144,256]{1,0:T(8,128)(2,1)S(1)} %fusion.2.beside_0), channel_id=1, source_target_pairs={{0,2},{1,0},{2,1},{3,5},{4,3},{5,4},{6,8},{7,6},{8,7},{9,11},{10,9... | collective-permute-start | bytes 221192 | tf_op jit(solution)/shard_map/ppermute | solution.py:142
  76.1 28.7 %all-to-all-start.3 = ((bf16[8,3,128,128]{3,2,1,0:T(8,128)(2,1)}), bf16[8,3,128,128]{3,2,1,0:T(8,128)(2,1)S(1)}, u32[]{:S(2)}, u32[]{:S(2)}) async-start(bf16[8,3,128,128]{3,2,1,0:T(8,128)(2,1)} %get-tuple-element.33), calls=%async_computation.3 | async-start | bytes 1572864 | tf_op jit(solution)/shard_map/all_to_all | solution.py:134
  82.5 12.5 %collective-permute-start.3 = (bf16[384,128]{1,0:T(8,128)(2,1)S(1)}, bf16[384,128]{1,0:T(8,128)(2,1)S(1)}, u32[]{:S(2)}, u32[]{:S(2)}) collective-permute-start(bf16[384,128]{1,0:T(8,128)(2,1)S(1)} %shard_map.105.own_ref), channel_id=1, source_target_pairs={{0,1},{1,2},{2,0},{3,4},{4,5},{5,3},{6,7},{7,8},{8,6},{9,10},{10,1... | collective-permute-start | bytes 294920 | tf_op jit(solution)/shard_map/ppermute | solution.py:142
  90.4 13.3 %collective-permute-start.4 = (bf16[384,128]{1,0:T(8,128)(2,1)S(1)}, bf16[384,128]{1,0:T(8,128)(2,1)S(1)}, u32[]{:S(2)}, u32[]{:S(2)}) collective-permute-start(bf16[384,128]{1,0:T(8,128)(2,1)S(1)} %shard_map.105.own_ref), channel_id=1, source_target_pairs={{0,2},{1,0},{2,1},{3,5},{4,3},{5,4},{6,8},{7,6},{8,7},{9,11},{10,9... | collective-permute-start | bytes 294920 | tf_op jit(solution)/shard_map/ppermute | solution.py:142
  104.8 26.5 %all-to-all-start.4 = ((bf16[8,3,128,128]{3,2,1,0:T(8,128)(2,1)}), bf16[8,3,128,128]{3,2,1,0:T(8,128)(2,1)S(1)}, u32[]{:S(2)}, u32[]{:S(2)}) async-start(bf16[8,3,128,128]{3,2,1,0:T(8,128)(2,1)} %get-tuple-element.37), calls=%async_computation.4 | async-start | bytes 1572864 | tf_op jit(solution)/shard_map/all_to_all | solution.py:134
  111.7 10.5 %collective-permute-start.5 = (bf16[384,128]{1,0:T(8,128)(2,1)S(1)}, bf16[384,128]{1,0:T(8,128)(2,1)S(1)}, u32[]{:S(2)}, u32[]{:S(2)}) collective-permute-start(bf16[384,128]{1,0:T(8,128)(2,1)S(1)} %shard_map.107.own_ref), channel_id=1, source_target_pairs={{0,1},{1,2},{2,0},{3,4},{4,5},{5,3},{6,7},{7,8},{8,6},{9,10},{10,1... | collective-permute-start | bytes 294920 | tf_op jit(solution)/shard_map/ppermute | solution.py:142
  118.8 12.0 %collective-permute-start.6 = (bf16[384,128]{1,0:T(8,128)(2,1)S(1)}, bf16[384,128]{1,0:T(8,128)(2,1)S(1)}, u32[]{:S(2)}, u32[]{:S(2)}) collective-permute-start(bf16[384,128]{1,0:T(8,128)(2,1)S(1)} %shard_map.107.own_ref), channel_id=1, source_target_pairs={{0,2},{1,0},{2,1},{3,5},{4,3},{5,4},{6,8},{7,6},{8,7},{9,11},{10,9... | collective-permute-start | bytes 294920 | tf_op jit(solution)/shard_map/ppermute | solution.py:142
  160.4 2.2 %copy-start.2 = (bf16[1,1,128,128,128]{4,3,2,1,0:T(8,128)(2,1)S(1)}, bf16[1,1,128,128,128]{4,3,2,1,0:T(8,128)(2,1)}, u32[]{:S(2)}) copy-start(bf16[1,1,128,128,128]{4,3,2,1,0:T(8,128)(2,1)} %param.13) | copy-start | bytes 12582916
  165.8 4.6 %collective-permute-start.7 = (bf16[2048,256]{1,0:T(8,128)(2,1)S(1)}, bf16[2048,256]{1,0:T(8,128)(2,1)S(1)}, u32[]{:S(2)}, u32[]{:S(2)}) collective-permute-start(bf16[2048,256]{1,0:T(8,128)(2,1)S(1)} %get-tuple-element.42), channel_id=1, source_target_pairs={{0,24},{24,0},{1,25},{25,1},{2,26},{26,2},{3,27},{27,3},{4,28},{28... | collective-permute-start | bytes 3145736 | tf_op jit(solution)/shard_map/ppermute | solution.py:198
  188.6 18.9 %all-to-all-start.7 = ((bf16[4,128,256]{2,1,0:T(8,128)(2,1)}), bf16[4,128,256]{2,1,0:T(8,128)(2,1)S(1)}, u32[]{:S(2)}, u32[]{:S(2)}) async-start(bf16[4,128,256]{2,1,0:T(8,128)(2,1)} %bitcast.9), calls=%async_computation.7 | async-start | bytes 524288 | tf_op jit(solution)/shard_map/all_to_all | solution.py:134

commit v8 on v7

--- a/solution.py
+++ b/solution.py
@@ -31,7 +31,7 @@
 
 
 def forward_kernel(
-    count_ref, pick_ref, place_ref, zh_ref, tiles_ref, near_ref, far_ref, out_0, out_1, src, acc
+    count_ref, pick_ref, place_ref, tiles_ref, near_ref, far_ref, out_0, out_1, src, acc
 ):
     half = near_ref.shape[0]
     edge = tiles_ref.shape[-1]
@@ -41,62 +41,60 @@
     accumulate(count_ref, pick_ref, place_ref, tiles_ref, src, acc, False)
     for y in range(Y):
         for k in range(ZH):
-            base = pl.multiple_of((y * ZH + (zh_ref[0] + k) % ZH) * edge, edge)
-            out_0[y, k] = acc[pl.ds(base, edge), :wide].astype(BF)
-            out_1[y, k] = acc[pl.ds(base, edge), wide:].astype(BF)
+            base = (y * ZH + k) * edge
+            out_0[y, k] = acc[base : base + edge, :wide].astype(BF)
+            out_1[y, k] = acc[base : base + edge, wide:].astype(BF)
 
 
 def backward_kernel(
-    count_ref, pick_ref, place_ref, zh_ref, tiles_ref, ups_0, ups_1, near_ref, far_ref, src, acc
+    count_ref, pick_ref, place_ref, tiles_ref, ups_0, ups_1, near_ref, far_ref, src, acc
 ):
     edge = tiles_ref.shape[-1]
     wide = ups_0.shape[-1]
     for y in range(Y):
         for k in range(ZH):
-            base = pl.multiple_of((y * ZH + (zh_ref[0] + k) % ZH) * edge, edge)
-            src[pl.ds(base, edge), :wide] = ups_0[y, k]
-            src[pl.ds(base, edge), wide:] = ups_1[y, k]
+            base = (y * ZH + k) * edge
+            src[base : base + edge, :wide] = ups_0[y, k]
+            src[base : base + edge, wide:] = ups_1[y, k]
     accumulate(count_ref, pick_ref, place_ref, tiles_ref, src, acc, True)
     half = near_ref.shape[0]
     near_ref[...] = acc[:half, :].astype(BF)
     far_ref[...] = acc[half:, :].astype(BF)
 
 
-def pack_kernel(h, along_y_ref, scaled_ref, out):
+def pack_kernel(h, zh_ref, along_y_ref, scaled_ref, out):
     n, wide = scaled_ref.shape[0], out.shape[-1]
+    own = scaled_ref[:, h * wide : (h + 1) * wide].astype(F32)
     for k in range(ZH):
-        summed = along_y_ref[0, k].astype(F32)
-        for y in range(1, Y):
+        summed = jnp.where(zh_ref[0] == k, own, 0.0)
+        for y in range(Y):
             summed += along_y_ref[y, k].astype(F32)
-        if k == 0:
-            summed += scaled_ref[:, h * wide : (h + 1) * wide].astype(F32)
         out[k * n : (k + 1) * n, :] = summed.astype(BF)
 
 
 def middle_kernel(
-    h, own_ref, back_1_ref, back_2_ref, beside_0, beside_1, beside_2, bias_ref,
-    activations_ref, upstream_ref, copies_ref,
-):
-    shared = (own_ref, back_1_ref, back_2_ref)
-    besides = (beside_0, beside_1, beside_2)
+    h, zh_ref, shared_ref, beside_ref, bias_ref, activations_ref, upstream_ref, copies_ref
+):
     n, wide = activations_ref.shape
     lanes = slice(h * wide, (h + 1) * wide)
     for k in range(ZH):
-        gathered = shared[0][k * n : (k + 1) * n, :].astype(F32)
+        gathered = shared_ref[0, k * n : (k + 1) * n, :].astype(F32)
         for j in range(1, ZH):
-            first = (k + j) % ZH * n
-            gathered += shared[j][first : first + n, :].astype(F32)
-        beside = besides[-k % ZH]
-        degree = beside[n:, :n].astype(F32)[:1]
+            gathered += shared_ref[j, k * n : (k + 1) * n, :].astype(F32)
+        degree = beside_ref[k, n:, :n].astype(F32)[:1]
         root = lax.rsqrt(jnp.broadcast_to(degree, (wide, n)).T)
         preact = root * gathered + bias_ref[:, lanes]
         sigmoid_value = jax.nn.sigmoid(preact)
         slope_value = sigmoid_value * (1.0 + preact * (1.0 - sigmoid_value))
-        cotangents = beside[:n, lanes].astype(F32)
+        cotangents = beside_ref[k, :n, lanes].astype(F32)
         upstream = (cotangents * slope_value * root).astype(BF)
-        if k == 0:
-            activations_ref[...] = (preact * sigmoid_value).astype(BF)
+        activations = (preact * sigmoid_value).astype(BF)
+
+        @pl.when(zh_ref[0] == k)
+        def _():
+            activations_ref[...] = activations
             upstream_ref[...] = upstream
+
         for y in range(Y):
             copies_ref[y, k] = upstream
 
@@ -109,7 +107,7 @@
     return pl.pallas_call(
         kernel,
         out_shape=tuple(jax.ShapeDtypeStruct(s, BF) for s in outs),
-        in_specs=[SMEM] * 4 + [VMEM] * (len(args) - 4),
+        in_specs=[SMEM] * 3 + [VMEM] * (len(args) - 3),
         out_specs=tuple(VMEM for _ in outs),
         scratch_shapes=[pltpu.VMEM((src_rows, feat), BF), pltpu.VMEM((acc_rows, feat), F32)],
         compiler_params=pltpu.CompilerParams(vmem_limit_bytes=24 * 1024 * 1024),
@@ -120,7 +118,7 @@
     return pl.pallas_call(
         kernel,
         out_shape=tuple(jax.ShapeDtypeStruct(s, BF) for s in outs),
-        in_specs=[VMEM] * len(args),
+        in_specs=[SMEM] + [VMEM] * (len(args) - 1),
         out_specs=tuple(VMEM for _ in outs),
         compiler_params=pltpu.CompilerParams(vmem_limit_bytes=24 * 1024 * 1024),
     )(*args)
@@ -136,10 +134,6 @@
 
 def spread(value, axis, size):
     return swap(jnp.broadcast_to(value[None], (size,) + value.shape), axis)
-
-
-def share(value, axis, size):
-    return [value] + [lax.ppermute(value, axis, shift(size, k)) for k in range(1, size)]
 
 
 def total(value):
@@ -156,8 +150,9 @@
     wide = feat // 2
     my_zh = lax.axis_index("zh").astype(jnp.int32)[None]
     block_zl, block_x, block_c = columns // (X * C), columns // C % X, columns % C
-    other = (block_c != lax.axis_index("c")).astype(jnp.int32)
-    column_at = (other * X + block_x) * ZL + block_zl
+    other = (block_c != lax.axis_index("c")).astype(jnp.int32) * (X * ZL)
+    column_at = other + block_x * ZL + block_zl
+    sum_at = other + block_zl * X + block_x
     sources, targets, chip = C * X * ZL * n, Y * ZH * n, X * ZL * n
 
     inv_root = lax.rsqrt(degrees.astype(F32))[:, None]
@@ -168,19 +163,19 @@
     far = lax.ppermute(near, "c", shift(C, 1))
     partials = call(
         forward_kernel, [(Y, ZH, n, wide)] * 2, sources, targets, feat,
-        count, column_at, rows, my_zh, tiles, near, far,
+        count, column_at, rows, tiles, near, far,
     )
     degree_rows = jnp.pad(degrees.astype(BF)[None], ((0, 15), (0, feat - n)))
     beside = jnp.concatenate([cotangent, degree_rows], 0)
     partials, beside = lax.optimization_barrier((partials, beside))
-    beside = share(beside, "zh", ZH)
+    beside = lax.all_gather(beside, "zh")
 
     def middle(along_y, h, after):
         along_y, _ = lax.optimization_barrier((along_y, after))
-        (mine,) = call_small(functools.partial(pack_kernel, h), [(ZH * n, wide)], along_y, scaled)
+        (mine,) = call_small(functools.partial(pack_kernel, h), [(ZH * n, wide)], my_zh, along_y, scaled)
         return call_small(
             functools.partial(middle_kernel, h), [(n, wide), (n, wide), (Y, ZH, n, wide)],
-            *share(mine, "zh", ZH), *beside, bias_term[None],
+            my_zh, lax.all_gather(mine, "zh"), beside, bias_term[None],
         )
 
     along_y_0 = swap(partials[0], "y")
@@ -193,12 +188,11 @@
 
     own, others = call(
         backward_kernel, [(chip, feat)] * 2, targets, sources, feat,
-        count, rows, column_at, my_zh, tiles, ups_0, ups_1,
+        count, rows, sum_at, tiles, ups_0, ups_1,
     )
     others = lax.ppermute(others, "c", shift(C, 1))
-    back = (own.astype(F32) + others.astype(F32)).astype(BF).reshape(X, ZL * n, feat)
-    back = total(swap(back, "x")).astype(BF).reshape(ZL, n, feat)
-    own_back = total(swap(back, "zl"))
+    back = (own.astype(F32) + others.astype(F32)).astype(BF).reshape(ZL * X, n, feat)
+    own_back = total(swap(back, ("zl", "x")))
     upstream = jnp.concatenate([upstream_0, upstream_1], 1)
     grad_hidden = (inv_root * (own_back + upstream.astype(F32))).astype(BF)
     feature_grad = jnp.einsum("nf,gf->ng", grad_hidden, weight, preferred_element_type=F32)

time: 209 us -> 206 us (0.986)
  the two profiles are of different devices: /device:TPU:2 before, /device:TPU:72 now
where the time goes in v8:
time: 206 us; the launch traced here: 205 us
  blocking collectives  119 us (58%)
  starting transfers between devices  36 us (17%)
  waiting for transfers between devices  31.8 us (15%)
  Pallas kernels  7.25 us (4%)
  local copies, waits for them, and re-layouts  4.74 us (2%)
  other arithmetic  2.83 us (1%)
    all_to_all x3, blocking collectives, swap(): return lax.all_to_all(value, axis, 0, 0, tiled=True)  57.3 us
    all_gather x2, blocking collectives, middle(): lax.all_gather(mine, 'zh')  39.7 us
    all_to_all x4, starting transfers between devices, swap(): return lax.all_to_all(value, axis, 0, 0, tiled=True)  32.2 us
    all_to_all x4, waiting for transfers between devices, swap(): return lax.all_to_all(value, axis, 0, 0, tiled=True)  27.3 us
    all_gather x1, blocking collectives, body(): beside = lax.all_gather(beside, 'zh')  22 us
    pallas_call x2, Pallas kernels, call(): pl.pallas_call(kernel, out_shape=tuple((jax.ShapeDtypeStruct(s, BF) for s...  5.3 us
    unnamed x16, local copies, waits for them, and re-layouts  4.63 us
  transfers between devices with their start and end apart: 6, of which 4 were waited for; matrix products, arithmetic and copies ran while one was open for 0% of the time, Pallas kernels for 1%

profile of v8, /device:TPU:72, one launch (start us, length us, event | category | flops | bytes accessed | tf_op | source)
XLA Modules:
  0.0 204.9 jit_solution(17581686948471198181)
XLA Ops:
  0.6 0.0 copy-start
  0.6 0.7 convert_rsqrt_fusion
  1.3 0.2 copy-done
  1.6 1.0 fusion.scaled_ref
  2.6 0.0 copy-start.7
  2.6 0.0 copy-start.5
  2.6 0.0 copy-start.6
  2.6 0.0 copy-start.4
  2.6 13.8 %all_to_all.35 = bf16[4,128,256]{2,1,0:T(8,128)(2,1)S(1)} all-to-all(bf16[4,128,256]{2,1,0:T(8,128)(2,1)S(1)} %broadcast_in_dim.11), channel_id=1, replica_groups=mesh['zl'=4,'x'=4,'c'=2,'y'=8,'zh'=3] {'zl'}, dimensions={0} | all-to-all | bytes 524288 | tf_op jit(solution)/shard_map/all_to_all | solution.py:132
  16.4 0.1 broadcast_in_dim.12
  16.5 17.6 %all_to_all.36 = bf16[4,4,128,256]{3,2,1,0:T(8,128)(2,1)S(1)} all-to-all(bf16[4,4,128,256]{3,2,1,0:T(8,128)(2,1)S(1)} %broadcast_in_dim.12), channel_id=1, replica_groups=mesh['zl'=4,'x'=4,'c'=2,'y'=8,'zh'=3] {'x'}, dimensions={0} | all-to-all | bytes 2097152 | tf_op jit(solution)/shard_map/all_to_all | solution.py:132
  34.1 1.9 collective-permute-start
  36.6 0.0 copy-done.7
  36.7 0.0 copy-done.5
  36.7 0.0 copy-done.6
  36.7 1.9 collective-permute-done.far_ref
  38.6 0.0 copy-done.4
  38.6 0.0 copy-start.1
  38.6 2.2 %copy-done.1 = bf16[1,1,128,128,128]{4,3,2,1,0:T(8,128)(2,1)S(1)} copy-done((bf16[1,1,128,128,128]{4,3,2,1,0:T(8,128)(2,1)S(1)}, bf16[1,1,128,128,128]{4,3,2,1,0:T(8,128)(2,1)}, u32[]{:S(2)}) %copy-start.1) | copy-done | bytes 4194328
  40.8 3.1 %shard_map.104 = (bf16[8,3,128,128]{3,2,1,0:T(8,128)(2,1)}, bf16[8,3,128,128]{3,2,1,0:T(8,128)(2,1)}) custom-call(s32[1]{0:T(128)} %bitcast.44.count_ref, s32[128]{0:T(128)S(1)} %add_add_fusion.1.pick_ref, s32[128]{0:T(128)S(1)} %bitcast.56, bf16[128,128,128]{2,1,0:T(8,128)(2,1)S(1)} %bitcast.46, bf16[2048,256]{1,0:T(8,128)(2,1)S(1)} %bitcast.49, ...), custom_call_target="tpu_custom_call" | custom-call | tf_op jit(solution)/shard_map/pallas_call | solution.py:107
  43.9 0.0 copy-start.3
  43.9 8.6 %all-to-all-start.2 = ((bf16[8,3,128,128]{3,2,1,0:T(8,128)(2,1)}), bf16[8,3,128,128]{3,2,1,0:T(8,128)(2,1)S(1)}, u32[]{:S(2)}, u32[]{:S(2)}) async-start(bf16[8,3,128,128]{3,2,1,0:T(8,128)(2,1)} %get-tuple-element.23), calls=%async_computation.2 | async-start | bytes 1572864 | tf_op jit(solution)/shard_map/all_to_all | solution.py:132
  52.4 22.0 %all-gather = bf16[432,256]{1,0:T(8,128)(2,1)S(1)} all-gather(bf16[144,256]{1,0:T(8,128)(2,1)S(1)} %fusion.2), channel_id=2, replica_groups=mesh['zl'=4,'x'=4,'c'=2,'y'=8,'zh'=3] {'zh'}, dimensions={0}, use_global_device_ids=true | all-gather | bytes 294912 | tf_op jit(solution)/shard_map/all_gather | solution.py:171
  74.5 0.0 all-to-all-done.2.along_y_ref
  74.5 7.2 %all-to-all-start.3 = ((bf16[8,3,128,128]{3,2,1,0:T(8,128)(2,1)}), bf16[8,3,128,128]{3,2,1,0:T(8,128)(2,1)S(1)}, u32[]{:S(2)}, u32[]{:S(2)}) async-start(bf16[8,3,128,128]{3,2,1,0:T(8,128)(2,1)} %get-tuple-element.29), calls=%async_computation.3 | async-start | bytes 1572864 | tf_op jit(solution)/shard_map/all_to_all | solution.py:132
  81.7 0.1 shard_map.105
  81.8 21.0 %all-gather.1 = bf16[1152,128]{1,0:T(8,128)(2,1)S(1)} all-gather(bf16[384,128]{1,0:T(8,128)(2,1)S(1)} %shard_map.105), channel_id=3, replica_groups=mesh['zl'=4,'x'=4,'c'=2,'y'=8,'zh'=3] {'zh'}, dimensions={0}, use_global_device_ids=true | all-gather | bytes 393216 | tf_op jit(solution)/shard_map/all_gather | solution.py:178
  102.8 0.0 copy-done.3
  102.8 1.3 shard_map.106
  104.1 0.0 all-to-all-done.3.along_y_ref
  104.1 7.2 %all-to-all-start.4 = ((bf16[8,3,128,128]{3,2,1,0:T(8,128)(2,1)}), bf16[8,3,128,128]{3,2,1,0:T(8,128)(2,1)S(1)}, u32[]{:S(2)}, u32[]{:S(2)}) async-start(bf16[8,3,128,128]{3,2,1,0:T(8,128)(2,1)} %get-tuple-element.33), calls=%async_computation.4 | async-start | bytes 1572864 | tf_op jit(solution)/shard_map/all_to_all | solution.py:132
  111.3 0.1 shard_map.107
  111.4 18.7 %all-gather.2 = bf16[1152,128]{1,0:T(8,128)(2,1)S(1)} all-gather(bf16[384,128]{1,0:T(8,128)(2,1)S(1)} %shard_map.107), channel_id=4, replica_groups=mesh['zl'=4,'x'=4,'c'=2,'y'=8,'zh'=3] {'zh'}, dimensions={0}, use_global_device_ids=true | all-gather | bytes 393216 | tf_op jit(solution)/shard_map/all_gather | solution.py:178
  130.1 0.4 shard_map.108
  130.5 1.9 all-to-all-done.4.ups_0
  132.4 26.0 %all_to_all.37.ups_1 = bf16[8,3,128,128]{3,2,1,0:T(8,128)(2,1)S(1)} all-to-all(bf16[8,3,128,128]{3,2,1,0:T(8,128)(2,1)S(1)} %get-tuple-element.36), channel_id=1, replica_groups=mesh['zl'=4,'x'=4,'c'=2,'y'=8,'zh'=3] {'y'}, dimensions={0} | all-to-all | bytes 1572864 | tf_op jit(solution)/shard_map/all_to_all | solution.py:132
  158.4 0.0 copy-start.2
  158.4 2.2 %copy-done.2 = bf16[1,1,128,128,128]{4,3,2,1,0:T(8,128)(2,1)S(1)} copy-done((bf16[1,1,128,128,128]{4,3,2,1,0:T(8,128)(2,1)S(1)}, bf16[1,1,128,128,128]{4,3,2,1,0:T(8,128)(2,1)}, u32[]{:S(2)}) %copy-start.2) | copy-done | bytes 4194328
  160.6 2.2 %shard_map.109 = (bf16[2048,256]{1,0:T(8,128)(2,1)S(1)}, bf16[2048,256]{1,0:T(8,128)(2,1)S(1)}) custom-call(s32[1]{0:T(128)} %bitcast.45.count_ref, s32[128]{0:T(128)S(1)} %bitcast.57, s32[128]{0:T(128)S(1)} %get-tuple-element.40.place_ref, bf16[128,128,128]{2,1,0:T(8,128)(2,1)S(1)} %bitcast.47, bf16[8,3,128,128]{3,2,1,0:T(8,128)(2,1)S(1)} %all-to-all-done.4.ups_0, ...), custom_call_target="tpu_custom_call" | custom-call | tf_op jit(solution)/shard_map/pallas_call | solution.py:107
  162.8 1.9 collective-permute-start.1
  164.8 2.6 %collective-permute-done.1 = bf16[2048,256]{1,0:T(8,128)(2,1)S(1)} collective-permute-done((bf16[2048,256]{1,0:T(8,128)(2,1)S(1)}, bf16[2048,256]{1,0:T(8,128)(2,1)S(1)}, u32[]{:S(2)}, u32[]{:S(2)}) %collective-permute-start.1) | collective-permute-done | bytes 1048608 | tf_op jit(solution)/shard_map/ppermute | solution.py:193
  167.4 1.3 add_convert_fusion
  168.7 9.2 %all-to-all-start.6 = ((bf16[16,128,256]{2,1,0:T(8,128)(2,1)}), bf16[16,128,256]{2,1,0:T(8,128)(2,1)S(1)}, u32[]{:S(2)}, u32[]{:S(2)}) async-start(bf16[16,128,256]{2,1,0:T(8,128)(2,1)} %bitcast.11), calls=%async_computation.6 | async-start | bytes 2097152 | tf_op jit(solution)/shard_map/all_to_all | solution.py:132
  177.9 0.6 pad_maximum_fusion
  178.5 25.4 %all-to-all-done.6 = bf16[16,128,256]{2,1,0:T(8,128)(2,1)S(1)} async-done(((bf16[16,128,256]{2,1,0:T(8,128)(2,1)}), bf16[16,128,256]{2,1,0:T(8,128)(2,1)S(1)}, u32[]{:S(2)}, u32[]{:S(2)}) %all-to-all-start.6) | async-done | bytes 1048608 | tf_op jit(solution)/shard_map/all_to_all | solution.py:132
  203.9 0.1 convert_reduce_fusion
  204.0 0.8 convolution_convert_fusion
  (5 shorter events, 0.1 us)
Async XLA Ops:
  0.6 0.9 copy-start
  2.6 34.1 %copy-start.7 = (s32[128]{0:T(128)S(1)}, s32[128]{0:T(128)}, u32[]{:S(2)}) copy-start(s32[128]{0:T(128)} %param.10) | copy-start | bytes 1540
  2.6 34.1 %copy-start.5 = (bf16[128,256]{1,0:T(8,128)(2,1)S(1)}, bf16[128,256]{1,0:T(8,128)(2,1)}, u32[]{:S(2)}) copy-start(bf16[128,256]{1,0:T(8,128)(2,1)} %param.17) | copy-start | bytes 196612
  2.6 34.1 %copy-start.6 = (s32[1,1,128]{2,1,0:T(1,128)S(1)}, s32[1,1,128]{2,1,0:T(1,128)}, u32[]{:S(2)}) copy-start(s32[1,1,128]{2,1,0:T(1,128)} %param.15) | copy-start | bytes 1540
  2.6 36.0 %copy-start.4 = (s32[1,1,128]{2,1,0:T(1,128)S(1)}, s32[1,1,128]{2,1,0:T(1,128)}, u32[]{:S(2)}) copy-start(s32[1,1,128]{2,1,0:T(1,128)} %param.14) | copy-start | bytes 1540
  34.1 4.5 %collective-permute-start = (bf16[2048,256]{1,0:T(8,128)(2,1)S(1)}, bf16[2048,256]{1,0:T(8,128)(2,1)S(1)}, u32[]{:S(2)}, u32[]{:S(2)}) collective-permute-start(bf16[2048,256]{1,0:T(8,128)(2,1)S(1)} %bitcast.48), channel_id=1, source_target_pairs={{0,24},{24,0},{1,25},{25,1},{2,26},{26,2},{3,27},{27,3},{4,28},{28... | collective-permute-start | bytes 3145736 | tf_op jit(solution)/shard_map/ppermute | solution.py:163
  38.6 2.2 %copy-start.1 = (bf16[1,1,128,128,128]{4,3,2,1,0:T(8,128)(2,1)S(1)}, bf16[1,1,128,128,128]{4,3,2,1,0:T(8,128)(2,1)}, u32[]{:S(2)}) copy-start(bf16[1,1,128,128,128]{4,3,2,1,0:T(8,128)(2,1)} %param.13) | copy-start | bytes 12582916
  43.9 58.9 %copy-start.3 = (f32[256]{0:T(256)S(1)}, f32[256]{0:T(256)}, u32[]{:S(2)}) copy-start(f32[256]{0:T(256)} %param.12) | copy-start | bytes 3076
  43.9 30.6 %all-to-all-start.2 = ((bf16[8,3,128,128]{3,2,1,0:T(8,128)(2,1)}), bf16[8,3,128,128]{3,2,1,0:T(8,128)(2,1)S(1)}, u32[]{:S(2)}, u32[]{:S(2)}) async-start(bf16[8,3,128,128]{3,2,1,0:T(8,128)(2,1)} %get-tuple-element.23), calls=%async_computation.2 | async-start | bytes 1572864 | tf_op jit(solution)/shard_map/all_to_all | solution.py:132
  74.5 29.6 %all-to-all-start.3 = ((bf16[8,3,128,128]{3,2,1,0:T(8,128)(2,1)}), bf16[8,3,128,128]{3,2,1,0:T(8,128)(2,1)S(1)}, u32[]{:S(2)}, u32[]{:S(2)}) async-start(bf16[8,3,128,128]{3,2,1,0:T(8,128)(2,1)} %get-tuple-element.29), calls=%async_computation.3 | async-start | bytes 1572864 | tf_op jit(solution)/shard_map/all_to_all | solution.py:132
  104.1 28.3 %all-to-all-start.4 = ((bf16[8,3,128,128]{3,2,1,0:T(8,128)(2,1)}), bf16[8,3,128,128]{3,2,1,0:T(8,128)(2,1)S(1)}, u32[]{:S(2)}, u32[]{:S(2)}) async-start(bf16[8,3,128,128]{3,2,1,0:T(8,128)(2,1)} %get-tuple-element.33), calls=%async_computation.4 | async-start | bytes 1572864 | tf_op jit(solution)/shard_map/all_to_all | solution.py:132
  158.4 2.2 %copy-start.2 = (bf16[1,1,128,128,128]{4,3,2,1,0:T(8,128)(2,1)S(1)}, bf16[1,1,128,128,128]{4,3,2,1,0:T(8,128)(2,1)}, u32[]{:S(2)}) copy-start(bf16[1,1,128,128,128]{4,3,2,1,0:T(8,128)(2,1)} %param.13) | copy-start | bytes 12582916
  162.8 4.6 %collective-permute-start.1 = (bf16[2048,256]{1,0:T(8,128)(2,1)S(1)}, bf16[2048,256]{1,0:T(8,128)(2,1)S(1)}, u32[]{:S(2)}, u32[]{:S(2)}) collective-permute-start(bf16[2048,256]{1,0:T(8,128)(2,1)S(1)} %get-tuple-element.38), channel_id=1, source_target_pairs={{0,24},{24,0},{1,25},{25,1},{2,26},{26,2},{3,27},{27,3},{4,28},{28... | collective-permute-start | bytes 3145736 | tf_op jit(solution)/shard_map/ppermute | solution.py:193
  168.7 35.2 %all-to-all-start.6 = ((bf16[16,128,256]{2,1,0:T(8,128)(2,1)}), bf16[16,128,256]{2,1,0:T(8,128)(2,1)S(1)}, u32[]{:S(2)}, u32[]{:S(2)}) async-start(bf16[16,128,256]{2,1,0:T(8,128)(2,1)} %bitcast.11), calls=%async_computation.6 | async-start | bytes 2097152 | tf_op jit(solution)/shard_map/all_to_all | solution.py:132

commit v9 on v8

--- a/solution.py
+++ b/solution.py
@@ -12,33 +12,50 @@
 BF, F32 = jnp.bfloat16, jnp.float32
 NODE_AXES = ("zl", "x", "c", "y", "zh")
 UNROLL = 16
-
-
-def accumulate(count_ref, pick_ref, place_ref, tiles_ref, src, acc, transposed):
-    edge = tiles_ref.shape[-1]
+PARTS = 4
+
+
+def fetch(tiles_ref, tiles, sems):
+    size = tiles.shape[0] // PARTS
+    copies = []
+    for part in range(PARTS):
+        slots = pl.ds(part * size, size)
+        copies.append(pltpu.make_async_copy(tiles_ref.at[slots], tiles.at[slots], sems.at[part]))
+        copies[-1].start()
+    return copies
+
+
+def accumulate(count_ref, pick_ref, place_ref, tiles, copies, src, acc, transposed):
+    edge = tiles.shape[-1]
+    size = tiles.shape[0] // PARTS
     dims = (((0,), (0,)), ((), ())) if transposed else (((1,), (0,)), ((), ()))
     acc[...] = jnp.zeros_like(acc)
 
-    def step(s, carry):
-        for u in range(UNROLL):
-            t = s * UNROLL + u
-            block = src[pl.ds(pl.multiple_of(pick_ref[t] * edge, edge), edge), :]
-            product = lax.dot_general(tiles_ref[t], block, dims, preferred_element_type=F32)
-            acc[pl.ds(pl.multiple_of(place_ref[t] * edge, edge), edge), :] += product
-        return carry
-
-    lax.fori_loop(0, count_ref[0] // UNROLL, step, 0)
+    for part in range(PARTS):
+        copies[part].wait()
+
+        def step(s, carry, first=part * size):
+            for u in range(UNROLL):
+                t = first + s * UNROLL + u
+                block = src[pl.ds(pl.multiple_of(pick_ref[t] * edge, edge), edge), :]
+                product = lax.dot_general(tiles[t], block, dims, preferred_element_type=F32)
+                acc[pl.ds(pl.multiple_of(place_ref[t] * edge, edge), edge), :] += product
+            return carry
+
+        live = jnp.clip(count_ref[0] - part * size, 0, size)
+        lax.fori_loop(0, live // UNROLL, step, 0)
 
 
 def forward_kernel(
-    count_ref, pick_ref, place_ref, tiles_ref, near_ref, far_ref, out_0, out_1, src, acc
-):
+    count_ref, pick_ref, place_ref, tiles_ref, near_ref, far_ref, out_0, out_1, src, acc, tiles, sems
+):
+    copies = fetch(tiles_ref, tiles, sems)
     half = near_ref.shape[0]
-    edge = tiles_ref.shape[-1]
+    edge = tiles.shape[-1]
     wide = out_0.shape[-1]
     src[:half] = near_ref[...]
     src[half:] = far_ref[...]
-    accumulate(count_ref, pick_ref, place_ref, tiles_ref, src, acc, False)
+    accumulate(count_ref, pick_ref, place_ref, tiles, copies, src, acc, False)
     for y in range(Y):
         for k in range(ZH):
             base = (y * ZH + k) * edge
@@ -47,16 +64,17 @@
 
 
 def backward_kernel(
-    count_ref, pick_ref, place_ref, tiles_ref, ups_0, ups_1, near_ref, far_ref, src, acc
-):
-    edge = tiles_ref.shape[-1]
+    count_ref, pick_ref, place_ref, tiles_ref, ups_0, ups_1, near_ref, far_ref, src, acc, tiles, sems
+):
+    copies = fetch(tiles_ref, tiles, sems)
+    edge = tiles.shape[-1]
     wide = ups_0.shape[-1]
     for y in range(Y):
         for k in range(ZH):
             base = (y * ZH + k) * edge
             src[base : base + edge, :wide] = ups_0[y, k]
             src[base : base + edge, wide:] = ups_1[y, k]
-    accumulate(count_ref, pick_ref, place_ref, tiles_ref, src, acc, True)
+    accumulate(count_ref, pick_ref, place_ref, tiles, copies, src, acc, True)
     half = near_ref.shape[0]
     near_ref[...] = acc[:half, :].astype(BF)
     far_ref[...] = acc[half:, :].astype(BF)
@@ -101,16 +119,23 @@
 
 SMEM = pl.BlockSpec(memory_space=pltpu.SMEM)
 VMEM = pl.BlockSpec(memory_space=pltpu.VMEM)
+HBM = pl.BlockSpec(memory_space=pltpu.HBM)
 
 
 def call(kernel, outs, src_rows, acc_rows, feat, *args):
+    tiles = args[3]
     return pl.pallas_call(
         kernel,
         out_shape=tuple(jax.ShapeDtypeStruct(s, BF) for s in outs),
-        in_specs=[SMEM] * 3 + [VMEM] * (len(args) - 3),
+        in_specs=[SMEM] * 3 + [HBM] + [VMEM] * (len(args) - 4),
         out_specs=tuple(VMEM for _ in outs),
-        scratch_shapes=[pltpu.VMEM((src_rows, feat), BF), pltpu.VMEM((acc_rows, feat), F32)],
-        compiler_params=pltpu.CompilerParams(vmem_limit_bytes=24 * 1024 * 1024),
+        scratch_shapes=[
+            pltpu.VMEM((src_rows, feat), BF),
+            pltpu.VMEM((acc_rows, feat), F32),
+            pltpu.VMEM(tiles.shape, BF),
+            pltpu.SemaphoreType.DMA((PARTS,)),
+        ],
+        compiler_params=pltpu.CompilerParams(vmem_limit_bytes=48 * 1024 * 1024),
     )(*args)
 
 

time: 206 us -> 202 us (0.981)
  the two profiles are of different devices: /device:TPU:72 before, /device:TPU:64 now
where the time goes in v9:
time: 202 us
  blocking collectives  119 us (59%)
  waiting for transfers between devices  33.9 us (17%)
  starting transfers between devices  28 us (14%)
  Pallas kernels  14.4 us (7%)
  other arithmetic  2.82 us (1%)
    all_to_all x3, blocking collectives, swap(): return lax.all_to_all(value, axis, 0, 0, tiled=True)  58.7 us
    all_gather x2, blocking collectives, middle(): lax.all_gather(mine, 'zh')  40.2 us
    all_to_all x4, waiting for transfers between devices, swap(): return lax.all_to_all(value, axis, 0, 0, tiled=True)  29.4 us
    all_to_all x4, starting transfers between devices, swap(): return lax.all_to_all(value, axis, 0, 0, tiled=True)  24.2 us
    all_gather x1, blocking collectives, body(): beside = lax.all_gather(beside, 'zh')  20 us
    pallas_call x2, Pallas kernels, call(): pl.pallas_call(kernel, out_shape=tuple((jax.ShapeDtypeStruct(s, BF) for s...  12.4 us
  transfers between devices with their start and end apart: 6, of which 6 were waited for; matrix products, arithmetic and copies ran while one was open for 0% of the time, Pallas kernels for 1%

profile of v9, /device:TPU:64, one launch (start us, length us, event | category | flops | bytes accessed | tf_op | source)
XLA Modules:
  0.0 201.7 jit_solution(25819087411538078)
XLA Ops:
  0.6 0.0 copy-start
  0.6 0.7 convert_rsqrt_fusion
  1.3 0.2 copy-done
  1.6 1.0 fusion.scaled_ref
  2.6 0.0 copy-start.5
  2.6 0.0 copy-start.3
  2.6 0.0 copy-start.4
  2.6 0.0 copy-start.2
  2.6 17.3 %all_to_all.35 = bf16[4,128,256]{2,1,0:T(8,128)(2,1)S(1)} all-to-all(bf16[4,128,256]{2,1,0:T(8,128)(2,1)S(1)} %broadcast_in_dim.11), channel_id=1, replica_groups=mesh['zl'=4,'x'=4,'c'=2,'y'=8,'zh'=3] {'zl'}, dimensions={0} | all-to-all | bytes 524288 | tf_op jit(solution)/shard_map/all_to_all | solution.py:157
  19.9 0.1 broadcast_in_dim.12
  20.0 14.1 %all_to_all.36 = bf16[4,4,128,256]{3,2,1,0:T(8,128)(2,1)S(1)} all-to-all(bf16[4,4,128,256]{3,2,1,0:T(8,128)(2,1)S(1)} %broadcast_in_dim.12), channel_id=1, replica_groups=mesh['zl'=4,'x'=4,'c'=2,'y'=8,'zh'=3] {'x'}, dimensions={0} | all-to-all | bytes 2097152 | tf_op jit(solution)/shard_map/all_to_all | solution.py:157
  34.1 1.9 collective-permute-start
  36.6 0.0 copy-done.5
  36.7 0.0 copy-done.3
  36.7 0.0 copy-done.4
  36.7 1.9 collective-permute-done.far_ref
  38.6 0.0 copy-done.2
  38.6 6.6 %shard_map.104 = (bf16[8,3,128,128]{3,2,1,0:T(8,128)(2,1)}, bf16[8,3,128,128]{3,2,1,0:T(8,128)(2,1)}) custom-call(s32[1]{0:T(128)} %bitcast.44.count_ref, s32[128]{0:T(128)S(1)} %add_add_fusion.1.pick_ref, s32[128]{0:T(128)S(1)} %bitcast.54, bf16[128,128,128]{2,1,0:T(8,128)(2,1)} %bitcast.56, bf16[2048,256]{1,0:T(8,128)(2,1)S(1)} %bitcast.47, ...), custom_call_target="tpu_custom_call" | custom-call | tf_op jit(solution)/shard_map/pallas_call | solution.py:127
  45.3 0.0 copy-start.1
  45.3 6.3 %all-to-all-start.2 = ((bf16[8,3,128,128]{3,2,1,0:T(8,128)(2,1)}), bf16[8,3,128,128]{3,2,1,0:T(8,128)(2,1)S(1)}, u32[]{:S(2)}, u32[]{:S(2)}) async-start(bf16[8,3,128,128]{3,2,1,0:T(8,128)(2,1)} %get-tuple-element.23), calls=%async_computation.2 | async-start | bytes 1572864 | tf_op jit(solution)/shard_map/all_to_all | solution.py:157
  51.6 20.0 %all-gather = bf16[432,256]{1,0:T(8,128)(2,1)S(1)} all-gather(bf16[144,256]{1,0:T(8,128)(2,1)S(1)} %fusion.2), channel_id=2, replica_groups=mesh['zl'=4,'x'=4,'c'=2,'y'=8,'zh'=3] {'zh'}, dimensions={0}, use_global_device_ids=true | all-gather | bytes 294912 | tf_op jit(solution)/shard_map/all_gather | solution.py:196
  71.6 2.0 all-to-all-done.2.along_y_ref
  73.6 5.3 %all-to-all-start.3 = ((bf16[8,3,128,128]{3,2,1,0:T(8,128)(2,1)}), bf16[8,3,128,128]{3,2,1,0:T(8,128)(2,1)S(1)}, u32[]{:S(2)}, u32[]{:S(2)}) async-start(bf16[8,3,128,128]{3,2,1,0:T(8,128)(2,1)} %get-tuple-element.29), calls=%async_computation.3 | async-start | bytes 1572864 | tf_op jit(solution)/shard_map/all_to_all | solution.py:157
  78.8 0.1 shard_map.105
  79.0 21.2 %all-gather.1 = bf16[1152,128]{1,0:T(8,128)(2,1)S(1)} all-gather(bf16[384,128]{1,0:T(8,128)(2,1)S(1)} %shard_map.105), channel_id=3, replica_groups=mesh['zl'=4,'x'=4,'c'=2,'y'=8,'zh'=3] {'zh'}, dimensions={0}, use_global_device_ids=true | all-gather | bytes 393216 | tf_op jit(solution)/shard_map/all_gather | solution.py:203
  100.1 0.0 copy-done.1
  100.1 1.3 shard_map.106
  101.4 0.5 all-to-all-done.3.along_y_ref
  101.9 7.1 %all-to-all-start.4 = ((bf16[8,3,128,128]{3,2,1,0:T(8,128)(2,1)}), bf16[8,3,128,128]{3,2,1,0:T(8,128)(2,1)S(1)}, u32[]{:S(2)}, u32[]{:S(2)}) async-start(bf16[8,3,128,128]{3,2,1,0:T(8,128)(2,1)} %get-tuple-element.33), calls=%async_computation.4 | async-start | bytes 1572864 | tf_op jit(solution)/shard_map/all_to_all | solution.py:157
  109.0 0.1 shard_map.107
  109.1 19.0 %all-gather.2 = bf16[1152,128]{1,0:T(8,128)(2,1)S(1)} all-gather(bf16[384,128]{1,0:T(8,128)(2,1)S(1)} %shard_map.107), channel_id=4, replica_groups=mesh['zl'=4,'x'=4,'c'=2,'y'=8,'zh'=3] {'zh'}, dimensions={0}, use_global_device_ids=true | all-gather | bytes 393216 | tf_op jit(solution)/shard_map/all_gather | solution.py:203
  128.1 0.4 shard_map.108
  128.5 1.6 all-to-all-done.4.ups_0
  130.1 27.4 %all_to_all.37.ups_1 = bf16[8,3,128,128]{3,2,1,0:T(8,128)(2,1)S(1)} all-to-all(bf16[8,3,128,128]{3,2,1,0:T(8,128)(2,1)S(1)} %get-tuple-element.36), channel_id=1, replica_groups=mesh['zl'=4,'x'=4,'c'=2,'y'=8,'zh'=3] {'y'}, dimensions={0} | all-to-all | bytes 1572864 | tf_op jit(solution)/shard_map/all_to_all | solution.py:157
  157.5 5.8 %shard_map.109 = (bf16[2048,256]{1,0:T(8,128)(2,1)S(1)}, bf16[2048,256]{1,0:T(8,128)(2,1)S(1)}) custom-call(s32[1]{0:T(128)} %bitcast.45.count_ref, s32[128]{0:T(128)S(1)} %bitcast.55, s32[128]{0:T(128)S(1)} %get-tuple-element.40.place_ref, bf16[128,128,128]{2,1,0:T(8,128)(2,1)} %bitcast.57, bf16[8,3,128,128]{3,2,1,0:T(8,128)(2,1)S(1)} %all-to-all-done.4.ups_0, ...), custom_call_target="tpu_custom_call" | custom-call | tf_op jit(solution)/shard_map/pallas_call | solution.py:127
  163.4 1.9 collective-permute-start.1
  165.3 2.6 %collective-permute-done.1 = bf16[2048,256]{1,0:T(8,128)(2,1)S(1)} collective-permute-done((bf16[2048,256]{1,0:T(8,128)(2,1)S(1)}, bf16[2048,256]{1,0:T(8,128)(2,1)S(1)}, u32[]{:S(2)}, u32[]{:S(2)}) %collective-permute-start.1) | collective-permute-done | bytes 1048608 | tf_op jit(solution)/shard_map/ppermute | solution.py:218
  167.9 1.3 add_convert_fusion
  169.2 5.5 %all-to-all-start.6 = ((bf16[16,128,256]{2,1,0:T(8,128)(2,1)}), bf16[16,128,256]{2,1,0:T(8,128)(2,1)S(1)}, u32[]{:S(2)}, u32[]{:S(2)}) async-start(bf16[16,128,256]{2,1,0:T(8,128)(2,1)} %bitcast.11), calls=%async_computation.6 | async-start | bytes 2097152 | tf_op jit(solution)/shard_map/all_to_all | solution.py:157
  174.7 0.6 pad_maximum_fusion
  175.4 25.4 %all-to-all-done.6 = bf16[16,128,256]{2,1,0:T(8,128)(2,1)S(1)} async-done(((bf16[16,128,256]{2,1,0:T(8,128)(2,1)}), bf16[16,128,256]{2,1,0:T(8,128)(2,1)S(1)}, u32[]{:S(2)}, u32[]{:S(2)}) %all-to-all-start.6) | async-done | bytes 1048608 | tf_op jit(solution)/shard_map/all_to_all | solution.py:157
  200.7 0.1 convert_reduce_fusion
  200.9 0.8 convolution_convert_fusion
  (5 shorter events, 0.1 us)
Async XLA Ops:
  0.6 0.9 copy-start
  2.6 34.1 %copy-start.5 = (s32[128]{0:T(128)S(1)}, s32[128]{0:T(128)}, u32[]{:S(2)}) copy-start(s32[128]{0:T(128)} %param.10) | copy-start | bytes 1540
  2.6 34.1 %copy-start.3 = (bf16[128,256]{1,0:T(8,128)(2,1)S(1)}, bf16[128,256]{1,0:T(8,128)(2,1)}, u32[]{:S(2)}) copy-start(bf16[128,256]{1,0:T(8,128)(2,1)} %param.17) | copy-start | bytes 196612
  2.6 34.1 %copy-start.4 = (s32[1,1,128]{2,1,0:T(1,128)S(1)}, s32[1,1,128]{2,1,0:T(1,128)}, u32[]{:S(2)}) copy-start(s32[1,1,128]{2,1,0:T(1,128)} %param.15) | copy-start | bytes 1540
  2.6 36.0 %copy-start.2 = (s32[1,1,128]{2,1,0:T(1,128)S(1)}, s32[1,1,128]{2,1,0:T(1,128)}, u32[]{:S(2)}) copy-start(s32[1,1,128]{2,1,0:T(1,128)} %param.14) | copy-start | bytes 1540
  34.1 4.5 %collective-permute-start = (bf16[2048,256]{1,0:T(8,128)(2,1)S(1)}, bf16[2048,256]{1,0:T(8,128)(2,1)S(1)}, u32[]{:S(2)}, u32[]{:S(2)}) collective-permute-start(bf16[2048,256]{1,0:T(8,128)(2,1)S(1)} %bitcast.46), channel_id=1, source_target_pairs={{0,24},{24,0},{1,25},{25,1},{2,26},{26,2},{3,27},{27,3},{4,28},{28... | collective-permute-start | bytes 3145736 | tf_op jit(solution)/shard_map/ppermute | solution.py:188
  45.3 54.9 %copy-start.1 = (f32[256]{0:T(256)S(1)}, f32[256]{0:T(256)}, u32[]{:S(2)}) copy-start(f32[256]{0:T(256)} %param.12) | copy-start | bytes 3076
  45.3 28.3 %all-to-all-start.2 = ((bf16[8,3,128,128]{3,2,1,0:T(8,128)(2,1)}), bf16[8,3,128,128]{3,2,1,0:T(8,128)(2,1)S(1)}, u32[]{:S(2)}, u32[]{:S(2)}) async-start(bf16[8,3,128,128]{3,2,1,0:T(8,128)(2,1)} %get-tuple-element.23), calls=%async_computation.2 | async-start | bytes 1572864 | tf_op jit(solution)/shard_map/all_to_all | solution.py:157
  73.6 28.3 %all-to-all-start.3 = ((bf16[8,3,128,128]{3,2,1,0:T(8,128)(2,1)}), bf16[8,3,128,128]{3,2,1,0:T(8,128)(2,1)S(1)}, u32[]{:S(2)}, u32[]{:S(2)}) async-start(bf16[8,3,128,128]{3,2,1,0:T(8,128)(2,1)} %get-tuple-element.29), calls=%async_computation.3 | async-start | bytes 1572864 | tf_op jit(solution)/shard_map/all_to_all | solution.py:157
  101.9 28.2 %all-to-all-start.4 = ((bf16[8,3,128,128]{3,2,1,0:T(8,128)(2,1)}), bf16[8,3,128,128]{3,2,1,0:T(8,128)(2,1)S(1)}, u32[]{:S(2)}, u32[]{:S(2)}) async-start(bf16[8,3,128,128]{3,2,1,0:T(8,128)(2,1)} %get-tuple-element.33), calls=%async_computation.4 | async-start | bytes 1572864 | tf_op jit(solution)/shard_map/all_to_all | solution.py:157
  163.4 4.6 %collective-permute-start.1 = (bf16[2048,256]{1,0:T(8,128)(2,1)S(1)}, bf16[2048,256]{1,0:T(8,128)(2,1)S(1)}, u32[]{:S(2)}, u32[]{:S(2)}) collective-permute-start(bf16[2048,256]{1,0:T(8,128)(2,1)S(1)} %get-tuple-element.38), channel_id=1, source_target_pairs={{0,24},{24,0},{1,25},{25,1},{2,26},{26,2},{3,27},{27,3},{4,28},{28... | collective-permute-start | bytes 3145736 | tf_op jit(solution)/shard_map/ppermute | solution.py:218
  169.2 31.5 %all-to-all-start.6 = ((bf16[16,128,256]{2,1,0:T(8,128)(2,1)}), bf16[16,128,256]{2,1,0:T(8,128)(2,1)S(1)}, u32[]{:S(2)}, u32[]{:S(2)}) async-start(bf16[16,128,256]{2,1,0:T(8,128)(2,1)} %bitcast.11), calls=%async_computation.6 | async-start | bytes 2097152 | tf_op jit(solution)/shard_map/all_to_all | solution.py:157
